TPU v7x, 512 devices: a whole 4x8x8 slice. The times are simulated.
512 devices in a mesh: section: 8 (over x, core), blk: 32 (over z, y_hi), head: 2 (over y_lo).
Axes of the slice: x: 4, y: 8 (y_hi: 4, y_lo: 2; y = y_hi * 2 + y_lo), z: 8, core: 2. Of those that a mesh axis runs over, the one named last changes fastest.
Arguments:
- hidden_in: bfloat16 [4, 256, 1536], P(None, 'blk', 'head'), may hold values from -6 to 6
- w_qkv: bfloat16 [8, 1536, 3, 1536], P('section', 'blk', None, 'head'), may hold values from -0.15625 to 0.15625
- norm_gain: float32 [8, 1536], P('section'), may hold values from 0.5 to 1.5
- qk_gain: float32 [8, 2, 128], P('section'), may hold values from 1 to 2
- text_states: bfloat16 [8, 256, 1536], P('section'), may hold values from -6 to 6
- text_len: int32 [1], replicated, may hold values from 64 to 256
- patch_len: int32 [4], replicated, may hold values from 128 to 256
- stale_flags: int32 [4, 8], replicated, may hold values from 0 to 1, as said below
- stale_kv: bfloat16 [8, 2, 4, 256, 1536], P('section', None, None, 'blk', 'head'), may hold values from -6 to 6
Outputs:
- hidden_out: bfloat16 [8, 4, 256, 1536], P('section', None, 'blk', 'head')
- new_cache: bfloat16 [8, 2, 4, 256, 1536], P('section', None, None, 'blk', 'head')
Inputs may be any that keep to these rules, and one draw needn't show every extreme that they name: `stale_flags`: 1 means that the micro-batch uses the previous step's keys and values at that layer, 0 that it uses its fresh ones; every layer has at least one micro-batch flagged 1 and at least one flagged 0.
All inputs are finite; a program needn't handle non-finite values.
Results may differ from a plain program's by a relative error of at most 0.02.
Values may be sent and summed in bfloat16 or wider, within the bound.
No kernel may reach another device: no remote copies, remote signals or barrier semaphores. Data moves between devices by JAX's collectives and lax.ppermute only.
A program may use at most 64 MiB of HBM per device.

v0:
```python
import jax
import jax.numpy as jnp
from jax import lax
from jax.sharding import PartitionSpec as P


def from_behind(value, axis, steps):
    count = lax.axis_size(axis)
    first, last = (max(0, -steps), min(count, count - steps))
    return lax.ppermute(value, axis, [(source, source + steps) for source in range(first, last)])


def norm_rows(values, row_gain):
    return values * lax.rsqrt(jnp.mean(values * values, axis=-1, keepdims=True) + 1e-06) * row_gain


def shards(
    hidden_in, w_qkv, norm_gain, qk_gain, text_states, text_len, patch_len, stale_flags, stale_kv
):
    n_section = lax.axis_size("section")
    section_idx = lax.axis_index("section")
    micro_count, tok_rows, half_width = hidden_in.shape
    head_dim = qk_gain.shape[2]
    heads_here = half_width // head_dim
    score_scale = head_dim ** (-0.5)
    weights = lax.all_gather(w_qkv[0], "blk", axis=0, tiled=True)
    row_gain = norm_gain[0]
    query_gain = qk_gain[0, 0]
    key_gain = qk_gain[0, 1]
    text_all = text_states[0]
    text_count = text_all.shape[0]
    text_normed = norm_rows(text_all.astype(jnp.float32), row_gain).astype(jnp.bfloat16)
    text_kv = jnp.einsum(
        "td,dch->tch", text_normed, weights[:, 1:], preferred_element_type=jnp.float32
    ).astype(jnp.bfloat16)
    text_keys = norm_rows(
        text_kv[:, 0].astype(jnp.float32).reshape(text_count, heads_here, head_dim), key_gain
    ).astype(jnp.bfloat16)
    text_values = text_kv[:, 1].reshape(text_count, heads_here, head_dim)
    text_mask = jnp.arange(text_count) < text_len[0]
    col_offset = lax.axis_index("head") * half_width

    def attend(queries, key_rows, value_rows, key_mask, totals):
        scores = (
            jnp.einsum("qhd,khd->hqk", queries, key_rows, preferred_element_type=jnp.float32)
            * score_scale
        )
        probs = jnp.where(key_mask[None, None, :], jnp.exp(scores), 0.0)
        numerator = totals[0] + jnp.einsum(
            "hqk,khd->qhd",
            probs.astype(jnp.bfloat16),
            value_rows,
            preferred_element_type=jnp.float32,
        )
        return (numerator, totals[1] + jnp.sum(probs, axis=2))

    whole_input = lax.all_gather(hidden_in, "head", axis=2, tiled=True)
    inflow_init = jnp.zeros((tok_rows, 2 * half_width), jnp.bfloat16)
    hidden_init = jnp.zeros((micro_count, tok_rows, half_width), jnp.bfloat16)
    cache_init = jnp.zeros((2, micro_count, tok_rows, half_width), jnp.bfloat16)

    def advance(tick, carried):
        inflow, hidden_acc, cache_acc = carried
        micro_at = tick - section_idx
        is_active = (micro_at >= 0) & (micro_at < micro_count)
        micro_at = jnp.clip(micro_at, 0, micro_count - 1)
        state_rows = jnp.where(
            section_idx == 0,
            lax.dynamic_index_in_dim(whole_input, micro_at, 0, keepdims=False),
            inflow,
        )
        state_float = state_rows.astype(jnp.float32)
        normed = norm_rows(state_float, row_gain).astype(jnp.bfloat16)
        projected = jnp.einsum("td,dch->tch", normed, weights, preferred_element_type=jnp.float32)
        fresh_kv = jnp.moveaxis(projected[:, 1:], 1, 0).astype(jnp.bfloat16)
        use_stale = lax.dynamic_slice(stale_flags, (micro_at, section_idx), (1, 1))[0, 0]
        stale_here = lax.dynamic_index_in_dim(stale_kv[0], micro_at, 1, keepdims=False)
        kept_kv = jnp.where(use_stale == 1, stale_here, fresh_kv)
        key_rows = norm_rows(
            kept_kv[0].astype(jnp.float32).reshape(tok_rows, heads_here, head_dim), key_gain
        ).astype(jnp.bfloat16)
        value_rows = kept_kv[1].reshape(tok_rows, heads_here, head_dim)
        queries = norm_rows(
            projected[:, 0].reshape(tok_rows, heads_here, head_dim), query_gain
        ).astype(jnp.bfloat16)
        patch_limit = lax.dynamic_index_in_dim(patch_len, micro_at, 0, keepdims=False)
        zero_num = jnp.zeros((tok_rows, heads_here, head_dim), jnp.float32)
        zero_den = jnp.zeros((heads_here, tok_rows), jnp.float32)
        text_totals = attend(queries, text_keys, text_values, text_mask, (zero_num, zero_den))
        piece_keys = lax.all_gather(key_rows, "blk", axis=0, tiled=True)
        piece_values = lax.all_gather(value_rows, "blk", axis=0, tiled=True)
        key_mask = jnp.arange(piece_keys.shape[0]) < patch_limit
        numerator, denominator = attend(queries, piece_keys, piece_values, key_mask, text_totals)
        attended = (numerator / jnp.transpose(denominator)[:, :, None]).reshape(
            tok_rows, half_width
        )
        own_rows = lax.dynamic_slice_in_dim(state_float, col_offset, half_width, 1)
        new_half = (own_rows + attended).astype(jnp.bfloat16)
        hidden_acc = jnp.where(
            is_active,
            lax.dynamic_update_index_in_dim(hidden_acc, new_half, micro_at, 0),
            hidden_acc,
        )
        cache_acc = jnp.where(
            is_active, lax.dynamic_update_index_in_dim(cache_acc, fresh_kv, micro_at, 1), cache_acc
        )
        whole_next = lax.all_gather(new_half, "head", axis=1, tiled=True)
        inflow = from_behind(whole_next, "section", 1)
        return (inflow, hidden_acc, cache_acc)

    finished = lax.fori_loop(
        0, micro_count + n_section - 1, advance, (inflow_init, hidden_init, cache_init)
    )
    return (finished[1][None], finished[2][None])


def solution(mesh):
    in_specs = (
        P(None, "blk", "head"),
        P("section", "blk", None, "head"),
        P("section", None),
        P("section", None, None),
        P("section", None, None),
        P(),
        P(),
        P(),
        P("section", None, None, "blk", "head"),
    )
    out_specs = (P("section", None, "blk", "head"), P("section", None, None, "blk", "head"))
    return jax.shard_map(shards, mesh=mesh, in_specs=in_specs, out_specs=out_specs, check_vma=False)
```

profile of v0, /device:TPU:7, one launch (start us, length us, event | category | flops | bytes accessed | tf_op | source)
XLA Modules:
  0.0 2113.0 jit_solution(14227111844353619712)
XLA Ops:
  14.6 127.5 %all-gather.3.cloned.1.call-done = bf16[1,1536,3,768]{3,1,2,0:T(8,128)(2,1)} async-done(((bf16[1,48,3,768]{3,1,2,0:T(8,128)(2,1)}), bf16[1,1536,3,768]{3,1,2,0:T(8,128)(2,1)}) %all-gather.3.cloned.1.call-update) | async-done | bytes 7077904 | tf_op jit(solution)/shard_map/all_gather | solution.py:26
  147.4 1958.1 %while.20 = (s32[]{:T(128)}, bf16[8,1536]{1,0:T(8,128)(2,1)S(1)}, bf16[4,8,768]{2,1,0:T(8,128)(2,1)S(1)}, bf16[2,4,8,768]{3,2,1,0:T(8,128)(2,1)S(1)}, pred[]{:T(...) while((s32[]{:T(128)}, bf16[8,1536]{1,0:T(8,128)(2,1)S(1)}, ...), condition=%wide.region_8.9_spmd.clone, body=%wide.region_2.8_spmd.clone.sunk | while | flops 69538368 | bytes 10395399 | solution.py:111
  154.8 67.9 %all_gather.41 = bf16[256,6,128]{2,0,1:T(8,128)(2,1)S(1)} all-gather(bf16[8,6,128]{2,0,1:T(8,128)(2,1)S(1)} %fusion.73), channel_id=1, replica_groups=mesh['section'=8,'blk'=32,'head'=2] {'blk'}, dimensions={0}, use_global_device_ids=true | all-gather | bytes 405504 | tf_op jit(solution)/shard_map/while/body/eval_jaxpr/all_gather | solution.py:90
  224.7 63.7 %all_gather.42 = bf16[256,6,128]{2,0,1:T(8,128)(2,1)S(1)} all-gather(bf16[8,6,128]{2,0,1:T(8,128)(2,1)S(1)} %slice_bitcast_fusion.5), channel_id=1, replica_groups=mesh['section'=8,'blk'=32,'head'=2] {'blk'}, dimensions={0}, use_global_device_ids=true | all-gather | bytes 405504 | tf_op jit(solution)/shard_map/while/body/eval_jaxpr/all_gather | solution.py:91
  332.8 66.5 %all_gather.41 = bf16[256,6,128]{2,0,1:T(8,128)(2,1)S(1)} all-gather(bf16[8,6,128]{2,0,1:T(8,128)(2,1)S(1)} %fusion.73), channel_id=1, replica_groups=mesh['section'=8,'blk'=32,'head'=2] {'blk'}, dimensions={0}, use_global_device_ids=true | all-gather | bytes 405504 | tf_op jit(solution)/shard_map/while/body/eval_jaxpr/all_gather | solution.py:90
  401.3 64.2 %all_gather.42 = bf16[256,6,128]{2,0,1:T(8,128)(2,1)S(1)} all-gather(bf16[8,6,128]{2,0,1:T(8,128)(2,1)S(1)} %slice_bitcast_fusion.5), channel_id=1, replica_groups=mesh['section'=8,'blk'=32,'head'=2] {'blk'}, dimensions={0}, use_global_device_ids=true | all-gather | bytes 405504 | tf_op jit(solution)/shard_map/while/body/eval_jaxpr/all_gather | solution.py:91
  471.1 32.2 %collective-permute-done = bf16[8,1536]{1,0:T(8,128)(2,1)S(1)} collective-permute-done((bf16[8,1536]{1,0:T(8,128)(2,1)S(1)}, bf16[8,1536]{1,0:T(8,128)(2,1)S(1)}, u32[]{:S(2)}, u32[]{:S(2)}) %collective-permute-start) | collective-permute-done | bytes 24608 | tf_op jit(solution)/shard_map/while/body/eval_jaxpr/ppermute | solution.py:10
  510.6 66.8 %all_gather.41 = bf16[256,6,128]{2,0,1:T(8,128)(2,1)S(1)} all-gather(bf16[8,6,128]{2,0,1:T(8,128)(2,1)S(1)} %fusion.73), channel_id=1, replica_groups=mesh['section'=8,'blk'=32,'head'=2] {'blk'}, dimensions={0}, use_global_device_ids=true | all-gather | bytes 405504 | tf_op jit(solution)/shard_map/while/body/eval_jaxpr/all_gather | solution.py:90
  579.4 63.7 %all_gather.42 = bf16[256,6,128]{2,0,1:T(8,128)(2,1)S(1)} all-gather(bf16[8,6,128]{2,0,1:T(8,128)(2,1)S(1)} %slice_bitcast_fusion.5), channel_id=1, replica_groups=mesh['section'=8,'blk'=32,'head'=2] {'blk'}, dimensions={0}, use_global_device_ids=true | all-gather | bytes 405504 | tf_op jit(solution)/shard_map/while/body/eval_jaxpr/all_gather | solution.py:91
  648.8 32.5 %collective-permute-done = bf16[8,1536]{1,0:T(8,128)(2,1)S(1)} collective-permute-done((bf16[8,1536]{1,0:T(8,128)(2,1)S(1)}, bf16[8,1536]{1,0:T(8,128)(2,1)S(1)}, u32[]{:S(2)}, u32[]{:S(2)}) %collective-permute-start) | collective-permute-done | bytes 24608 | tf_op jit(solution)/shard_map/while/body/eval_jaxpr/ppermute | solution.py:10
  688.6 66.8 %all_gather.41 = bf16[256,6,128]{2,0,1:T(8,128)(2,1)S(1)} all-gather(bf16[8,6,128]{2,0,1:T(8,128)(2,1)S(1)} %fusion.73), channel_id=1, replica_groups=mesh['section'=8,'blk'=32,'head'=2] {'blk'}, dimensions={0}, use_global_device_ids=true | all-gather | bytes 405504 | tf_op jit(solution)/shard_map/while/body/eval_jaxpr/all_gather | solution.py:90
  757.4 64.1 %all_gather.42 = bf16[256,6,128]{2,0,1:T(8,128)(2,1)S(1)} all-gather(bf16[8,6,128]{2,0,1:T(8,128)(2,1)S(1)} %slice_bitcast_fusion.5), channel_id=1, replica_groups=mesh['section'=8,'blk'=32,'head'=2] {'blk'}, dimensions={0}, use_global_device_ids=true | all-gather | bytes 405504 | tf_op jit(solution)/shard_map/while/body/eval_jaxpr/all_gather | solution.py:91
  827.2 32.4 %collective-permute-done = bf16[8,1536]{1,0:T(8,128)(2,1)S(1)} collective-permute-done((bf16[8,1536]{1,0:T(8,128)(2,1)S(1)}, bf16[8,1536]{1,0:T(8,128)(2,1)S(1)}, u32[]{:S(2)}, u32[]{:S(2)}) %collective-permute-start) | collective-permute-done | bytes 24608 | tf_op jit(solution)/shard_map/while/body/eval_jaxpr/ppermute | solution.py:10
  866.9 66.0 %all_gather.41 = bf16[256,6,128]{2,0,1:T(8,128)(2,1)S(1)} all-gather(bf16[8,6,128]{2,0,1:T(8,128)(2,1)S(1)} %fusion.73), channel_id=1, replica_groups=mesh['section'=8,'blk'=32,'head'=2] {'blk'}, dimensions={0}, use_global_device_ids=true | all-gather | bytes 405504 | tf_op jit(solution)/shard_map/while/body/eval_jaxpr/all_gather | solution.py:90
  934.9 64.7 %all_gather.42 = bf16[256,6,128]{2,0,1:T(8,128)(2,1)S(1)} all-gather(bf16[8,6,128]{2,0,1:T(8,128)(2,1)S(1)} %slice_bitcast_fusion.5), channel_id=1, replica_groups=mesh['section'=8,'blk'=32,'head'=2] {'blk'}, dimensions={0}, use_global_device_ids=true | all-gather | bytes 405504 | tf_op jit(solution)/shard_map/while/body/eval_jaxpr/all_gather | solution.py:91
  1005.3 32.4 %collective-permute-done = bf16[8,1536]{1,0:T(8,128)(2,1)S(1)} collective-permute-done((bf16[8,1536]{1,0:T(8,128)(2,1)S(1)}, bf16[8,1536]{1,0:T(8,128)(2,1)S(1)}, u32[]{:S(2)}, u32[]{:S(2)}) %collective-permute-start) | collective-permute-done | bytes 24608 | tf_op jit(solution)/shard_map/while/body/eval_jaxpr/ppermute | solution.py:10
  1045.0 65.9 %all_gather.41 = bf16[256,6,128]{2,0,1:T(8,128)(2,1)S(1)} all-gather(bf16[8,6,128]{2,0,1:T(8,128)(2,1)S(1)} %fusion.73), channel_id=1, replica_groups=mesh['section'=8,'blk'=32,'head'=2] {'blk'}, dimensions={0}, use_global_device_ids=true | all-gather | bytes 405504 | tf_op jit(solution)/shard_map/while/body/eval_jaxpr/all_gather | solution.py:90
  1112.9 64.2 %all_gather.42 = bf16[256,6,128]{2,0,1:T(8,128)(2,1)S(1)} all-gather(bf16[8,6,128]{2,0,1:T(8,128)(2,1)S(1)} %slice_bitcast_fusion.5), channel_id=1, replica_groups=mesh['section'=8,'blk'=32,'head'=2] {'blk'}, dimensions={0}, use_global_device_ids=true | all-gather | bytes 405504 | tf_op jit(solution)/shard_map/while/body/eval_jaxpr/all_gather | solution.py:91
  1182.7 33.1 %collective-permute-done = bf16[8,1536]{1,0:T(8,128)(2,1)S(1)} collective-permute-done((bf16[8,1536]{1,0:T(8,128)(2,1)S(1)}, bf16[8,1536]{1,0:T(8,128)(2,1)S(1)}, u32[]{:S(2)}, u32[]{:S(2)}) %collective-permute-start) | collective-permute-done | bytes 24608 | tf_op jit(solution)/shard_map/while/body/eval_jaxpr/ppermute | solution.py:10
  1223.1 66.7 %all_gather.41 = bf16[256,6,128]{2,0,1:T(8,128)(2,1)S(1)} all-gather(bf16[8,6,128]{2,0,1:T(8,128)(2,1)S(1)} %fusion.73), channel_id=1, replica_groups=mesh['section'=8,'blk'=32,'head'=2] {'blk'}, dimensions={0}, use_global_device_ids=true | all-gather | bytes 405504 | tf_op jit(solution)/shard_map/while/body/eval_jaxpr/all_gather | solution.py:90
  1291.8 64.0 %all_gather.42 = bf16[256,6,128]{2,0,1:T(8,128)(2,1)S(1)} all-gather(bf16[8,6,128]{2,0,1:T(8,128)(2,1)S(1)} %slice_bitcast_fusion.5), channel_id=1, replica_groups=mesh['section'=8,'blk'=32,'head'=2] {'blk'}, dimensions={0}, use_global_device_ids=true | all-gather | bytes 405504 | tf_op jit(solution)/shard_map/while/body/eval_jaxpr/all_gather | solution.py:91
  1361.4 32.4 %collective-permute-done = bf16[8,1536]{1,0:T(8,128)(2,1)S(1)} collective-permute-done((bf16[8,1536]{1,0:T(8,128)(2,1)S(1)}, bf16[8,1536]{1,0:T(8,128)(2,1)S(1)}, u32[]{:S(2)}, u32[]{:S(2)}) %collective-permute-start) | collective-permute-done | bytes 24608 | tf_op jit(solution)/shard_map/while/body/eval_jaxpr/ppermute | solution.py:10
  1401.1 65.7 %all_gather.41 = bf16[256,6,128]{2,0,1:T(8,128)(2,1)S(1)} all-gather(bf16[8,6,128]{2,0,1:T(8,128)(2,1)S(1)} %fusion.73), channel_id=1, replica_groups=mesh['section'=8,'blk'=32,'head'=2] {'blk'}, dimensions={0}, use_global_device_ids=true | all-gather | bytes 405504 | tf_op jit(solution)/shard_map/while/body/eval_jaxpr/all_gather | solution.py:90
  1468.8 65.1 %all_gather.42 = bf16[256,6,128]{2,0,1:T(8,128)(2,1)S(1)} all-gather(bf16[8,6,128]{2,0,1:T(8,128)(2,1)S(1)} %slice_bitcast_fusion.5), channel_id=1, replica_groups=mesh['section'=8,'blk'=32,'head'=2] {'blk'}, dimensions={0}, use_global_device_ids=true | all-gather | bytes 405504 | tf_op jit(solution)/shard_map/while/body/eval_jaxpr/all_gather | solution.py:91
  1579.2 65.2 %all_gather.41 = bf16[256,6,128]{2,0,1:T(8,128)(2,1)S(1)} all-gather(bf16[8,6,128]{2,0,1:T(8,128)(2,1)S(1)} %fusion.73), channel_id=1, replica_groups=mesh['section'=8,'blk'=32,'head'=2] {'blk'}, dimensions={0}, use_global_device_ids=true | all-gather | bytes 405504 | tf_op jit(solution)/shard_map/while/body/eval_jaxpr/all_gather | solution.py:90
  1646.4 65.4 %all_gather.42 = bf16[256,6,128]{2,0,1:T(8,128)(2,1)S(1)} all-gather(bf16[8,6,128]{2,0,1:T(8,128)(2,1)S(1)} %slice_bitcast_fusion.5), channel_id=1, replica_groups=mesh['section'=8,'blk'=32,'head'=2] {'blk'}, dimensions={0}, use_global_device_ids=true | all-gather | bytes 405504 | tf_op jit(solution)/shard_map/while/body/eval_jaxpr/all_gather | solution.py:91
  1717.6 32.2 %collective-permute-done = bf16[8,1536]{1,0:T(8,128)(2,1)S(1)} collective-permute-done((bf16[8,1536]{1,0:T(8,128)(2,1)S(1)}, bf16[8,1536]{1,0:T(8,128)(2,1)S(1)}, u32[]{:S(2)}, u32[]{:S(2)}) %collective-permute-start) | collective-permute-done | bytes 24608 | tf_op jit(solution)/shard_map/while/body/eval_jaxpr/ppermute | solution.py:10
  1757.1 65.2 %all_gather.41 = bf16[256,6,128]{2,0,1:T(8,128)(2,1)S(1)} all-gather(bf16[8,6,128]{2,0,1:T(8,128)(2,1)S(1)} %fusion.73), channel_id=1, replica_groups=mesh['section'=8,'blk'=32,'head'=2] {'blk'}, dimensions={0}, use_global_device_ids=true | all-gather | bytes 405504 | tf_op jit(solution)/shard_map/while/body/eval_jaxpr/all_gather | solution.py:90
  1824.3 65.3 %all_gather.42 = bf16[256,6,128]{2,0,1:T(8,128)(2,1)S(1)} all-gather(bf16[8,6,128]{2,0,1:T(8,128)(2,1)S(1)} %slice_bitcast_fusion.5), channel_id=1, replica_groups=mesh['section'=8,'blk'=32,'head'=2] {'blk'}, dimensions={0}, use_global_device_ids=true | all-gather | bytes 405504 | tf_op jit(solution)/shard_map/while/body/eval_jaxpr/all_gather | solution.py:91
  1934.7 65.9 %all_gather.41 = bf16[256,6,128]{2,0,1:T(8,128)(2,1)S(1)} all-gather(bf16[8,6,128]{2,0,1:T(8,128)(2,1)S(1)} %fusion.73), channel_id=1, replica_groups=mesh['section'=8,'blk'=32,'head'=2] {'blk'}, dimensions={0}, use_global_device_ids=true | all-gather | bytes 405504 | tf_op jit(solution)/shard_map/while/body/eval_jaxpr/all_gather | solution.py:90
  2002.6 64.1 %all_gather.42 = bf16[256,6,128]{2,0,1:T(8,128)(2,1)S(1)} all-gather(bf16[8,6,128]{2,0,1:T(8,128)(2,1)S(1)} %slice_bitcast_fusion.5), channel_id=1, replica_groups=mesh['section'=8,'blk'=32,'head'=2] {'blk'}, dimensions={0}, use_global_device_ids=true | all-gather | bytes 405504 | tf_op jit(solution)/shard_map/while/body/eval_jaxpr/all_gather | solution.py:91
  2072.8 32.7 %collective-permute-done = bf16[8,1536]{1,0:T(8,128)(2,1)S(1)} collective-permute-done((bf16[8,1536]{1,0:T(8,128)(2,1)S(1)}, bf16[8,1536]{1,0:T(8,128)(2,1)S(1)}, u32[]{:S(2)}, u32[]{:S(2)}) %collective-permute-start) | collective-permute-done | bytes 24608 | tf_op jit(solution)/shard_map/while/body/eval_jaxpr/ppermute | solution.py:10
  (294 shorter events, 265.7 us)
Async XLA Ops:
  7.2 134.9 %all-gather.3.cloned.1.call-start = ((), (), s32[]{:S(2)}) async-start(), calls=%async_computation | async-start | bytes 7299072 | tf_op jit(solution)/shard_map/all_gather | solution.py:26
  146.1 1.3 copy-start.2
  146.1 1.3 copy-start.3
  292.9 32.6 %collective-permute-start = (bf16[8,1536]{1,0:T(8,128)(2,1)S(1)}, bf16[8,1536]{1,0:T(8,128)(2,1)S(1)}, u32[]{:S(2)}, u32[]{:S(2)}) collective-permute-start(bf16[8,1536]{1,0:T(8,128)(2,1)S(1)} %all_gather.43), channel_id=1, source_target_pairs={{0,64},{64,128},{128,192},{192,256},{256,320},{320,384},{384,448},... | collective-permute-start | bytes 73736 | tf_op jit(solution)/shard_map/while/body/eval_jaxpr/ppermute | solution.py:10
  469.8 33.6 %collective-permute-start = (bf16[8,1536]{1,0:T(8,128)(2,1)S(1)}, bf16[8,1536]{1,0:T(8,128)(2,1)S(1)}, u32[]{:S(2)}, u32[]{:S(2)}) collective-permute-start(bf16[8,1536]{1,0:T(8,128)(2,1)S(1)} %all_gather.43), channel_id=1, source_target_pairs={{0,64},{64,128},{128,192},{192,256},{256,320},{320,384},{384,448},... | collective-permute-start | bytes 73736 | tf_op jit(solution)/shard_map/while/body/eval_jaxpr/ppermute | solution.py:10
  647.5 33.8 %collective-permute-start = (bf16[8,1536]{1,0:T(8,128)(2,1)S(1)}, bf16[8,1536]{1,0:T(8,128)(2,1)S(1)}, u32[]{:S(2)}, u32[]{:S(2)}) collective-permute-start(bf16[8,1536]{1,0:T(8,128)(2,1)S(1)} %all_gather.43), channel_id=1, source_target_pairs={{0,64},{64,128},{128,192},{192,256},{256,320},{320,384},{384,448},... | collective-permute-start | bytes 73736 | tf_op jit(solution)/shard_map/while/body/eval_jaxpr/ppermute | solution.py:10
  825.8 33.8 %collective-permute-start = (bf16[8,1536]{1,0:T(8,128)(2,1)S(1)}, bf16[8,1536]{1,0:T(8,128)(2,1)S(1)}, u32[]{:S(2)}, u32[]{:S(2)}) collective-permute-start(bf16[8,1536]{1,0:T(8,128)(2,1)S(1)} %all_gather.43), channel_id=1, source_target_pairs={{0,64},{64,128},{128,192},{192,256},{256,320},{320,384},{384,448},... | collective-permute-start | bytes 73736 | tf_op jit(solution)/shard_map/while/body/eval_jaxpr/ppermute | solution.py:10
  1003.9 33.7 %collective-permute-start = (bf16[8,1536]{1,0:T(8,128)(2,1)S(1)}, bf16[8,1536]{1,0:T(8,128)(2,1)S(1)}, u32[]{:S(2)}, u32[]{:S(2)}) collective-permute-start(bf16[8,1536]{1,0:T(8,128)(2,1)S(1)} %all_gather.43), channel_id=1, source_target_pairs={{0,64},{64,128},{128,192},{192,256},{256,320},{320,384},{384,448},... | collective-permute-start | bytes 73736 | tf_op jit(solution)/shard_map/while/body/eval_jaxpr/ppermute | solution.py:10
  1181.3 34.5 %collective-permute-start = (bf16[8,1536]{1,0:T(8,128)(2,1)S(1)}, bf16[8,1536]{1,0:T(8,128)(2,1)S(1)}, u32[]{:S(2)}, u32[]{:S(2)}) collective-permute-start(bf16[8,1536]{1,0:T(8,128)(2,1)S(1)} %all_gather.43), channel_id=1, source_target_pairs={{0,64},{64,128},{128,192},{192,256},{256,320},{320,384},{384,448},... | collective-permute-start | bytes 73736 | tf_op jit(solution)/shard_map/while/body/eval_jaxpr/ppermute | solution.py:10
  1360.0 33.7 %collective-permute-start = (bf16[8,1536]{1,0:T(8,128)(2,1)S(1)}, bf16[8,1536]{1,0:T(8,128)(2,1)S(1)}, u32[]{:S(2)}, u32[]{:S(2)}) collective-permute-start(bf16[8,1536]{1,0:T(8,128)(2,1)S(1)} %all_gather.43), channel_id=1, source_target_pairs={{0,64},{64,128},{128,192},{192,256},{256,320},{320,384},{384,448},... | collective-permute-start | bytes 73736 | tf_op jit(solution)/shard_map/while/body/eval_jaxpr/ppermute | solution.py:10
  1538.4 33.5 %collective-permute-start = (bf16[8,1536]{1,0:T(8,128)(2,1)S(1)}, bf16[8,1536]{1,0:T(8,128)(2,1)S(1)}, u32[]{:S(2)}, u32[]{:S(2)}) collective-permute-start(bf16[8,1536]{1,0:T(8,128)(2,1)S(1)} %all_gather.43), channel_id=1, source_target_pairs={{0,64},{64,128},{128,192},{192,256},{256,320},{320,384},{384,448},... | collective-permute-start | bytes 73736 | tf_op jit(solution)/shard_map/while/body/eval_jaxpr/ppermute | solution.py:10
  1716.2 33.6 %collective-permute-start = (bf16[8,1536]{1,0:T(8,128)(2,1)S(1)}, bf16[8,1536]{1,0:T(8,128)(2,1)S(1)}, u32[]{:S(2)}, u32[]{:S(2)}) collective-permute-start(bf16[8,1536]{1,0:T(8,128)(2,1)S(1)} %all_gather.43), channel_id=1, source_target_pairs={{0,64},{64,128},{128,192},{192,256},{256,320},{320,384},{384,448},... | collective-permute-start | bytes 73736 | tf_op jit(solution)/shard_map/while/body/eval_jaxpr/ppermute | solution.py:10
  1894.1 33.2 %collective-permute-start = (bf16[8,1536]{1,0:T(8,128)(2,1)S(1)}, bf16[8,1536]{1,0:T(8,128)(2,1)S(1)}, u32[]{:S(2)}, u32[]{:S(2)}) collective-permute-start(bf16[8,1536]{1,0:T(8,128)(2,1)S(1)} %all_gather.43), channel_id=1, source_target_pairs={{0,64},{64,128},{128,192},{192,256},{256,320},{320,384},{384,448},... | collective-permute-start | bytes 73736 | tf_op jit(solution)/shard_map/while/body/eval_jaxpr/ppermute | solution.py:10
  2071.5 34.0 %collective-permute-start = (bf16[8,1536]{1,0:T(8,128)(2,1)S(1)}, bf16[8,1536]{1,0:T(8,128)(2,1)S(1)}, u32[]{:S(2)}, u32[]{:S(2)}) collective-permute-start(bf16[8,1536]{1,0:T(8,128)(2,1)S(1)} %all_gather.43), channel_id=1, source_target_pairs={{0,64},{64,128},{128,192},{192,256},{256,320},{320,384},{384,448},... | collective-permute-start | bytes 73736 | tf_op jit(solution)/shard_map/while/body/eval_jaxpr/ppermute | solution.py:10
  2105.5 0.6 copy-start
  2105.5 0.7 copy-start.1
Sparse Core Ops, SparseCore 0:
  11.2 130.8 all-gather.2
where the time goes:
time: 2120 us; the launch traced here: 2110 us
  blocking collectives  1480 us (70%)
  waiting for transfers between devices  484 us (23%)
  matrix products  59.8 us (3%)
  other arithmetic  30.2 us (1%)
  local copies, waits for them, and re-layouts  24.7 us (1%)
    all_gather x11, blocking collectives, advance(): piece_keys = lax.all_gather(key_rows, 'blk', axis=0, tiled=True)  729 us
    all_gather x11, blocking collectives, advance(): piece_values = lax.all_gather(value_rows, 'blk', axis=0, tiled=True)  708 us
    ppermute x11, waiting for transfers between devices, from_behind(): lax.ppermute(value, axis, [(source, source + steps) for source in range(f...  355 us
    all_gather x1, waiting for transfers between devices, shards(): weights = lax.all_gather(w_qkv[0], 'blk', axis=0, tiled=True)  128 us
    dot_general x11, matrix products, advance(): jnp.einsum('td,dch->tch', normed, weights, preferred_element_type=jnp.flo...  44.7 us
  transfers between devices with their start and end apart: 12, of which 12 were waited for; matrix products, arithmetic and copies ran while one was open for 0% of the time, Pallas kernels for 0%

commit v1 on v0

v1 whole, which is shorter than its diff:
```python
import functools
import jax
import jax.numpy as jnp
from jax import lax
from jax.experimental import pallas as pl
from jax.experimental.pallas import tpu as pltpu
from jax.sharding import PartitionSpec as P

AX = ("section", "blk", "head")
PLANE = ("blk", "head")
BF = jnp.bfloat16
F32 = jnp.float32
ROWS = 48
QUAD = [(a, c) for a in range(2) for c in range(2)]
TARGET = {(half, side): (1 + side, 2 - half) for half in range(2) for side in range(2)}


def place(z, y):
    return (z % 8) * 8 + y % 8


def quadrant_groups():
    return [[place(z + 4 * a, y + 4 * c) for a, c in QUAD] for z in range(4) for y in range(4)]


def block_groups():
    order = [TARGET[half, side] for half in range(2) for side in range(2)]
    return [[place(z + 2 * i, y + 2 * j) for z, y in order] for i in range(4) for j in range(4)]


def weight_pairs(zl, swapped, sections):
    pairs = []
    for s in range(sections):
        for a, c in QUAD:
            for half in range(2):
                for yh in range(2):
                    z, y = TARGET[half, 1 - yh if swapped else yh]
                    pairs.append((
                        s * 64 + place(4 * a + zl, 4 * c + 2 * yh + half),
                        s * 64 + place(4 * a + z, 4 * c + y),
                    ))
    return pairs


def hop_pairs(step):
    return [
        (step * 64 + place(4 * a + z, 4 * c + y), (step + 1) * 64 + place(4 * a + z, 4 * c + y))
        for a, c in QUAD
        for z, y in TARGET.values()
    ]


def head_norm(block, gain):
    mean = jnp.mean(block * block, axis=-1, keepdims=True)
    return block * lax.rsqrt(mean + 1e-06) * gain


def prep_kernel(
    heads, scalars, *refs
):
    pieces, (text_ref, gain_ref, qk_ref, stale_ref), (w_ref, tk_ref, tv_ref, sk_ref), (sems,) = (
        refs[:8], refs[8:12], refs[12:16], refs[16:]
    )
    width = heads * 128
    side = scalars[0]
    copies = []
    for zl in range(4):
        for swapped in range(2):
            yh = side if swapped == 0 else 1 - side
            for k, (a, c) in enumerate(QUAD):
                block = (4 * a + zl) * 4 + 2 * c + yh
                row = pl.multiple_of(block * ROWS, 16)
                for part in range(3):
                    copy = pltpu.make_async_copy(
                        pieces[2 * zl + swapped].at[k, pl.ds(part * ROWS, ROWS), :],
                        w_ref.at[pl.ds(row, ROWS), pl.ds(part * width, width)],
                        sems.at[len(copies)],
                    )
                    copy.start()
                    copies.append(copy)
    text = text_ref[...].astype(F32)
    mean = jnp.mean(text * text, axis=-1, keepdims=True)
    normed = (text * lax.rsqrt(mean + 1e-06) * gain_ref[...]).astype(BF)
    key_gain = qk_ref[1:2, :]
    for h in range(heads):
        cols = slice(h * 128, (h + 1) * 128)
        sk_ref[:, cols] = head_norm(stale_ref[0, :, cols].astype(F32), key_gain).astype(BF)
    for copy in copies:
        copy.wait()
    kv = jnp.dot(normed, w_ref[:, width:], preferred_element_type=F32).astype(BF)
    for h in range(heads):
        cols = slice(h * 128, (h + 1) * 128)
        tk_ref[:, cols] = head_norm(kv[:, cols].astype(F32), key_gain).astype(BF)
    tv_ref[...] = kv[:, width:]


def layer_kernel(
    heads, scalars, x_ref, own_ref, w_ref, gain_ref, qk_ref, tk_ref, tv_ref, sk_ref, sv_ref,
    out_ref, cache_ref,
):
    width = heads * 128
    stale, limit, text_limit = scalars[1] == 1, scalars[2], scalars[3]
    parts = [x_ref[q].astype(F32) for q in range(4)]
    total = sum(jnp.sum(part * part, axis=-1, keepdims=True) for part in parts)
    scale = lax.rsqrt(total / (4 * width) + 1e-06)
    normed = jnp.concatenate(
        [
            (part * scale * gain_ref[:, q * width : (q + 1) * width]).astype(BF)
            for q, part in enumerate(parts)
        ],
        axis=1,
    )
    projected = jnp.dot(normed, w_ref[...], preferred_element_type=F32)
    fresh = projected[:, width:].astype(BF)
    cache_ref[0] = fresh[:, :width]
    cache_ref[1] = fresh[:, width:]
    query_gain, key_gain = qk_ref[0:1, :], qk_ref[1:2, :]
    tokens = out_ref.shape[0]
    own_mask = lax.broadcasted_iota(jnp.int32, (tokens, tokens), 1) < limit
    text_mask = lax.broadcasted_iota(jnp.int32, (tokens, tk_ref.shape[0]), 1) < text_limit
    contract = (((1,), (1,)), ((), ()))
    for h in range(heads):
        cols = slice(h * 128, (h + 1) * 128)
        queries = head_norm(projected[:, cols], query_gain).astype(BF)
        keys = head_norm(fresh[:, cols].astype(F32), key_gain).astype(BF)
        keys = jnp.where(stale, sk_ref[:, cols], keys)
        values = jnp.where(stale, sv_ref[:, cols], fresh[:, width + h * 128 : width + (h + 1) * 128])
        own = lax.dot_general(queries, keys, contract, preferred_element_type=F32)
        own = jnp.where(own_mask, jnp.exp(own * 128 ** (-0.5)), 0.0)
        text = lax.dot_general(queries, tk_ref[:, cols], contract, preferred_element_type=F32)
        text = jnp.where(text_mask, jnp.exp(text * 128 ** (-0.5)), 0.0)
        numerator = jnp.dot(text.astype(BF), tv_ref[:, cols], preferred_element_type=F32)
        numerator += jnp.dot(own.astype(BF), values, preferred_element_type=F32)
        denominator = jnp.sum(own, axis=1, keepdims=True) + jnp.sum(text, axis=1, keepdims=True)
        out_ref[:, cols] = (own_ref[:, cols].astype(F32) + numerator / denominator).astype(BF)


def shards(
    hidden_in, w_qkv, norm_gain, qk_gain, text_states, text_len, patch_len, stale_flags, stale_kv
):
    sections = lax.axis_size("section")
    section = lax.axis_index("section")
    blk = lax.axis_index("blk")
    half = lax.axis_index("head")
    micros, tok, half_width = hidden_in.shape
    width = half_width // 2
    heads = width // 128
    z, y_hi = blk // 4, blk % 4
    micro = 2 * (z // 4) + y_hi // 2
    side = jnp.where(z % 4 == 2, 1, 0)
    swap = y_hi % 2 == 1

    w = jnp.moveaxis(w_qkv[0], 1, 0).reshape(3, ROWS, 2, width)
    w = jnp.moveaxis(w, 2, 0).reshape(1, 2, 3 * ROWS, width)
    old = jnp.moveaxis(stale_kv[0].reshape(2, micros, tok, 2, width), (1, 3), (0, 1))
    first = jnp.moveaxis(hidden_in.reshape(micros, tok, 2, width), 2, 1)
    packed = jnp.concatenate(
        [
            jnp.broadcast_to(w, (micros,) + w.shape[1:]),
            old.reshape(micros, 2, 2 * tok, width),
            first,
        ],
        axis=2,
    )
    packed = jnp.where(swap, packed[:, ::-1], packed)
    spread = lax.all_to_all(
        packed, PLANE, 0, 0, axis_index_groups=quadrant_groups(), tiled=True
    )
    lanes = (spread[:, 0], spread[:, 1])
    pieces = [
        lax.ppermute(lanes[swapped], AX, weight_pairs(zl, swapped, sections))
        for zl in range(4)
        for swapped in range(2)
    ]
    tails = [piece[:, 3 * ROWS :] for piece in pieces]
    straight = jnp.stack([jnp.stack(tails[2 * i : 2 * i + 2]) for i in range(4)])
    straight = jnp.where(side == 1, straight[:, ::-1], straight)
    tail = straight.reshape(4, 2, 2, 2, 3, tok, width).transpose(4, 2, 0, 3, 1, 5, 6)
    tail = tail.reshape(3, 32 * tok, width)
    stale_value, state = tail[1], tail[2]

    flag = lax.dynamic_slice(stale_flags, (micro, section), (1, 1))[0, 0]
    limit = lax.dynamic_slice(patch_len, (micro,), (1,))[0]
    scalars = jnp.stack([side, flag, limit, text_len[0]]).astype(jnp.int32)
    tokens, text_count, depth = 32 * tok, text_states.shape[1], text_states.shape[2]
    vmem = pl.BlockSpec(memory_space=pltpu.VMEM)
    smem = pl.BlockSpec(memory_space=pltpu.SMEM)
    qk = qk_gain[0]
    block = jax.ShapeDtypeStruct((tokens, width), BF)
    weights, text_key, text_value, stale_key = pl.pallas_call(
        functools.partial(prep_kernel, heads),
        out_shape=[jax.ShapeDtypeStruct((depth, 3 * width), BF)]
        + [jax.ShapeDtypeStruct((text_count, width), BF)] * 2
        + [block],
        in_specs=[smem] + [pl.BlockSpec(memory_space=pl.ANY)] * 8 + [vmem] * 4,
        out_specs=[vmem] * 4,
        scratch_shapes=[pltpu.SemaphoreType.DMA((96,))],
        compiler_params=pltpu.CompilerParams(vmem_limit_bytes=40 * 2**20),
        name="prepare",
    )(scalars, *pieces, text_states[0], norm_gain, qk, tail)

    layer = pl.pallas_call(
        functools.partial(layer_kernel, heads),
        out_shape=[block, jax.ShapeDtypeStruct((2, tokens, width), BF)],
        in_specs=[smem] + [vmem] * 9,
        out_specs=[vmem] * 2,
        compiler_params=pltpu.CompilerParams(vmem_limit_bytes=40 * 2**20),
        name="layer",
    )
    kept_hidden = kept_cache = None
    for step in range(sections):
        if step:
            state = lax.ppermute(state, AX, hop_pairs(step - 1))
        whole = lax.all_to_all(
            jnp.broadcast_to(state[None], (4,) + state.shape),
            PLANE, 0, 0, axis_index_groups=block_groups(), tiled=True,
        )
        state, cache = layer(
            scalars, whole, state, weights, norm_gain, qk, text_key, text_value, stale_key,
            stale_value,
        )
        if step:
            here = section == step
            kept_hidden = jnp.where(here, state, kept_hidden)
            kept_cache = jnp.where(here, cache, kept_cache)
        else:
            kept_hidden, kept_cache = state, cache

    result = jnp.concatenate([kept_hidden[None], kept_cache]).reshape(3, 32, tok, width)
    result = lax.all_to_all(jnp.moveaxis(result, 1, 0), "blk", 0, 0, tiled=True)
    chosen = []
    for a, c in QUAD:
        for which in range(2):
            options = []
            for h in range(2):
                tz, ty = TARGET[h, which]
                options.append(result[(4 * a + tz) * 4 + 2 * c + ty // 2])
            chosen.append(jnp.where(half == 1, options[1], options[0]))
    out = jnp.stack(chosen).reshape(micros, 2, 3, tok, width).transpose(2, 0, 3, 1, 4)
    out = out.reshape(3, micros, tok, half_width)
    return (out[0][None], out[1:][None])


def solution(mesh):
    in_specs = (
        P(None, "blk", "head"),
        P("section", "blk", None, "head"),
        P("section", None),
        P("section", None, None),
        P("section", None, None),
        P(),
        P(),
        P(),
        P("section", None, None, "blk", "head"),
    )
    out_specs = (P("section", None, "blk", "head"), P("section", None, None, "blk", "head"))
    return jax.shard_map(shards, mesh=mesh, in_specs=in_specs, out_specs=out_specs, check_vma=False)
```

time: 2120 us -> 360 us (0.17)
  the two profiles are of different devices: /device:TPU:7 before, /device:TPU:14 now
where the time goes in v1:
time: 360 us; the launch traced here: 358 us
  blocking collectives  122 us (34%)
  starting transfers between devices  87.3 us (24%)
  waiting for transfers between devices  78 us (22%)
  local copies, waits for them, and re-layouts  39 us (11%)
  Pallas kernels  25.5 us (7%)
    all_to_all x6, blocking collectives, shards(): lax.all_to_all(jnp.broadcast_to(state[None], (4,) + state.shape), PLANE,...  75.1 us
    ppermute x8, waiting for transfers between devices, shards(): lax.ppermute(lanes[swapped], AX, weight_pairs(zl, swapped, sections))  49.4 us
    all_to_all x1, blocking collectives, shards(): lax.all_to_all(packed, PLANE, 0, 0, axis_index_groups=quadrant_groups(),...  47.3 us
    all_to_all x2, starting transfers between devices, shards(): lax.all_to_all(jnp.broadcast_to(state[None], (4,) + state.shape), PLANE,...  44.4 us
    unnamed x134, local copies, waits for them, and re-layouts  29.6 us
    all_to_all x1, starting transfers between devices, shards(): result = lax.all_to_all(jnp.moveaxis(result, 1, 0), 'blk', 0, 0, tiled=True)  28.4 us
    all_to_all x1, waiting for transfers between devices, shards(): result = lax.all_to_all(jnp.moveaxis(result, 1, 0), 'blk', 0, 0, tiled=True)  21.9 us
    pallas_call x8, Pallas kernels, shards(): layer(scalars, whole, state, weights, norm_gain, qk, text_key, text_value...  21.9 us
  transfers between devices with their start and end apart: 18, of which 4 were waited for; matrix products, arithmetic and copies ran while one was open for 1% of the time, Pallas kernels for 1%

profile of v1, /device:TPU:14, one launch (start us, length us, event | category | flops | bytes accessed | tf_op | source)
XLA Modules:
  0.0 358.0 jit_solution(3559158441931958790)
XLA Ops:
  3.9 47.3 %all_to_all.50 = bf16[4,2,168,384]{3,2,1,0:T(8,128)(2,1)S(1)} all-to-all(bf16[4,2,168,384]{3,2,1,0:T(8,128)(2,1)S(1)} %reverse_select_fusion), channel_id=1, replica_groups={{0,4,32,36},{1,5,33,37},{2,6,34,38},{3,7,35,39},{8,12,40,44},{9,13,41,4..., dimensions={0} | all-to-all | bytes 2064384 | tf_op jit(solution)/shard_map/all_to_all | solution.py:166
  51.3 4.3 %collective-permute-start.1 = (bf16[4,168,384]{2,1,0:T(8,128)(2,1)S(1)}, bf16[4,168,384]{2,1,0:T(8,128)(2,1)S(1)}, u32[]{:S(2)}, u32[]{:S(2)}) collective-permute-start(bf16[4,168,384]{2,1,0:T(8,128)(2,1)S(1)} %get-tuple-element.43), channel_id=1, source_target_pairs={{0,18},{2,10},{1,17},{3,9},{4,22},{6,14},{5,21},{7,13},{32,50},{34... | collective-permute-start | bytes 1548296 | tf_op jit(solution)/shard_map/ppermute | solution.py:171
  55.6 1.3 collective-permute-start
  59.1 40.1 %collective-permute-done.1.refs_1_ = bf16[4,168,384]{2,1,0:T(8,128)(2,1)S(1)} collective-permute-done((bf16[4,168,384]{2,1,0:T(8,128)(2,1)S(1)}, bf16[4,168,384]{2,1,0:T(8,128)(2,1)S(1)}, u32[]{:S(2)}, u32[]{:S(2)}) %collective-permute-start.1) | collective-permute-done | bytes 516128 | tf_op jit(solution)/shard_map/ppermute | solution.py:171
  99.9 9.3 %collective-permute-done.refs_0_ = bf16[4,168,384]{2,1,0:T(8,128)(2,1)S(1)} collective-permute-done((bf16[4,168,384]{2,1,0:T(8,128)(2,1)S(1)}, bf16[4,168,384]{2,1,0:T(8,128)(2,1)S(1)}, u32[]{:S(2)}, u32[]{:S(2)}) %collective-permute-start) | collective-permute-done | bytes 516128 | tf_op jit(solution)/shard_map/ppermute | solution.py:171
  118.4 37.0 %all-to-all-start.1 = ((bf16[4,256,384]{2,1,0:T(8,128)(2,1)}), bf16[4,256,384]{2,1,0:T(8,128)(2,1)}, u32[]{:S(2)}, u32[]{:S(2)}) async-start(bf16[4,256,384]{2,1,0:T(8,128)(2,1)} %broadcast_in_dim.27), calls=%async_computation.1 | async-start | bytes 1572864 | tf_op jit(solution)/shard_map/all_to_all | solution.py:214
  156.6 1.3 dynamic_slice.6
  157.9 1.4 pad_add_fusion.scalars
  159.3 1.1 copy-done.14
  160.3 1.1 copy-done.19
  162.5 1.0 copy-done.23
  163.5 1.0 copy-done.25
  169.8 3.6 prepare.1
  180.0 3.2 layer.8
  184.9 13.7 %all_to_all.51.x_ref = bf16[4,256,384]{2,1,0:T(8,128)(2,1)S(1)} all-to-all(bf16[4,256,384]{2,1,0:T(8,128)(2,1)S(1)} %broadcast_in_dim.28), channel_id=1, replica_groups={{10,18,9,17},{12,20,11,19},{14,22,13,21},{8,16,15,23},{26,34,25,33},{28..., dimensions={0} | all-to-all | bytes 1572864 | tf_op jit(solution)/shard_map/all_to_all | solution.py:214
  198.6 2.6 layer.9
  201.9 12.8 %all_to_all.52.x_ref = bf16[4,256,384]{2,1,0:T(8,128)(2,1)S(1)} all-to-all(bf16[4,256,384]{2,1,0:T(8,128)(2,1)S(1)} %broadcast_in_dim.29), channel_id=1, replica_groups={{10,18,9,17},{12,20,11,19},{14,22,13,21},{8,16,15,23},{26,34,25,33},{28..., dimensions={0} | all-to-all | bytes 1572864 | tf_op jit(solution)/shard_map/all_to_all | solution.py:214
  214.8 2.6 layer.10
  218.1 12.2 %all_to_all.53.x_ref = bf16[4,256,384]{2,1,0:T(8,128)(2,1)S(1)} all-to-all(bf16[4,256,384]{2,1,0:T(8,128)(2,1)S(1)} %broadcast_in_dim.30), channel_id=1, replica_groups={{10,18,9,17},{12,20,11,19},{14,22,13,21},{8,16,15,23},{26,34,25,33},{28..., dimensions={0} | all-to-all | bytes 1572864 | tf_op jit(solution)/shard_map/all_to_all | solution.py:214
  230.3 2.6 layer.11
  233.7 12.2 %all_to_all.54.x_ref = bf16[4,256,384]{2,1,0:T(8,128)(2,1)S(1)} all-to-all(bf16[4,256,384]{2,1,0:T(8,128)(2,1)S(1)} %broadcast_in_dim.31), channel_id=1, replica_groups={{10,18,9,17},{12,20,11,19},{14,22,13,21},{8,16,15,23},{26,34,25,33},{28..., dimensions={0} | all-to-all | bytes 1572864 | tf_op jit(solution)/shard_map/all_to_all | solution.py:214
  245.8 2.6 layer.12
  249.2 12.1 %all_to_all.55.x_ref = bf16[4,256,384]{2,1,0:T(8,128)(2,1)S(1)} all-to-all(bf16[4,256,384]{2,1,0:T(8,128)(2,1)S(1)} %broadcast_in_dim.32), channel_id=1, replica_groups={{10,18,9,17},{12,20,11,19},{14,22,13,21},{8,16,15,23},{26,34,25,33},{28..., dimensions={0} | all-to-all | bytes 1572864 | tf_op jit(solution)/shard_map/all_to_all | solution.py:214
  261.3 2.6 layer.13
  264.7 12.2 %all_to_all.56.x_ref = bf16[4,256,384]{2,1,0:T(8,128)(2,1)S(1)} all-to-all(bf16[4,256,384]{2,1,0:T(8,128)(2,1)S(1)} %broadcast_in_dim.33), channel_id=1, replica_groups={{10,18,9,17},{12,20,11,19},{14,22,13,21},{8,16,15,23},{26,34,25,33},{28..., dimensions={0} | all-to-all | bytes 1572864 | tf_op jit(solution)/shard_map/all_to_all | solution.py:214
  276.9 2.6 layer.14
  282.6 7.4 %all-to-all-start.8 = ((bf16[4,256,384]{2,1,0:T(8,128)(2,1)}), bf16[4,256,384]{2,1,0:T(8,128)(2,1)}, u32[]{:S(2)}, u32[]{:S(2)}) async-start(bf16[4,256,384]{2,1,0:T(8,128)(2,1)} %broadcast_in_dim.34), calls=%async_computation.8 | async-start | bytes 1572864 | tf_op jit(solution)/shard_map/all_to_all | solution.py:214
  290.0 6.7 %all-to-all-done.8.x_ref = bf16[4,256,384]{2,1,0:T(8,128)(2,1)} async-done(((bf16[4,256,384]{2,1,0:T(8,128)(2,1)}), bf16[4,256,384]{2,1,0:T(8,128)(2,1)}, u32[]{:S(2)}, u32[]{:S(2)}) %all-to-all-start.8) | async-done | bytes 786464 | tf_op jit(solution)/shard_map/all_to_all | solution.py:214
  301.4 3.3 layer.15
  305.0 1.3 maximum_bitcast_fusion
  306.2 28.4 %all-to-all-start.9 = ((bf16[32,3,8,384]{3,2,1,0:T(8,128)(2,1)}), bf16[32,3,8,384]{3,2,1,0:T(8,128)(2,1)S(1)}, u32[]{:S(2)}, u32[]{:S(2)}) async-start(bf16[32,3,8,384]{3,2,1,0:T(8,128)(2,1)} %maximum_bitcast_fusion), calls=%async_computation.9 | async-start | bytes 1179648 | tf_op jit(solution)/shard_map/all_to_all | solution.py:230
  334.6 21.9 %all-to-all-done.9 = bf16[32,3,8,384]{3,2,1,0:T(8,128)(2,1)S(1)} async-done(((bf16[32,3,8,384]{3,2,1,0:T(8,128)(2,1)}), bf16[32,3,8,384]{3,2,1,0:T(8,128)(2,1)S(1)}, u32[]{:S(2)}, u32[]{:S(2)}) %all-to-all-start.9) | async-done | bytes 589856 | tf_op jit(solution)/shard_map/all_to_all | solution.py:230
  (203 shorter events, 43.2 us)
Async XLA Ops:
  51.3 47.9 %collective-permute-start.1 = (bf16[4,168,384]{2,1,0:T(8,128)(2,1)S(1)}, bf16[4,168,384]{2,1,0:T(8,128)(2,1)S(1)}, u32[]{:S(2)}, u32[]{:S(2)}) collective-permute-start(bf16[4,168,384]{2,1,0:T(8,128)(2,1)S(1)} %get-tuple-element.43), channel_id=1, source_target_pairs={{0,18},{2,10},{1,17},{3,9},{4,22},{6,14},{5,21},{7,13},{32,50},{34... | collective-permute-start | bytes 1548296 | tf_op jit(solution)/shard_map/ppermute | solution.py:171
  55.6 53.5 %collective-permute-start = (bf16[4,168,384]{2,1,0:T(8,128)(2,1)S(1)}, bf16[4,168,384]{2,1,0:T(8,128)(2,1)S(1)}, u32[]{:S(2)}, u32[]{:S(2)}) collective-permute-start(bf16[4,168,384]{2,1,0:T(8,128)(2,1)S(1)} %get-tuple-element.42), channel_id=1, source_target_pairs={{0,10},{2,18},{1,9},{3,17},{4,14},{6,22},{5,13},{7,21},{32,42},{34... | collective-permute-start | bytes 1548296 | tf_op jit(solution)/shard_map/ppermute | solution.py:171
  57.0 52.9 %collective-permute-start.3 = (bf16[4,168,384]{2,1,0:T(8,128)(2,1)S(1)}, bf16[4,168,384]{2,1,0:T(8,128)(2,1)S(1)}, u32[]{:S(2)}, u32[]{:S(2)}) collective-permute-start(bf16[4,168,384]{2,1,0:T(8,128)(2,1)S(1)} %get-tuple-element.43), channel_id=1, source_target_pairs={{8,18},{10,10},{9,17},{11,9},{12,22},{14,14},{13,21},{15,13},{40,5... | collective-permute-start | bytes 1548296 | tf_op jit(solution)/shard_map/ppermute | solution.py:171
  57.7 53.7 %collective-permute-start.2 = (bf16[4,168,384]{2,1,0:T(8,128)(2,1)S(1)}, bf16[4,168,384]{2,1,0:T(8,128)(2,1)S(1)}, u32[]{:S(2)}, u32[]{:S(2)}) collective-permute-start(bf16[4,168,384]{2,1,0:T(8,128)(2,1)S(1)} %get-tuple-element.42), channel_id=1, source_target_pairs={{8,10},{10,18},{9,9},{11,17},{12,14},{14,22},{13,13},{15,21},{40,4... | collective-permute-start | bytes 1548296 | tf_op jit(solution)/shard_map/ppermute | solution.py:171
  58.4 53.9 %collective-permute-start.5 = (bf16[4,168,384]{2,1,0:T(8,128)(2,1)S(1)}, bf16[4,168,384]{2,1,0:T(8,128)(2,1)S(1)}, u32[]{:S(2)}, u32[]{:S(2)}) collective-permute-start(bf16[4,168,384]{2,1,0:T(8,128)(2,1)S(1)} %get-tuple-element.43), channel_id=1, source_target_pairs={{16,18},{18,10},{17,17},{19,9},{20,22},{22,14},{21,21},{23,13},{48... | collective-permute-start | bytes 1548296 | tf_op jit(solution)/shard_map/ppermute | solution.py:171
  99.1 16.7 %copy-start.20 = (bf16[4,168,384]{2,1,0:T(8,128)(2,1)}, bf16[4,168,384]{2,1,0:T(8,128)(2,1)S(1)}, u32[]{:S(2)}) copy-start(bf16[4,168,384]{2,1,0:T(8,128)(2,1)S(1)} %collective-permute-done.1.refs_1_) | copy-start | bytes 1548292
  99.1 14.0 %collective-permute-start.4 = (bf16[4,168,384]{2,1,0:T(8,128)(2,1)S(1)}, bf16[4,168,384]{2,1,0:T(8,128)(2,1)S(1)}, u32[]{:S(2)}, u32[]{:S(2)}) collective-permute-start(bf16[4,168,384]{2,1,0:T(8,128)(2,1)S(1)} %get-tuple-element.42), channel_id=1, source_target_pairs={{16,10},{18,18},{17,9},{19,17},{20,14},{22,22},{21,13},{23,21},{48... | collective-permute-start | bytes 1548296 | tf_op jit(solution)/shard_map/ppermute | solution.py:171
  109.2 4.8 %collective-permute-start.7 = (bf16[4,168,384]{2,1,0:T(8,128)(2,1)S(1)}, bf16[4,168,384]{2,1,0:T(8,128)(2,1)S(1)}, u32[]{:S(2)}, u32[]{:S(2)}) collective-permute-start(bf16[4,168,384]{2,1,0:T(8,128)(2,1)S(1)} %get-tuple-element.43), channel_id=1, source_target_pairs={{24,18},{26,10},{25,17},{27,9},{28,22},{30,14},{29,21},{31,13},{56... | collective-permute-start | bytes 1548296 | tf_op jit(solution)/shard_map/ppermute | solution.py:171
  109.9 4.8 %collective-permute-start.6 = (bf16[4,168,384]{2,1,0:T(8,128)(2,1)S(1)}, bf16[4,168,384]{2,1,0:T(8,128)(2,1)S(1)}, u32[]{:S(2)}, u32[]{:S(2)}) collective-permute-start(bf16[4,168,384]{2,1,0:T(8,128)(2,1)S(1)} %get-tuple-element.42), channel_id=1, source_target_pairs={{24,10},{26,18},{25,9},{27,17},{28,14},{30,22},{29,13},{31,21},{56... | collective-permute-start | bytes 1548296 | tf_op jit(solution)/shard_map/ppermute | solution.py:171
  115.8 40.2 %copy-start.66 = (s32[4]{0:T(128)S(1)}, s32[4]{0:T(128)}, u32[]{:S(2)}) copy-start(s32[4]{0:T(128)} %param.15) | copy-start | bytes 52
  115.8 43.4 %copy-start.36 = (f32[1,1536]{1,0:T(1,128)S(1)}, f32[1,1536]{1,0:T(1,128)}, u32[]{:S(2)}) copy-start(f32[1,1536]{1,0:T(1,128)} %gain_ref.15) | copy-start | bytes 18436
  115.9 43.4 %copy-start.65 = (f32[1,2,128]{2,1,0:T(2,128)S(1)}, f32[1,2,128]{2,1,0:T(2,128)}, u32[]{:S(2)}) copy-start(f32[1,2,128]{2,1,0:T(2,128)} %param.12) | copy-start | bytes 3076
  115.9 43.3 %copy-start.13 = (bf16[4,2,2,2,3,8,384]{6,5,1,3,0,2,4:T(8,128)(2,1)}, bf16[4,2,2,2,3,8,384]{6,5,1,3,0,2,4:T(8,128)(2,1)S(1)}, u32[]{:S(2)}) copy-start(bf16[4,2,2,2,3,8,384]{6,5,1,3,0,2,4:T(8,128)(2,1)S(1)} %copy.35) | copy-start | bytes 1769476
  118.4 57.0 %all-to-all-start.1 = ((bf16[4,256,384]{2,1,0:T(8,128)(2,1)}), bf16[4,256,384]{2,1,0:T(8,128)(2,1)}, u32[]{:S(2)}, u32[]{:S(2)}) async-start(bf16[4,256,384]{2,1,0:T(8,128)(2,1)} %broadcast_in_dim.27), calls=%async_computation.1 | async-start | bytes 1572864 | tf_op jit(solution)/shard_map/all_to_all | solution.py:214
  184.0 0.8 collective-permute-start.8
  201.1 16.2 %copy-start.39 = (bf16[2,256,384]{2,1,0:T(8,128)(2,1)}, bf16[2,256,384]{2,1,0:T(8,128)(2,1)S(1)}, u32[]{:S(2)}) copy-start(bf16[2,256,384]{2,1,0:T(8,128)(2,1)S(1)} %get-tuple-element.40) | copy-start | bytes 1179652
  201.1 0.7 collective-permute-start.9
  217.3 15.5 %copy-start.41 = (bf16[2,256,384]{2,1,0:T(8,128)(2,1)}, bf16[2,256,384]{2,1,0:T(8,128)(2,1)S(1)}, u32[]{:S(2)}) copy-start(bf16[2,256,384]{2,1,0:T(8,128)(2,1)S(1)} %get-tuple-element.39) | copy-start | bytes 1179652
  217.3 15.5 %copy-start.55 = (bf16[256,384]{1,0:T(8,128)(2,1)}, bf16[256,384]{1,0:T(8,128)(2,1)S(1)}, u32[]{:S(2)}) copy-start(bf16[256,384]{1,0:T(8,128)(2,1)S(1)} %get-tuple-element.28) | copy-start | bytes 589828
  217.4 0.7 collective-permute-start.10
  232.9 15.5 %copy-start.43 = (bf16[2,256,384]{2,1,0:T(8,128)(2,1)}, bf16[2,256,384]{2,1,0:T(8,128)(2,1)S(1)}, u32[]{:S(2)}) copy-start(bf16[2,256,384]{2,1,0:T(8,128)(2,1)S(1)} %get-tuple-element.38) | copy-start | bytes 1179652
  232.9 15.5 %copy-start.57 = (bf16[256,384]{1,0:T(8,128)(2,1)}, bf16[256,384]{1,0:T(8,128)(2,1)S(1)}, u32[]{:S(2)}) copy-start(bf16[256,384]{1,0:T(8,128)(2,1)S(1)} %get-tuple-element.29) | copy-start | bytes 589828
  232.9 0.7 collective-permute-start.11
  248.4 15.5 %copy-start.45 = (bf16[2,256,384]{2,1,0:T(8,128)(2,1)}, bf16[2,256,384]{2,1,0:T(8,128)(2,1)S(1)}, u32[]{:S(2)}) copy-start(bf16[2,256,384]{2,1,0:T(8,128)(2,1)S(1)} %get-tuple-element.37) | copy-start | bytes 1179652
  248.4 15.5 %copy-start.59 = (bf16[256,384]{1,0:T(8,128)(2,1)}, bf16[256,384]{1,0:T(8,128)(2,1)S(1)}, u32[]{:S(2)}) copy-start(bf16[256,384]{1,0:T(8,128)(2,1)S(1)} %get-tuple-element.30) | copy-start | bytes 589828
  248.4 0.7 collective-permute-start.12
  263.9 15.5 %copy-start.47 = (bf16[2,256,384]{2,1,0:T(8,128)(2,1)}, bf16[2,256,384]{2,1,0:T(8,128)(2,1)S(1)}, u32[]{:S(2)}) copy-start(bf16[2,256,384]{2,1,0:T(8,128)(2,1)S(1)} %get-tuple-element.36) | copy-start | bytes 1179652
  263.9 15.5 %copy-start.61 = (bf16[256,384]{1,0:T(8,128)(2,1)}, bf16[256,384]{1,0:T(8,128)(2,1)S(1)}, u32[]{:S(2)}) copy-start(bf16[256,384]{1,0:T(8,128)(2,1)S(1)} %get-tuple-element.31) | copy-start | bytes 589828
  264.0 0.7 collective-permute-start.13
  280.3 0.7 collective-permute-start.14
  282.6 14.1 %all-to-all-start.8 = ((bf16[4,256,384]{2,1,0:T(8,128)(2,1)}), bf16[4,256,384]{2,1,0:T(8,128)(2,1)}, u32[]{:S(2)}, u32[]{:S(2)}) async-start(bf16[4,256,384]{2,1,0:T(8,128)(2,1)} %broadcast_in_dim.34), calls=%async_computation.8 | async-start | bytes 1572864 | tf_op jit(solution)/shard_map/all_to_all | solution.py:214
  306.2 50.3 %all-to-all-start.9 = ((bf16[32,3,8,384]{3,2,1,0:T(8,128)(2,1)}), bf16[32,3,8,384]{3,2,1,0:T(8,128)(2,1)S(1)}, u32[]{:S(2)}, u32[]{:S(2)}) async-start(bf16[32,3,8,384]{3,2,1,0:T(8,128)(2,1)} %maximum_bitcast_fusion), calls=%async_computation.9 | async-start | bytes 1179648 | tf_op jit(solution)/shard_map/all_to_all | solution.py:230
  (53 other events, 117.0 us)

commit v2 on v1

v2 whole, which is shorter than its diff:
```python
import functools
import jax
import jax.numpy as jnp
from jax import lax
from jax.experimental import pallas as pl
from jax.experimental.pallas import tpu as pltpu
from jax.sharding import PartitionSpec as P

AX = ("section", "blk", "head")
PLANE = ("blk", "head")
BF = jnp.bfloat16
F32 = jnp.float32
ROWS = 48
TAIL = 32
PIECE = 3 * ROWS + TAIL
HBM = pl.BlockSpec(memory_space=pltpu.HBM)
VMEM = pl.BlockSpec(memory_space=pltpu.VMEM)
SMEM = pl.BlockSpec(memory_space=pltpu.SMEM)


def at(section, z, y):
    return section * 64 + z * 8 + y


def ring_groups(sections):
    groups = []
    for s in range(sections):
        for i in range(8):
            groups.append([at(s, j, i) if s % 2 == 0 else at(s, i, j) for j in range(8)])
    return groups


def even_pairs(k, sections):
    return [
        (at(s, z, 2 * k + half), at(s, z, z // 2 * 2 + half))
        for s in range(0, sections, 2)
        for z in range(8)
        for half in range(2)
    ]


def odd_pairs(i, lane, sections):
    return [
        (at(s, 2 * i + low, y), at(s, y // 2 * 2 + (low ^ lane), y))
        for s in range(1, sections, 2)
        for low in range(2)
        for y in range(8)
    ]


def block_groups(odd):
    order = [(h, q) if odd else (q, h) for h in range(2) for q in range(2)]
    return [[at(0, 2 * i + z, 2 * j + y) for z, y in order] for i in range(4) for j in range(4)]


def hop_pairs(step):
    return [
        (at(step, 2 * m + i, 2 * m + j), at(step + 1, 2 * m + i, 2 * m + j))
        for m in range(4)
        for i in range(2)
        for j in range(2)
    ]


def position():
    section, blk, head = lax.axis_index("section"), lax.axis_index("blk"), lax.axis_index("head")
    z_low = lax.rem(blk // 4, 2)
    odd = lax.rem(section, 2)
    half = jnp.where(odd == 1, z_low, head)
    side = jnp.where(odd == 1, head, z_low)
    return section, odd, blk // 8, half, side


def head_norm(block, gain):
    mean = jnp.mean(block * block, axis=-1, keepdims=True)
    return block * lax.rsqrt(mean + 1e-06) * gain


def prep_kernel(heads, *refs):
    evens, odds, (text_ref, gain_ref, qk_ref) = refs[:4], refs[4:12], refs[12:15]
    w_ref, tk_ref, tv_ref, sk_ref, sv_ref, state_ref = refs[15:21]
    tails, stale_key, stale_value, state, sems = refs[21:]
    width = heads * 128
    _, odd, _, half, _ = position()

    def block_copies(source, block, first):
        row = block * ROWS
        if not isinstance(row, int):
            row = pl.multiple_of(row, 16)
        made = [
            pltpu.make_async_copy(
                source.at[pl.ds(part * ROWS, ROWS), :],
                w_ref.at[pl.ds(row, ROWS), pl.ds(part * width, width)],
                sems.at[first + part],
            )
            for part in range(3)
        ]
        made.append(
            pltpu.make_async_copy(
                source.at[pl.ds(3 * ROWS, TAIL), :], tails.at[block], sems.at[first + 3]
            )
        )
        return made

    even_copies = []
    for k in range(4):
        for z in range(8):
            even_copies += block_copies(evens[k].at[z], z * 4 + k, len(even_copies))
    odd_copies = []
    for i in range(4):
        for lane in range(2):
            z = 2 * i + (half if lane == 0 else 1 - half)
            for y_hi in range(4):
                odd_copies += block_copies(
                    odds[2 * i + lane].at[y_hi], z * 4 + y_hi, len(odd_copies)
                )

    @pl.when(odd == 0)
    def _():
        for copy in even_copies:
            copy.start()

    @pl.when(odd == 1)
    def _():
        for copy in odd_copies:
            copy.start()

    text = text_ref[...].astype(F32)
    mean = jnp.mean(text * text, axis=-1, keepdims=True)
    normed = (text * lax.rsqrt(mean + 1e-06) * gain_ref[...]).astype(BF)
    key_gain = qk_ref[1:2, :]

    @pl.when(odd == 0)
    def _():
        for copy in even_copies:
            copy.wait()

    @pl.when(odd == 1)
    def _():
        for copy in odd_copies:
            copy.wait()

    for b in range(32):
        tail = tails[b].astype(F32)
        stale_key[8 * b : 8 * b + 8, :] = tail[0:8]
        stale_value[8 * b : 8 * b + 8, :] = tail[8:16]
        state[8 * b : 8 * b + 8, :] = tail[16:24]
    sv_ref[...] = stale_value[...].astype(BF)
    state_ref[...] = state[...].astype(BF)
    kv = jnp.dot(normed, w_ref[:, width:], preferred_element_type=F32).astype(BF)
    for h in range(heads):
        cols = slice(h * 128, (h + 1) * 128)
        sk_ref[:, cols] = head_norm(stale_key[:, cols], key_gain).astype(BF)
        tk_ref[:, cols] = head_norm(kv[:, cols].astype(F32), key_gain).astype(BF)
    tv_ref[...] = kv[:, width:]


def layer_kernel(
    heads, flag_ref, patch_ref, text_len_ref, x_ref, w_ref, gain_ref, qk_ref, tk_ref, tv_ref,
    sk_ref, sv_ref, out_ref, cache_ref,
):
    width = heads * 128
    section, _, micro, half, side = position()
    stale, limit, text_limit = flag_ref[micro, section] == 1, patch_ref[micro], text_len_ref[0]
    own_ref = x_ref.at[2 * half + side]
    parts = [x_ref[q].astype(F32) for q in range(4)]
    total = sum(jnp.sum(part * part, axis=-1, keepdims=True) for part in parts)
    scale = lax.rsqrt(total / (4 * width) + 1e-06)
    normed = jnp.concatenate(
        [
            (part * scale * gain_ref[:, q * width : (q + 1) * width]).astype(BF)
            for q, part in enumerate(parts)
        ],
        axis=1,
    )
    projected = jnp.dot(normed, w_ref[...], preferred_element_type=F32)
    fresh = projected[:, width:].astype(BF)
    cache_ref[0] = fresh[:, :width]
    cache_ref[1] = fresh[:, width:]
    query_gain, key_gain = qk_ref[0:1, :], qk_ref[1:2, :]
    tokens = out_ref.shape[0]
    own_mask = lax.broadcasted_iota(jnp.int32, (tokens, tokens), 1) < limit
    text_mask = lax.broadcasted_iota(jnp.int32, (tokens, tk_ref.shape[0]), 1) < text_limit
    contract = (((1,), (1,)), ((), ()))
    for h in range(heads):
        cols = slice(h * 128, (h + 1) * 128)
        queries = head_norm(projected[:, cols], query_gain).astype(BF)
        keys = head_norm(fresh[:, cols].astype(F32), key_gain).astype(BF)
        keys = jnp.where(stale, sk_ref[:, cols], keys)
        values = jnp.where(stale, sv_ref[:, cols], fresh[:, width + h * 128 : width + (h + 1) * 128])
        own = lax.dot_general(queries, keys, contract, preferred_element_type=F32)
        own = jnp.where(own_mask, jnp.exp(own * 128 ** (-0.5)), 0.0)
        text = lax.dot_general(queries, tk_ref[:, cols], contract, preferred_element_type=F32)
        text = jnp.where(text_mask, jnp.exp(text * 128 ** (-0.5)), 0.0)
        numerator = jnp.dot(text.astype(BF), tv_ref[:, cols], preferred_element_type=F32)
        numerator += jnp.dot(own.astype(BF), values, preferred_element_type=F32)
        denominator = jnp.sum(own, axis=1, keepdims=True) + jnp.sum(text, axis=1, keepdims=True)
        out_ref[:, cols] = (own_ref[:, cols].astype(F32) + numerator / denominator).astype(BF)


def shards(
    hidden_in, w_qkv, norm_gain, qk_gain, text_states, text_len, patch_len, stale_flags, stale_kv
):
    sections = lax.axis_size("section")
    section = lax.axis_index("section")
    z = lax.axis_index("blk") // 4
    head = lax.axis_index("head")
    odd = section % 2 == 1
    micros, tok, half_width = hidden_in.shape
    width = half_width // 2
    heads = width // 128
    tokens, text_count, depth = 32 * tok, text_states.shape[1], text_states.shape[2]

    w = jnp.moveaxis(w_qkv[0], 1, 0).reshape(3, ROWS, 2, width)
    w = jnp.moveaxis(w, 2, 0).reshape(1, 2, 3 * ROWS, width)
    old = jnp.moveaxis(stale_kv[0].reshape(2, micros, tok, 2, width), (1, 3), (0, 1))
    first = jnp.moveaxis(hidden_in.reshape(micros, tok, 2, width), 2, 1)
    packed = jnp.concatenate(
        [
            jnp.broadcast_to(w, (micros,) + w.shape[1:]),
            old.reshape(micros, 2, 2 * tok, width),
            first,
            jnp.zeros((micros, 2, TAIL - 3 * tok, width), BF),
        ],
        axis=2,
    ).reshape(2 * micros, PIECE, width)
    ring = lax.all_to_all(packed, AX, 0, 0, axis_index_groups=ring_groups(sections), tiled=True)
    evens = [lax.ppermute(ring, AX, even_pairs(k, sections)) for k in range(4)]
    by_half = ring.reshape(4, 2, PIECE, width)
    low = z % 2 == 1
    lanes = (
        jnp.where(low, by_half[:, 1], by_half[:, 0]),
        jnp.where(low, by_half[:, 0], by_half[:, 1]),
    )
    odds = [
        lax.ppermute(lanes[lane], AX, odd_pairs(i, lane, sections))
        for i in range(4)
        for lane in range(2)
    ]

    qk = qk_gain[0]
    block = jax.ShapeDtypeStruct((tokens, width), BF)
    text_block = jax.ShapeDtypeStruct((text_count, width), BF)
    weights, text_key, text_value, stale_key, stale_value, state = pl.pallas_call(
        functools.partial(prep_kernel, heads),
        out_shape=[jax.ShapeDtypeStruct((depth, 3 * width), BF), text_block, text_block]
        + [block] * 3,
        in_specs=[HBM] * 12 + [VMEM] * 3,
        out_specs=[VMEM] * 6,
        scratch_shapes=[
            pltpu.VMEM((32, TAIL, width), BF),
            pltpu.VMEM((tokens, width), F32),
            pltpu.VMEM((tokens, width), F32),
            pltpu.VMEM((tokens, width), F32),
            pltpu.SemaphoreType.DMA((128,)),
        ],
        compiler_params=pltpu.CompilerParams(vmem_limit_bytes=40 * 2**20),
        name="prepare",
    )(*evens, *odds, text_states[0], norm_gain, qk)

    layer = pl.pallas_call(
        functools.partial(layer_kernel, heads),
        out_shape=[block, jax.ShapeDtypeStruct((2, tokens, width), BF)],
        in_specs=[SMEM] * 3 + [VMEM] * 8,
        out_specs=[VMEM] * 2,
        compiler_params=pltpu.CompilerParams(vmem_limit_bytes=40 * 2**20),
        name="layer",
    )

    def advance(step, entering):
        whole = lax.all_to_all(
            jnp.broadcast_to(entering[None], (4,) + entering.shape),
            PLANE, 0, 0,
            axis_index_groups=block_groups(step > 0 and step % 2 == 0),
            tiled=True,
        )
        return layer(
            stale_flags, patch_len, text_len, whole, weights, norm_gain, qk, text_key, text_value,
            stale_key, stale_value,
        )

    kept = (state, jnp.zeros((2, tokens, width), BF))
    for step in range(sections):
        entering = lax.ppermute(kept[0], AX, hop_pairs(step - 1)) if step else state
        kept = lax.cond(
            section == step,
            lambda entering, *kept: tuple(advance(step, entering)),
            lambda entering, *kept: tuple(kept),
            entering, *kept,
        )

    result = jnp.concatenate([kept[0][None], kept[1]]).reshape(3, 32, tok, width)
    result = lax.all_to_all(jnp.moveaxis(result, 1, 0), "blk", 0, 0, tiled=True)
    found = [
        jnp.stack([result[(2 * m + j) * 4 + m] for m in range(micros)]) for j in range(2)
    ]
    swap = [
        (at(s, 0, 0) + 2 * b + h, at(s, 0, 0) + 2 * b + 1 - h)
        for s in range(1, sections, 2)
        for b in range(32)
        for h in range(2)
    ]
    other = lax.ppermute(jnp.where(head == 0, found[1], found[0]), AX, swap)
    left = jnp.where(odd & (head == 1), other, found[0])
    right = jnp.where(odd & (head == 0), other, found[1])
    out = jnp.stack([left, right]).transpose(2, 1, 3, 0, 4)
    out = out.reshape(3, micros, tok, half_width)
    return (out[0][None], out[1:][None])


def solution(mesh):
    in_specs = (
        P(None, "blk", "head"),
        P("section", "blk", None, "head"),
        P("section", None),
        P("section", None, None),
        P("section", None, None),
        P(),
        P(),
        P(),
        P("section", None, None, "blk", "head"),
    )
    out_specs = (P("section", None, "blk", "head"), P("section", None, None, "blk", "head"))
    return jax.shard_map(shards, mesh=mesh, in_specs=in_specs, out_specs=out_specs, check_vma=False)
```

time: 360 us -> 297 us (0.82)
  the two profiles are of different devices: /device:TPU:14 before, /device:TPU:7 now
where the time goes in v2:
time: 297 us; the launch traced here: 295 us
  waiting for transfers between devices  209 us (70%)
  starting transfers between devices  34.5 us (12%)
  local copies, waits for them, and re-layouts  18.6 us (6%)
  blocking collectives  14.6 us (5%)
  Pallas kernels  10.9 us (4%)
  other arithmetic  5.36 us (2%)
    ppermute x7, waiting for transfers between devices, shards(): entering = lax.ppermute(kept[0], AX, hop_pairs(step - 1)) if step else state  133 us
    ppermute x8, waiting for transfers between devices, shards(): lax.ppermute(lanes[lane], AX, odd_pairs(i, lane, sections))  41.3 us
    all_to_all x1, waiting for transfers between devices, shards(): lax.all_to_all(packed, AX, 0, 0, axis_index_groups=ring_groups(sections),...  18.3 us
    all_to_all x1, blocking collectives, advance(): lax.all_to_all(jnp.broadcast_to(entering[None], (4,) + entering.shape), P...  14.6 us
    unnamed x38, local copies, waits for them, and re-layouts  14.1 us
    all_to_all x1, waiting for transfers between devices, shards(): result = lax.all_to_all(jnp.moveaxis(result, 1, 0), 'blk', 0, 0, tiled=True)  13.9 us
    ppermute x8, starting transfers between devices, shards(): lax.ppermute(lanes[lane], AX, odd_pairs(i, lane, sections))  12.7 us
    all_to_all x1, starting transfers between devices, shards(): lax.all_to_all(packed, AX, 0, 0, axis_index_groups=ring_groups(sections),...  6.82 us
  transfers between devices with their start and end apart: 22, of which 8 were waited for; matrix products, arithmetic and copies ran while one was open for 0% of the time, Pallas kernels for 0%

profile of v2, /device:TPU:7, one launch (start us, length us, event | category | flops | bytes accessed | tf_op | source)
XLA Modules:
  0.0 294.8 jit_solution(10918695799569605404)
XLA Ops:
  3.5 1.4 maximum_maximum_fusion
  4.9 6.8 %all-to-all-start.8 = ((bf16[8,176,384]{2,1,0:T(8,128)(2,1)}), bf16[8,176,384]{2,1,0:T(8,128)(2,1)}, u32[]{:S(2)}, u32[]{:S(2)}) async-start(bf16[8,176,384]{2,1,0:T(8,128)(2,1)} %maximum_maximum_fusion), calls=%async_computation.8 | async-start | bytes 2162688 | tf_op jit(solution)/shard_map/all_to_all | solution.py:227
  11.7 18.3 %all-to-all-done.8 = bf16[8,176,384]{2,1,0:T(8,128)(2,1)} async-done(((bf16[8,176,384]{2,1,0:T(8,128)(2,1)}), bf16[8,176,384]{2,1,0:T(8,128)(2,1)}, u32[]{:S(2)}, u32[]{:S(2)}) %all-to-all-start.8) | async-done | bytes 1081376 | tf_op jit(solution)/shard_map/all_to_all | solution.py:227
  30.0 2.1 select_bitcast_fusion
  32.1 1.3 collective-permute-start.10
  33.4 1.3 collective-permute-start.11
  35.4 4.3 %collective-permute-start.5 = (bf16[4,176,384]{2,1,0:T(8,128)(2,1)}, bf16[4,176,384]{2,1,0:T(8,128)(2,1)S(1)}, u32[]{:S(2)}, u32[]{:S(2)}) collective-permute-start(bf16[4,176,384]{2,1,0:T(8,128)(2,1)} %get-tuple-element.349), channel_id=1, source_target_pairs={{64,72},{65,73},{66,90},{67,91},{68,108},{69,109},{70,126},{71,127... | collective-permute-start | bytes 1622024 | tf_op jit(solution)/shard_map/ppermute | solution.py:236
  39.7 1.3 collective-permute-start.6
  41.0 8.0 %collective-permute-done.10.refs_10_ = bf16[4,176,384]{2,1,0:T(8,128)(2,1)S(1)} collective-permute-done((bf16[4,176,384]{2,1,0:T(8,128)(2,1)S(1)}, bf16[4,176,384]{2,1,0:T(8,128)(2,1)S(1)}, u32[]{:S(2)}, u32[]{:S(2)}) %collective-permute-start.10) | collective-permute-done | bytes 540704 | tf_op jit(solution)/shard_map/ppermute | solution.py:236
  49.8 1.3 collective-permute-start.7
  51.0 15.6 %collective-permute-done.11.refs_11_ = bf16[4,176,384]{2,1,0:T(8,128)(2,1)S(1)} collective-permute-done((bf16[4,176,384]{2,1,0:T(8,128)(2,1)}, bf16[4,176,384]{2,1,0:T(8,128)(2,1)S(1)}, u32[]{:S(2)}, u32[]{:S(2)}) %collective-permute-start.11) | collective-permute-done | bytes 540704 | tf_op jit(solution)/shard_map/ppermute | solution.py:236
  67.4 1.3 collective-permute-start.8
  74.2 1.7 collective-permute-start.3
  75.8 5.6 %collective-permute-done.8.refs_8_ = bf16[4,176,384]{2,1,0:T(8,128)(2,1)S(1)} collective-permute-done((bf16[4,176,384]{2,1,0:T(8,128)(2,1)S(1)}, bf16[4,176,384]{2,1,0:T(8,128)(2,1)S(1)}, u32[]{:S(2)}, u32[]{:S(2)}) %collective-permute-start.8) | collective-permute-done | bytes 540704 | tf_op jit(solution)/shard_map/ppermute | solution.py:236
  82.3 1.3 collective-permute-start.9
  83.6 12.1 %collective-permute-done.9.refs_9_ = bf16[4,176,384]{2,1,0:T(8,128)(2,1)} collective-permute-done((bf16[4,176,384]{2,1,0:T(8,128)(2,1)}, bf16[4,176,384]{2,1,0:T(8,128)(2,1)}, u32[]{:S(2)}, u32[]{:S(2)}) %collective-permute-start.9) | collective-permute-done | bytes 540704 | tf_op jit(solution)/shard_map/ppermute | solution.py:236
  95.7 1.1 copy-done
  96.9 1.0 copy-done.2
  97.9 1.0 copy-done.4
  99.0 1.0 copy-done.6
  100.0 1.0 copy-done.8
  104.2 5.6 %prepare.1 = (bf16[1536,1152]{1,0:T(8,128)(2,1)}, bf16[256,384]{1,0:T(8,128)(2,1)S(1)}, bf16[256,384]{1,0:T(8,128)(2,1)}, bf16[256,384]{1,0:T(8,128)(2,1)}, bf16...) custom-call(bf16[8,176,384]{2,1,0:T(8,128)(2,1)S(1)} %collective-permute-done.refs_0_, ...), custom_call_target="tpu_custom_call" | custom-call | tf_op jit(solution)/shard_map/prepare/pallas_call | solution.py:244
  114.3 1.3 collective-permute-start.18
  115.6 132.6 %collective-permute-done.18 = bf16[256,384]{1,0:T(8,128)(2,1)S(1)} collective-permute-done((bf16[256,384]{1,0:T(8,128)(2,1)}, bf16[256,384]{1,0:T(8,128)(2,1)S(1)}, u32[]{:S(2)}, u32[]{:S(2)}) %collective-permute-start.18) | collective-permute-done | bytes 196640 | tf_op jit(solution)/shard_map/ppermute | solution.py:284
  248.3 20.1 %conditional.15 = ((bf16[256,384]{1,0:T(8,128)(2,1)}, bf16[2,256,384]{2,1,0:T(8,128)(2,1)S(1)})) conditional(s32[]{:T(128)} %convert_element_type.24, (bf16[256,384]{1,0:T(8,128)(2,1)}, bf16[2,256,384]{2,1,0:T(8,128)(2,1)S(1)}) %get-tuple-element.401, (bf16[256,384]{1,0:T(8,128)(2,1)S(1)}, s32[4,8]{1,0:T(4,128)S(1)}, s32[4]{0:T(128)S(1)}, ...), branch_computations={%region_14.15_spmd, %region_15.16_spmd} | conditional | bytes 4915292 | solution.py:285
  248.3 14.6 %all_to_all.49.x_ref = bf16[4,256,384]{2,1,0:T(8,128)(2,1)S(1)} all-to-all(bf16[4,256,384]{2,1,0:T(8,128)(2,1)S(1)} %broadcast_in_dim.38), channel_id=1, replica_groups={{0,8,1,9},{2,10,3,11},{4,12,5,13},{6,14,7,15},{16,24,17,25},{18,26,19,2..., dimensions={0} | all-to-all | bytes 1572864 | tf_op jit(solution)/shard_map/cond/branch_1_fun/all_to_all | solution.py:271
  263.0 5.4 %layer.15 = (bf16[256,384]{1,0:T(8,128)(2,1)}, bf16[2,256,384]{2,1,0:T(8,128)(2,1)S(1)}) custom-call(s32[4,8]{1,0:T(4,128)S(1)} %get-tuple-element.298.flag_ref, s32[4]{0:T(128)S(1)} %get-tuple-element.299.patch_ref, s32[1]{0:T(128)} %get-tuple-element.300.text_len_ref, bf16[4,256,384]{2,1,0:T(8,128)(2,1)S(1)} %all_to_all.49.x_ref, ...), custom_call_target="tpu_custom_call" | custom-call | tf_op jit(solution)/shard_map/cond/branch_1_fun/layer/pallas_call | solution.py:277
  268.4 1.8 maximum_bitcast_fusion
  270.2 3.9 %all-to-all-start.9 = ((bf16[32,3,8,384]{3,2,1,0:T(8,128)(2,1)}), bf16[32,3,8,384]{3,2,1,0:T(8,128)(2,1)S(1)}, u32[]{:S(2)}, u32[]{:S(2)}) async-start(bf16[32,3,8,384]{3,2,1,0:T(8,128)(2,1)} %maximum_bitcast_fusion), calls=%async_computation.9 | async-start | bytes 1179648 | tf_op jit(solution)/shard_map/all_to_all | solution.py:293
  274.1 13.9 %all-to-all-done.9 = bf16[32,3,8,384]{3,2,1,0:T(8,128)(2,1)S(1)} async-done(((bf16[32,3,8,384]{3,2,1,0:T(8,128)(2,1)}), bf16[32,3,8,384]{3,2,1,0:T(8,128)(2,1)S(1)}, u32[]{:S(2)}, u32[]{:S(2)}) %all-to-all-start.9) | async-done | bytes 589856 | tf_op jit(solution)/shard_map/all_to_all | solution.py:293
  288.0 1.9 collective-permute-start.19
  290.0 3.1 %collective-permute-done.19 = bf16[4,3,8,384]{3,2,1,0:T(8,128)(2,1)S(1)} collective-permute-done((bf16[4,3,8,384]{3,2,1,0:T(8,128)(2,1)S(1)}, bf16[4,3,8,384]{3,2,1,0:T(8,128)(2,1)S(1)}, u32[]{:S(2)}, u32[]{:S(2)}) %collective-permute-start.19) | collective-permute-done | bytes 73760 | tf_op jit(solution)/shard_map/ppermute | solution.py:303
  (90 shorter events, 20.6 us)
Async XLA Ops:
  4.9 25.1 %all-to-all-start.8 = ((bf16[8,176,384]{2,1,0:T(8,128)(2,1)}), bf16[8,176,384]{2,1,0:T(8,128)(2,1)}, u32[]{:S(2)}, u32[]{:S(2)}) async-start(bf16[8,176,384]{2,1,0:T(8,128)(2,1)} %maximum_maximum_fusion), calls=%async_computation.8 | async-start | bytes 2162688 | tf_op jit(solution)/shard_map/all_to_all | solution.py:227
  30.0 65.8 %copy-start.39 = (f32[1,1536]{1,0:T(1,128)S(1)}, f32[1,1536]{1,0:T(1,128)}, u32[]{:S(2)}) copy-start(f32[1,1536]{1,0:T(1,128)} %refs_13_.1) | copy-start | bytes 18436
  30.0 65.8 %copy-start.41 = (f32[1,2,128]{2,1,0:T(2,128)S(1)}, f32[1,2,128]{2,1,0:T(2,128)}, u32[]{:S(2)}) copy-start(f32[1,2,128]{2,1,0:T(2,128)} %param.28) | copy-start | bytes 3076
  32.1 16.9 %collective-permute-start.10 = (bf16[4,176,384]{2,1,0:T(8,128)(2,1)S(1)}, bf16[4,176,384]{2,1,0:T(8,128)(2,1)S(1)}, u32[]{:S(2)}, u32[]{:S(2)}) collective-permute-start(bf16[4,176,384]{2,1,0:T(8,128)(2,1)S(1)} %get-tuple-element.350), channel_id=1, source_target_pairs={{112,64},{113,65},{114,82},{115,83},{116,100},{117,101},{118,118},... | collective-permute-start | bytes 1622024 | tf_op jit(solution)/shard_map/ppermute | solution.py:236
  33.4 33.2 %collective-permute-start.11 = (bf16[4,176,384]{2,1,0:T(8,128)(2,1)}, bf16[4,176,384]{2,1,0:T(8,128)(2,1)S(1)}, u32[]{:S(2)}, u32[]{:S(2)}) collective-permute-start(bf16[4,176,384]{2,1,0:T(8,128)(2,1)} %get-tuple-element.349), channel_id=1, source_target_pairs={{112,72},{113,73},{114,90},{115,91},{116,108},{117,109},{118,126},... | collective-permute-start | bytes 1622024 | tf_op jit(solution)/shard_map/ppermute | solution.py:236
  34.7 34.0 %collective-permute-start.4 = (bf16[4,176,384]{2,1,0:T(8,128)(2,1)S(1)}, bf16[4,176,384]{2,1,0:T(8,128)(2,1)S(1)}, u32[]{:S(2)}, u32[]{:S(2)}) collective-permute-start(bf16[4,176,384]{2,1,0:T(8,128)(2,1)S(1)} %get-tuple-element.350), channel_id=1, source_target_pairs={{64,64},{65,65},{66,82},{67,83},{68,100},{69,101},{70,118},{71,119... | collective-permute-start | bytes 1622024 | tf_op jit(solution)/shard_map/ppermute | solution.py:236
  35.4 34.9 %collective-permute-start.5 = (bf16[4,176,384]{2,1,0:T(8,128)(2,1)}, bf16[4,176,384]{2,1,0:T(8,128)(2,1)S(1)}, u32[]{:S(2)}, u32[]{:S(2)}) collective-permute-start(bf16[4,176,384]{2,1,0:T(8,128)(2,1)} %get-tuple-element.349), channel_id=1, source_target_pairs={{64,72},{65,73},{66,90},{67,91},{68,108},{69,109},{70,126},{71,127... | collective-permute-start | bytes 1622024 | tf_op jit(solution)/shard_map/ppermute | solution.py:236
  39.7 32.1 %collective-permute-start.6 = (bf16[4,176,384]{2,1,0:T(8,128)(2,1)S(1)}, bf16[4,176,384]{2,1,0:T(8,128)(2,1)S(1)}, u32[]{:S(2)}, u32[]{:S(2)}) collective-permute-start(bf16[4,176,384]{2,1,0:T(8,128)(2,1)S(1)} %get-tuple-element.350), channel_id=1, source_target_pairs={{80,64},{81,65},{82,82},{83,83},{84,100},{85,101},{86,118},{87,119... | collective-permute-start | bytes 1622024 | tf_op jit(solution)/shard_map/ppermute | solution.py:236
  49.8 23.6 %collective-permute-start.7 = (bf16[4,176,384]{2,1,0:T(8,128)(2,1)}, bf16[4,176,384]{2,1,0:T(8,128)(2,1)S(1)}, u32[]{:S(2)}, u32[]{:S(2)}) collective-permute-start(bf16[4,176,384]{2,1,0:T(8,128)(2,1)} %get-tuple-element.349), channel_id=1, source_target_pairs={{80,72},{81,73},{82,90},{83,91},{84,108},{85,109},{86,126},{87,127... | collective-permute-start | bytes 1622024 | tf_op jit(solution)/shard_map/ppermute | solution.py:236
  67.4 14.0 %collective-permute-start.8 = (bf16[4,176,384]{2,1,0:T(8,128)(2,1)S(1)}, bf16[4,176,384]{2,1,0:T(8,128)(2,1)S(1)}, u32[]{:S(2)}, u32[]{:S(2)}) collective-permute-start(bf16[4,176,384]{2,1,0:T(8,128)(2,1)S(1)} %get-tuple-element.350), channel_id=1, source_target_pairs={{96,64},{97,65},{98,82},{99,83},{100,100},{101,101},{102,118},{103... | collective-permute-start | bytes 1622024 | tf_op jit(solution)/shard_map/ppermute | solution.py:236
  69.5 26.2 %collective-permute-start = (bf16[8,176,384]{2,1,0:T(8,128)(2,1)}, bf16[8,176,384]{2,1,0:T(8,128)(2,1)S(1)}, u32[]{:S(2)}, u32[]{:S(2)}) collective-permute-start(bf16[8,176,384]{2,1,0:T(8,128)(2,1)} %all-to-all-done.8), channel_id=1, source_target_pairs={{0,0},{1,1},{8,8},{9,9},{16,18},{17,19},{24,26},{25,27},{32,36},{3... | collective-permute-start | bytes 3244040 | tf_op jit(solution)/shard_map/ppermute | solution.py:228
  71.1 24.6 %collective-permute-start.1 = (bf16[8,176,384]{2,1,0:T(8,128)(2,1)}, bf16[8,176,384]{2,1,0:T(8,128)(2,1)S(1)}, u32[]{:S(2)}, u32[]{:S(2)}) collective-permute-start(bf16[8,176,384]{2,1,0:T(8,128)(2,1)} %all-to-all-done.8), channel_id=1, source_target_pairs={{2,0},{3,1},{10,8},{11,9},{18,18},{19,19},{26,26},{27,27},{34,36},... | collective-permute-start | bytes 3244040 | tf_op jit(solution)/shard_map/ppermute | solution.py:228
  72.6 23.1 %collective-permute-start.2 = (bf16[8,176,384]{2,1,0:T(8,128)(2,1)}, bf16[8,176,384]{2,1,0:T(8,128)(2,1)S(1)}, u32[]{:S(2)}, u32[]{:S(2)}) collective-permute-start(bf16[8,176,384]{2,1,0:T(8,128)(2,1)} %all-to-all-done.8), channel_id=1, source_target_pairs={{4,0},{5,1},{12,8},{13,9},{20,18},{21,19},{28,26},{29,27},{36,36},... | collective-permute-start | bytes 3244040 | tf_op jit(solution)/shard_map/ppermute | solution.py:228
  74.2 21.5 %collective-permute-start.3 = (bf16[8,176,384]{2,1,0:T(8,128)(2,1)}, bf16[8,176,384]{2,1,0:T(8,128)(2,1)}, u32[]{:S(2)}, u32[]{:S(2)}) collective-permute-start(bf16[8,176,384]{2,1,0:T(8,128)(2,1)} %all-to-all-done.8), channel_id=1, source_target_pairs={{6,0},{7,1},{14,8},{15,9},{22,18},{23,19},{30,26},{31,27},{38,36},... | collective-permute-start | bytes 3244040 | tf_op jit(solution)/shard_map/ppermute | solution.py:228
  82.3 13.4 %collective-permute-start.9 = (bf16[4,176,384]{2,1,0:T(8,128)(2,1)}, bf16[4,176,384]{2,1,0:T(8,128)(2,1)}, u32[]{:S(2)}, u32[]{:S(2)}) collective-permute-start(bf16[4,176,384]{2,1,0:T(8,128)(2,1)} %get-tuple-element.349), channel_id=1, source_target_pairs={{96,72},{97,73},{98,90},{99,91},{100,108},{101,109},{102,126},{103... | collective-permute-start | bytes 1622024 | tf_op jit(solution)/shard_map/ppermute | solution.py:236
  95.7 1.1 copy-start
  99.0 1.0 copy-start.6
  100.0 1.0 copy-start.8
  104.2 5.6 %copy-start.40 = (s32[4,8]{1,0:T(4,128)S(1)}, s32[4,8]{1,0:T(4,128)}, u32[]{:S(2)}) copy-start(s32[4,8]{1,0:T(4,128)} %param.32) | copy-start | bytes 388
  104.2 5.6 %copy-start.42 = (s32[4]{0:T(128)S(1)}, s32[4]{0:T(128)}, u32[]{:S(2)}) copy-start(s32[4]{0:T(128)} %param.31) | copy-start | bytes 52
  109.9 0.7 collective-permute-start.12
  110.6 0.7 collective-permute-start.13
  111.5 0.7 collective-permute-start.14
  112.2 0.7 collective-permute-start.15
  112.9 0.7 collective-permute-start.16
  113.6 0.7 collective-permute-start.17
  114.3 133.9 %collective-permute-start.18 = (bf16[256,384]{1,0:T(8,128)(2,1)}, bf16[256,384]{1,0:T(8,128)(2,1)S(1)}, u32[]{:S(2)}, u32[]{:S(2)}) collective-permute-start(bf16[256,384]{1,0:T(8,128)(2,1)} %get-tuple-element.338), channel_id=1, source_target_pairs={{384,448},{385,449},{392,456},{393,457},{402,466},{403,467},{410,4... | collective-permute-start | bytes 589832 | tf_op jit(solution)/shard_map/ppermute | solution.py:284
  248.3 14.7 %copy-start.22 = (bf16[256,384]{1,0:T(8,128)(2,1)S(1)}, bf16[256,384]{1,0:T(8,128)(2,1)}, u32[]{:S(2)}) copy-start(bf16[256,384]{1,0:T(8,128)(2,1)} %get-tuple-element.306.tv_ref) | copy-start | bytes 589828 | tf_op jit(solution)/shard_map/cond
  248.3 14.7 %copy-start.30 = (bf16[256,384]{1,0:T(8,128)(2,1)S(1)}, bf16[256,384]{1,0:T(8,128)(2,1)}, u32[]{:S(2)}) copy-start(bf16[256,384]{1,0:T(8,128)(2,1)} %get-tuple-element.307.sk_ref) | copy-start | bytes 589828 | tf_op jit(solution)/shard_map/cond
  248.3 14.7 %copy-start.38 = (bf16[256,384]{1,0:T(8,128)(2,1)S(1)}, bf16[256,384]{1,0:T(8,128)(2,1)}, u32[]{:S(2)}) copy-start(bf16[256,384]{1,0:T(8,128)(2,1)} %get-tuple-element.308.sv_ref) | copy-start | bytes 589828 | tf_op jit(solution)/shard_map/cond
  270.2 17.8 %all-to-all-start.9 = ((bf16[32,3,8,384]{3,2,1,0:T(8,128)(2,1)}), bf16[32,3,8,384]{3,2,1,0:T(8,128)(2,1)S(1)}, u32[]{:S(2)}, u32[]{:S(2)}) async-start(bf16[32,3,8,384]{3,2,1,0:T(8,128)(2,1)} %maximum_bitcast_fusion), calls=%async_computation.9 | async-start | bytes 1179648 | tf_op jit(solution)/shard_map/all_to_all | solution.py:293
  288.0 5.1 %collective-permute-start.19 = (bf16[4,3,8,384]{3,2,1,0:T(8,128)(2,1)S(1)}, bf16[4,3,8,384]{3,2,1,0:T(8,128)(2,1)S(1)}, u32[]{:S(2)}, u32[]{:S(2)}) collective-permute-start(bf16[4,3,8,384]{3,2,1,0:T(8,128)(2,1)S(1)} %broadcast_select_fusion), channel_id=1, source_target_pairs={{64,65},{65,64},{66,67},{67,66},{68,69},{69,68},{70,71},{71,70},{7... | collective-permute-start | bytes 221192 | tf_op jit(solution)/shard_map/ppermute | solution.py:303
  (12 other events, 10.9 us)

commit v3 on v2

--- a/solution.py
+++ b/solution.py
@@ -13,6 +13,7 @@
 ROWS = 48
 TAIL = 32
 PIECE = 3 * ROWS + TAIL
+MOVES = [(2, 0), (2, 1), (1, 0), (1, 1), (3, 0), (3, 1), (0, 1)]
 HBM = pl.BlockSpec(memory_space=pltpu.HBM)
 VMEM = pl.BlockSpec(memory_space=pltpu.VMEM)
 SMEM = pl.BlockSpec(memory_space=pltpu.SMEM)
@@ -30,22 +31,20 @@
     return groups
 
 
-def even_pairs(k, sections):
-    return [
-        (at(s, z, 2 * k + half), at(s, z, z // 2 * 2 + half))
+def move_pairs(ahead, lane, sections):
+    even = [
+        (at(s, z, (2 * (z // 2 + ahead)) % 8 + half), at(s, z, z // 2 * 2 + half))
         for s in range(0, sections, 2)
         for z in range(8)
         for half in range(2)
     ]
-
-
-def odd_pairs(i, lane, sections):
-    return [
-        (at(s, 2 * i + low, y), at(s, y // 2 * 2 + (low ^ lane), y))
+    odd = [
+        (at(s, (2 * (y // 2 + ahead)) % 8 + low, y), at(s, y // 2 * 2 + (low ^ lane), y))
         for s in range(1, sections, 2)
         for low in range(2)
         for y in range(8)
     ]
+    return odd if ahead == 0 else even + odd
 
 
 def block_groups(odd):
@@ -77,16 +76,14 @@
 
 
 def prep_kernel(heads, *refs):
-    evens, odds, (text_ref, gain_ref, qk_ref) = refs[:4], refs[4:12], refs[12:15]
-    w_ref, tk_ref, tv_ref, sk_ref, sv_ref, state_ref = refs[15:21]
-    tails, stale_key, stale_value, state, sems = refs[21:]
+    pieces, (text_ref, gain_ref, qk_ref), w_ref = refs[:9], refs[9:12], refs[12]
+    tk_ref, tv_ref, sk_ref, sv_ref, state_ref = refs[13:18]
+    tails, stale_key, stale_value, state, sems = refs[18:]
     width = heads * 128
-    _, odd, _, half, _ = position()
+    _, odd, micro, half, _ = position()
 
     def block_copies(source, block, first):
-        row = block * ROWS
-        if not isinstance(row, int):
-            row = pl.multiple_of(row, 16)
+        row = pl.multiple_of(block * ROWS, 16)
         made = [
             pltpu.make_async_copy(
                 source.at[pl.ds(part * ROWS, ROWS), :],
@@ -102,18 +99,18 @@
         )
         return made
 
-    even_copies = []
-    for k in range(4):
-        for z in range(8):
-            even_copies += block_copies(evens[k].at[z], z * 4 + k, len(even_copies))
-    odd_copies = []
-    for i in range(4):
+    even_copies, odd_copies = [], []
+    for ahead in range(4):
+        far = lax.rem(micro + ahead, 4)
         for lane in range(2):
-            z = 2 * i + (half if lane == 0 else 1 - half)
-            for y_hi in range(4):
-                odd_copies += block_copies(
-                    odds[2 * i + lane].at[y_hi], z * 4 + y_hi, len(odd_copies)
-                )
+            local = 7 + lane
+            even_piece = pieces[MOVES.index((ahead, lane)) if ahead else local]
+            odd_piece = pieces[MOVES.index((ahead, lane)) if ahead or lane else local]
+            z = 2 * far + (half if lane == 0 else 1 - half)
+            for j in range(4):
+                first = len(even_copies)
+                even_copies += block_copies(even_piece.at[j], (4 * lane + j) * 4 + far, first)
+                odd_copies += block_copies(odd_piece.at[j], z * 4 + j, first)
 
     @pl.when(odd == 0)
     def _():
@@ -156,10 +153,16 @@
 
 
 def layer_kernel(
-    heads, flag_ref, patch_ref, text_len_ref, x_ref, w_ref, gain_ref, qk_ref, tk_ref, tv_ref,
-    sk_ref, sv_ref, out_ref, cache_ref,
+    heads, flag_ref, patch_ref, text_len_ref, x_ref, w_hbm, gain_ref, qk_ref, tk_ref, tv_ref,
+    sk_ref, sv_ref, out_ref, cache_ref, w_ref, sems,
 ):
     width = heads * 128
+    copies = [
+        pltpu.make_async_copy(w_hbm.at[:, part], w_ref.at[:, part], sems.at[k])
+        for k, part in enumerate((pl.ds(0, width), pl.ds(width, 2 * width)))
+    ]
+    for copy in copies:
+        copy.start()
     section, _, micro, half, side = position()
     stale, limit, text_limit = flag_ref[micro, section] == 1, patch_ref[micro], text_len_ref[0]
     own_ref = x_ref.at[2 * half + side]
@@ -173,28 +176,33 @@
         ],
         axis=1,
     )
-    projected = jnp.dot(normed, w_ref[...], preferred_element_type=F32)
-    fresh = projected[:, width:].astype(BF)
-    cache_ref[0] = fresh[:, :width]
-    cache_ref[1] = fresh[:, width:]
     query_gain, key_gain = qk_ref[0:1, :], qk_ref[1:2, :]
     tokens = out_ref.shape[0]
     own_mask = lax.broadcasted_iota(jnp.int32, (tokens, tokens), 1) < limit
     text_mask = lax.broadcasted_iota(jnp.int32, (tokens, tk_ref.shape[0]), 1) < text_limit
     contract = (((1,), (1,)), ((), ()))
-    for h in range(heads):
-        cols = slice(h * 128, (h + 1) * 128)
-        queries = head_norm(projected[:, cols], query_gain).astype(BF)
+    spans = [slice(h * 128, (h + 1) * 128) for h in range(heads)]
+    copies[0].wait()
+    projected = jnp.dot(normed, w_ref[:, :width], preferred_element_type=F32)
+    queries = [head_norm(projected[:, cols], query_gain).astype(BF) for cols in spans]
+    numerators, denominators = [], []
+    for h, cols in enumerate(spans):
+        text = lax.dot_general(queries[h], tk_ref[:, cols], contract, preferred_element_type=F32)
+        text = jnp.where(text_mask, jnp.exp(text * 128 ** (-0.5)), 0.0)
+        numerators.append(jnp.dot(text.astype(BF), tv_ref[:, cols], preferred_element_type=F32))
+        denominators.append(jnp.sum(text, axis=1, keepdims=True))
+    copies[1].wait()
+    fresh = jnp.dot(normed, w_ref[:, width:], preferred_element_type=F32).astype(BF)
+    cache_ref[0] = fresh[:, :width]
+    cache_ref[1] = fresh[:, width:]
+    for h, cols in enumerate(spans):
         keys = head_norm(fresh[:, cols].astype(F32), key_gain).astype(BF)
         keys = jnp.where(stale, sk_ref[:, cols], keys)
         values = jnp.where(stale, sv_ref[:, cols], fresh[:, width + h * 128 : width + (h + 1) * 128])
-        own = lax.dot_general(queries, keys, contract, preferred_element_type=F32)
+        own = lax.dot_general(queries[h], keys, contract, preferred_element_type=F32)
         own = jnp.where(own_mask, jnp.exp(own * 128 ** (-0.5)), 0.0)
-        text = lax.dot_general(queries, tk_ref[:, cols], contract, preferred_element_type=F32)
-        text = jnp.where(text_mask, jnp.exp(text * 128 ** (-0.5)), 0.0)
-        numerator = jnp.dot(text.astype(BF), tv_ref[:, cols], preferred_element_type=F32)
-        numerator += jnp.dot(own.astype(BF), values, preferred_element_type=F32)
-        denominator = jnp.sum(own, axis=1, keepdims=True) + jnp.sum(text, axis=1, keepdims=True)
+        numerator = numerators[h] + jnp.dot(own.astype(BF), values, preferred_element_type=F32)
+        denominator = denominators[h] + jnp.sum(own, axis=1, keepdims=True)
         out_ref[:, cols] = (own_ref[:, cols].astype(F32) + numerator / denominator).astype(BF)
 
 
@@ -225,18 +233,14 @@
         axis=2,
     ).reshape(2 * micros, PIECE, width)
     ring = lax.all_to_all(packed, AX, 0, 0, axis_index_groups=ring_groups(sections), tiled=True)
-    evens = [lax.ppermute(ring, AX, even_pairs(k, sections)) for k in range(4)]
     by_half = ring.reshape(4, 2, PIECE, width)
     low = z % 2 == 1
     lanes = (
-        jnp.where(low, by_half[:, 1], by_half[:, 0]),
-        jnp.where(low, by_half[:, 0], by_half[:, 1]),
+        jnp.where(odd, jnp.where(low, by_half[:, 1], by_half[:, 0]), ring[:4]),
+        jnp.where(odd, jnp.where(low, by_half[:, 0], by_half[:, 1]), ring[4:]),
     )
-    odds = [
-        lax.ppermute(lanes[lane], AX, odd_pairs(i, lane, sections))
-        for i in range(4)
-        for lane in range(2)
-    ]
+    pieces = [lax.ppermute(lanes[lane], AX, move_pairs(ahead, lane, sections)) for ahead, lane in MOVES]
+    pieces = [pltpu.with_memory_space_constraint(piece, pltpu.HBM) for piece in (*pieces, *lanes)]
 
     qk = qk_gain[0]
     block = jax.ShapeDtypeStruct((tokens, width), BF)
@@ -245,7 +249,7 @@
         functools.partial(prep_kernel, heads),
         out_shape=[jax.ShapeDtypeStruct((depth, 3 * width), BF), text_block, text_block]
         + [block] * 3,
-        in_specs=[HBM] * 12 + [VMEM] * 3,
+        in_specs=[HBM] * 9 + [VMEM] * 3,
         out_specs=[VMEM] * 6,
         scratch_shapes=[
             pltpu.VMEM((32, TAIL, width), BF),
@@ -254,16 +258,17 @@
             pltpu.VMEM((tokens, width), F32),
             pltpu.SemaphoreType.DMA((128,)),
         ],
-        compiler_params=pltpu.CompilerParams(vmem_limit_bytes=40 * 2**20),
+        compiler_params=pltpu.CompilerParams(vmem_limit_bytes=16 * 2**20),
         name="prepare",
-    )(*evens, *odds, text_states[0], norm_gain, qk)
+    )(*pieces, text_states[0], norm_gain, qk)
 
     layer = pl.pallas_call(
         functools.partial(layer_kernel, heads),
         out_shape=[block, jax.ShapeDtypeStruct((2, tokens, width), BF)],
-        in_specs=[SMEM] * 3 + [VMEM] * 8,
+        in_specs=[SMEM] * 3 + [VMEM] + [HBM] + [VMEM] * 6,
         out_specs=[VMEM] * 2,
-        compiler_params=pltpu.CompilerParams(vmem_limit_bytes=40 * 2**20),
+        scratch_shapes=[pltpu.VMEM((depth, 3 * width), BF), pltpu.SemaphoreType.DMA((2,))],
+        compiler_params=pltpu.CompilerParams(vmem_limit_bytes=16 * 2**20),
         name="layer",
     )
 
@@ -279,6 +284,7 @@
             stale_key, stale_value,
         )
 
+    weights = pltpu.with_memory_space_constraint(weights, pltpu.HBM)
     kept = (state, jnp.zeros((2, tokens, width), BF))
     for step in range(sections):
         entering = lax.ppermute(kept[0], AX, hop_pairs(step - 1)) if step else state

time: 297 us -> 265 us (0.89)
  local copies, waits for them, and re-layouts: 18.6 us -> 4.53 us
  waiting for transfers between devices: 209 us -> 201 us
  blocking collectives: 14.6 us -> 9.8 us
    unnamed x38 -> x20, local copies, waits for them, and re-layouts: 14.1 us -> 0.04 us
    ppermute x12 -> x7, waiting for transfers between devices: 41.3 us -> 35.1 us  [shards(): lax.ppermute(lanes[lane], AX, move_pairs(ahead, lane, sections))]
    ppermute x12 -> x7, starting transfers between devices: 16.5 us -> 10.9 us  [shards(): lax.ppermute(lanes[lane], AX, move_pairs(ahead, lane, sections))]
    all_to_all x1, blocking collectives: 14.6 us -> 9.8 us  [advance(): lax.all_to_all(jnp.broadcast_to(entering[None], (4,) + entering.shape), P...]
    all_to_all x1, starting transfers between devices: 3.9 us -> 8.06 us  [shards(): result = lax.all_to_all(jnp.moveaxis(result, 1, 0), 'blk', 0, 0, tiled=True)]
  transfers between devices with their start and end apart: 22 -> 17, of which waited for: 8 -> 8; matrix products, arithmetic and copies ran while one was open for 0% -> 0% of each run, Pallas kernels for 0% -> 0%
where the time goes in v3:
time: 265 us; the launch traced here: 264 us
  waiting for transfers between devices  201 us (76%)
  starting transfers between devices  34.1 us (13%)
  Pallas kernels  10.9 us (4%)
  blocking collectives  9.8 us (4%)
  local copies, waits for them, and re-layouts  4.53 us (2%)
    ppermute x7, waiting for transfers between devices, shards(): entering = lax.ppermute(kept[0], AX, hop_pairs(step - 1)) if step else state  131 us
    ppermute x7, waiting for transfers between devices, shards(): lax.ppermute(lanes[lane], AX, move_pairs(ahead, lane, sections))  35.1 us
    all_to_all x1, waiting for transfers between devices, shards(): lax.all_to_all(packed, AX, 0, 0, axis_index_groups=ring_groups(sections),...  18.2 us
    all_to_all x1, waiting for transfers between devices, shards(): result = lax.all_to_all(jnp.moveaxis(result, 1, 0), 'blk', 0, 0, tiled=True)  14 us
    ppermute x7, starting transfers between devices, shards(): lax.ppermute(lanes[lane], AX, move_pairs(ahead, lane, sections))  10.9 us
    all_to_all x1, blocking collectives, advance(): lax.all_to_all(jnp.broadcast_to(entering[None], (4,) + entering.shape), P...  9.8 us
    all_to_all x1, starting transfers between devices, shards(): result = lax.all_to_all(jnp.moveaxis(result, 1, 0), 'blk', 0, 0, tiled=True)  8.06 us
    all_to_all x1, starting transfers between devices, shards(): lax.all_to_all(packed, AX, 0, 0, axis_index_groups=ring_groups(sections),...  6.82 us
  transfers between devices with their start and end apart: 17, of which 8 were waited for; matrix products, arithmetic and copies ran while one was open for 0% of the time, Pallas kernels for 0%

profile of v3, /device:TPU:7, one launch (start us, length us, event | category | flops | bytes accessed | tf_op | source)
XLA Modules:
  0.0 264.1 jit_solution(722215950294087075)
XLA Ops:
  0.6 0.8 fusion.1
  1.4 1.0 reshape.52
  2.4 0.9 copy.28
  3.5 1.4 maximum_maximum_fusion
  4.9 6.8 %all-to-all-start.8 = ((bf16[8,176,384]{2,1,0:T(8,128)(2,1)}), bf16[8,176,384]{2,1,0:T(8,128)(2,1)S(1)}, u32[]{:S(2)}, u32[]{:S(2)}) async-start(bf16[8,176,384]{2,1,0:T(8,128)(2,1)} %maximum_maximum_fusion), calls=%async_computation.8 | async-start | bytes 2162688 | tf_op jit(solution)/shard_map/all_to_all | solution.py:235
  11.7 18.2 %all-to-all-done.8 = bf16[8,176,384]{2,1,0:T(8,128)(2,1)S(1)} async-done(((bf16[8,176,384]{2,1,0:T(8,128)(2,1)}), bf16[8,176,384]{2,1,0:T(8,128)(2,1)S(1)}, u32[]{:S(2)}, u32[]{:S(2)}) %all-to-all-start.8) | async-done | bytes 1081376 | tf_op jit(solution)/shard_map/all_to_all | solution.py:235
  30.0 1.4 collective-permute-start
  31.5 1.3 collective-permute-start.1
  32.8 1.3 collective-permute-start.2
  34.1 1.3 collective-permute-start.3
  35.4 1.3 collective-permute-start.4
  36.7 10.6 %collective-permute-done.refs_0_ = bf16[4,176,384]{2,1,0:T(8,128)(2,1)S(1)} collective-permute-done((bf16[4,176,384]{2,1,0:T(8,128)(2,1)S(1)}, bf16[4,176,384]{2,1,0:T(8,128)(2,1)S(1)}, u32[]{:S(2)}, u32[]{:S(2)}) %collective-permute-start) | collective-permute-done | bytes 540704 | tf_op jit(solution)/shard_map/ppermute | solution.py:242
  47.2 1.3 collective-permute-start.5
  48.5 4.5 %collective-permute-done.1.refs_1_ = bf16[4,176,384]{2,1,0:T(8,128)(2,1)S(1)} collective-permute-done((bf16[4,176,384]{2,1,0:T(8,128)(2,1)S(1)}, bf16[4,176,384]{2,1,0:T(8,128)(2,1)S(1)}, u32[]{:S(2)}, u32[]{:S(2)}) %collective-permute-start.1) | collective-permute-done | bytes 540704 | tf_op jit(solution)/shard_map/ppermute | solution.py:242
  53.1 3.0 %collective-permute-start.6 = (bf16[4,176,384]{2,1,0:T(8,128)(2,1)S(1)}, bf16[4,176,384]{2,1,0:T(8,128)(2,1)}, u32[]{:S(2)}, u32[]{:S(2)}) collective-permute-start(bf16[4,176,384]{2,1,0:T(8,128)(2,1)S(1)} %get-tuple-element.349.refs_8_), channel_id=1, source_target_pairs={{64,72},{65,73},{82,90},{83,91},{100,108},{101,109},{118,126},{119... | collective-permute-start | bytes 1622024 | tf_op jit(solution)/shard_map/ppermute | solution.py:242
  56.1 11.2 %collective-permute-done.2.refs_2_ = bf16[4,176,384]{2,1,0:T(8,128)(2,1)S(1)} collective-permute-done((bf16[4,176,384]{2,1,0:T(8,128)(2,1)S(1)}, bf16[4,176,384]{2,1,0:T(8,128)(2,1)S(1)}, u32[]{:S(2)}, u32[]{:S(2)}) %collective-permute-start.2) | collective-permute-done | bytes 540704 | tf_op jit(solution)/shard_map/ppermute | solution.py:242
  67.4 8.8 %collective-permute-done.5.refs_5_ = bf16[4,176,384]{2,1,0:T(8,128)(2,1)} collective-permute-done((bf16[4,176,384]{2,1,0:T(8,128)(2,1)S(1)}, bf16[4,176,384]{2,1,0:T(8,128)(2,1)}, u32[]{:S(2)}, u32[]{:S(2)}) %collective-permute-start.5) | collective-permute-done | bytes 540704 | tf_op jit(solution)/shard_map/ppermute | solution.py:242
  76.3 6.0 %prepare.1 = (bf16[1536,1152]{1,0:T(8,128)(2,1)}, bf16[256,384]{1,0:T(8,128)(2,1)S(1)}, bf16[256,384]{1,0:T(8,128)(2,1)S(1)}, bf16[256,384]{1,0:T(8,128)(2,1)S(1...) custom-call(bf16[4,176,384]{2,1,0:T(8,128)(2,1)} %copy-done.3, bf16[4,176,384]{2,1,0:T(8,128)(2,1)} %copy-done.4, ...), custom_call_target="tpu_custom_call" | custom-call | tf_op jit(solution)/shard_map/prepare/pallas_call | solution.py:248
  83.1 0.7 collective-permute-start.8
  84.0 0.7 collective-permute-start.9
  84.7 0.7 collective-permute-start.10
  86.8 1.3 collective-permute-start.13
  88.1 131.2 %collective-permute-done.13 = bf16[256,384]{1,0:T(8,128)(2,1)S(1)} collective-permute-done((bf16[256,384]{1,0:T(8,128)(2,1)S(1)}, bf16[256,384]{1,0:T(8,128)(2,1)S(1)}, u32[]{:S(2)}, u32[]{:S(2)}) %collective-permute-start.13) | collective-permute-done | bytes 196640 | tf_op jit(solution)/shard_map/ppermute | solution.py:290
  219.3 15.1 %conditional.15 = ((bf16[256,384]{1,0:T(8,128)(2,1)S(1)}, bf16[2,256,384]{2,1,0:T(8,128)(2,1)S(1)})) conditional(s32[]{:T(128)} %convert_element_type.24, (bf16[256,384]{1,0:T(8,128)(2,1)S(1)}, bf16[2,256,384]{2,1,0:T(8,128)(2,1)S(1)}) %get-tuple-element.401, (bf16[256,384]{1,0:T(8,128)(2,1)S(1)}, s32[4,8]{1,0:T(4,128)S(1)}, s32[4]{0:T(128)S(1)}, ...), branch_computations={%region_14.15_spmd, %region_15.16_spmd} | conditional | bytes 2555912 | solution.py:291
  219.4 9.8 %all_to_all.49.x_ref = bf16[4,256,384]{2,1,0:T(8,128)(2,1)S(1)} all-to-all(bf16[4,256,384]{2,1,0:T(8,128)(2,1)S(1)} %broadcast_in_dim.38), channel_id=1, replica_groups={{0,8,1,9},{2,10,3,11},{4,12,5,13},{6,14,7,15},{16,24,17,25},{18,26,19,2..., dimensions={0} | all-to-all | bytes 1572864 | tf_op jit(solution)/shard_map/cond/branch_1_fun/all_to_all | solution.py:276
  229.2 4.9 %layer.15 = (bf16[256,384]{1,0:T(8,128)(2,1)S(1)}, bf16[2,256,384]{2,1,0:T(8,128)(2,1)S(1)}) custom-call(s32[4,8]{1,0:T(4,128)S(1)} %get-tuple-element.298.flag_ref, s32[4]{0:T(128)S(1)} %get-tuple-element.299.patch_ref, s32[1]{0:T(128)} %get-tuple-element.300.text_len_ref, bf16[4,256,384]{2,1,0:T(8,128)(2,1)S(1)} %all_to_all.49.x_ref, ...), custom_call_target="tpu_custom_call" | custom-call | tf_op jit(solution)/shard_map/cond/branch_1_fun/layer/pallas_call | solution.py:282
  234.4 0.9 maximum_bitcast_fusion
  235.3 8.1 %all-to-all-start.9 = ((bf16[32,3,8,384]{3,2,1,0:T(8,128)(2,1)}), bf16[32,3,8,384]{3,2,1,0:T(8,128)(2,1)S(1)}, u32[]{:S(2)}, u32[]{:S(2)}) async-start(bf16[32,3,8,384]{3,2,1,0:T(8,128)(2,1)} %maximum_bitcast_fusion), calls=%async_computation.9 | async-start | bytes 1179648 | tf_op jit(solution)/shard_map/all_to_all | solution.py:299
  243.4 14.0 %all-to-all-done.9 = bf16[32,3,8,384]{3,2,1,0:T(8,128)(2,1)S(1)} async-done(((bf16[32,3,8,384]{3,2,1,0:T(8,128)(2,1)}), bf16[32,3,8,384]{3,2,1,0:T(8,128)(2,1)S(1)}, u32[]{:S(2)}, u32[]{:S(2)}) %all-to-all-start.9) | async-done | bytes 589856 | tf_op jit(solution)/shard_map/all_to_all | solution.py:299
  257.4 3.0 %collective-permute-start.14 = (bf16[4,3,8,384]{3,2,1,0:T(8,128)(2,1)S(1)}, bf16[4,3,8,384]{3,2,1,0:T(8,128)(2,1)S(1)}, u32[]{:S(2)}, u32[]{:S(2)}) collective-permute-start(bf16[4,3,8,384]{3,2,1,0:T(8,128)(2,1)S(1)} %broadcast_select_fusion), channel_id=1, source_target_pairs={{64,65},{65,64},{66,67},{67,66},{68,69},{69,68},{70,71},{71,70},{7... | collective-permute-start | bytes 221192 | tf_op jit(solution)/shard_map/ppermute | solution.py:309
  260.4 2.1 collective-permute-done.14
  262.7 0.7 broadcast_in_dim.54
  (56 shorter events, 3.8 us)
Async XLA Ops:
  4.9 25.0 %all-to-all-start.8 = ((bf16[8,176,384]{2,1,0:T(8,128)(2,1)}), bf16[8,176,384]{2,1,0:T(8,128)(2,1)S(1)}, u32[]{:S(2)}, u32[]{:S(2)}) async-start(bf16[8,176,384]{2,1,0:T(8,128)(2,1)} %maximum_maximum_fusion), calls=%async_computation.8 | async-start | bytes 2162688 | tf_op jit(solution)/shard_map/all_to_all | solution.py:235
  29.9 46.3 %copy-start = (bf16[1,256,1536]{2,1,0:T(8,128)(2,1)S(1)}, bf16[1,256,1536]{2,1,0:T(8,128)(2,1)}, u32[]{:S(2)}) copy-start(bf16[1,256,1536]{2,1,0:T(8,128)(2,1)} %param.29) | copy-start | bytes 2359300
  29.9 46.4 %copy-start.6 = (f32[1,1536]{1,0:T(1,128)S(1)}, f32[1,1536]{1,0:T(1,128)}, u32[]{:S(2)}) copy-start(f32[1,1536]{1,0:T(1,128)} %refs_10_.1) | copy-start | bytes 18436
  29.9 46.4 %copy-start.8 = (f32[1,2,128]{2,1,0:T(2,128)S(1)}, f32[1,2,128]{2,1,0:T(2,128)}, u32[]{:S(2)}) copy-start(f32[1,2,128]{2,1,0:T(2,128)} %param.28) | copy-start | bytes 3076
  30.0 46.2 %copy-start.1 = (bf16[4,176,384]{2,1,0:T(8,128)(2,1)}, bf16[4,176,384]{2,1,0:T(8,128)(2,1)S(1)}, u32[]{:S(2)}) copy-start(bf16[4,176,384]{2,1,0:T(8,128)(2,1)S(1)} %get-tuple-element.349.refs_8_) | copy-start | bytes 1622020
  30.0 46.2 %copy-start.2 = (bf16[4,176,384]{2,1,0:T(8,128)(2,1)}, bf16[4,176,384]{2,1,0:T(8,128)(2,1)S(1)}, u32[]{:S(2)}) copy-start(bf16[4,176,384]{2,1,0:T(8,128)(2,1)S(1)} %get-tuple-element.350.refs_7_) | copy-start | bytes 1622020
  30.0 17.2 %collective-permute-start = (bf16[4,176,384]{2,1,0:T(8,128)(2,1)S(1)}, bf16[4,176,384]{2,1,0:T(8,128)(2,1)S(1)}, u32[]{:S(2)}, u32[]{:S(2)}) collective-permute-start(bf16[4,176,384]{2,1,0:T(8,128)(2,1)S(1)} %get-tuple-element.350.refs_7_), channel_id=1, source_target_pairs={{4,0},{5,1},{12,8},{13,9},{22,18},{23,19},{30,26},{31,27},{32,36},... | collective-permute-start | bytes 1622024 | tf_op jit(solution)/shard_map/ppermute | solution.py:242
  31.5 21.6 %collective-permute-start.1 = (bf16[4,176,384]{2,1,0:T(8,128)(2,1)S(1)}, bf16[4,176,384]{2,1,0:T(8,128)(2,1)S(1)}, u32[]{:S(2)}, u32[]{:S(2)}) collective-permute-start(bf16[4,176,384]{2,1,0:T(8,128)(2,1)S(1)} %get-tuple-element.349.refs_8_), channel_id=1, source_target_pairs={{4,0},{5,1},{12,8},{13,9},{22,18},{23,19},{30,26},{31,27},{32,36},... | collective-permute-start | bytes 1622024 | tf_op jit(solution)/shard_map/ppermute | solution.py:242
  32.8 34.6 %collective-permute-start.2 = (bf16[4,176,384]{2,1,0:T(8,128)(2,1)S(1)}, bf16[4,176,384]{2,1,0:T(8,128)(2,1)S(1)}, u32[]{:S(2)}, u32[]{:S(2)}) collective-permute-start(bf16[4,176,384]{2,1,0:T(8,128)(2,1)S(1)} %get-tuple-element.350.refs_7_), channel_id=1, source_target_pairs={{2,0},{3,1},{10,8},{11,9},{20,18},{21,19},{28,26},{29,27},{38,36},... | collective-permute-start | bytes 1622024 | tf_op jit(solution)/shard_map/ppermute | solution.py:242
  34.1 33.3 %collective-permute-start.3 = (bf16[4,176,384]{2,1,0:T(8,128)(2,1)S(1)}, bf16[4,176,384]{2,1,0:T(8,128)(2,1)}, u32[]{:S(2)}, u32[]{:S(2)}) collective-permute-start(bf16[4,176,384]{2,1,0:T(8,128)(2,1)S(1)} %get-tuple-element.349.refs_8_), channel_id=1, source_target_pairs={{2,0},{3,1},{10,8},{11,9},{20,18},{21,19},{28,26},{29,27},{38,36},... | collective-permute-start | bytes 1622024 | tf_op jit(solution)/shard_map/ppermute | solution.py:242
  35.4 32.0 %collective-permute-start.4 = (bf16[4,176,384]{2,1,0:T(8,128)(2,1)S(1)}, bf16[4,176,384]{2,1,0:T(8,128)(2,1)}, u32[]{:S(2)}, u32[]{:S(2)}) collective-permute-start(bf16[4,176,384]{2,1,0:T(8,128)(2,1)S(1)} %get-tuple-element.350.refs_7_), channel_id=1, source_target_pairs={{6,0},{7,1},{14,8},{15,9},{16,18},{17,19},{24,26},{25,27},{34,36},... | collective-permute-start | bytes 1622024 | tf_op jit(solution)/shard_map/ppermute | solution.py:242
  47.2 28.9 %copy-start.3 = (bf16[4,176,384]{2,1,0:T(8,128)(2,1)}, bf16[4,176,384]{2,1,0:T(8,128)(2,1)S(1)}, u32[]{:S(2)}) copy-start(bf16[4,176,384]{2,1,0:T(8,128)(2,1)S(1)} %collective-permute-done.refs_0_) | copy-start | bytes 1622020
  47.2 28.9 %collective-permute-start.5 = (bf16[4,176,384]{2,1,0:T(8,128)(2,1)S(1)}, bf16[4,176,384]{2,1,0:T(8,128)(2,1)}, u32[]{:S(2)}, u32[]{:S(2)}) collective-permute-start(bf16[4,176,384]{2,1,0:T(8,128)(2,1)S(1)} %get-tuple-element.349.refs_8_), channel_id=1, source_target_pairs={{6,0},{7,1},{14,8},{15,9},{16,18},{17,19},{24,26},{25,27},{34,36},... | collective-permute-start | bytes 1622024 | tf_op jit(solution)/shard_map/ppermute | solution.py:242
  53.1 23.1 %copy-start.4 = (bf16[4,176,384]{2,1,0:T(8,128)(2,1)}, bf16[4,176,384]{2,1,0:T(8,128)(2,1)S(1)}, u32[]{:S(2)}) copy-start(bf16[4,176,384]{2,1,0:T(8,128)(2,1)S(1)} %collective-permute-done.1.refs_1_) | copy-start | bytes 1622020
  53.1 23.1 %collective-permute-start.6 = (bf16[4,176,384]{2,1,0:T(8,128)(2,1)S(1)}, bf16[4,176,384]{2,1,0:T(8,128)(2,1)}, u32[]{:S(2)}, u32[]{:S(2)}) collective-permute-start(bf16[4,176,384]{2,1,0:T(8,128)(2,1)S(1)} %get-tuple-element.349.refs_8_), channel_id=1, source_target_pairs={{64,72},{65,73},{82,90},{83,91},{100,108},{101,109},{118,126},{119... | collective-permute-start | bytes 1622024 | tf_op jit(solution)/shard_map/ppermute | solution.py:242
  67.4 8.8 %copy-start.5 = (bf16[4,176,384]{2,1,0:T(8,128)(2,1)}, bf16[4,176,384]{2,1,0:T(8,128)(2,1)S(1)}, u32[]{:S(2)}) copy-start(bf16[4,176,384]{2,1,0:T(8,128)(2,1)S(1)} %collective-permute-done.2.refs_2_) | copy-start | bytes 1622020
  76.2 6.0 %copy-start.7 = (s32[4,8]{1,0:T(4,128)S(1)}, s32[4,8]{1,0:T(4,128)}, u32[]{:S(2)}) copy-start(s32[4,8]{1,0:T(4,128)} %param.32) | copy-start | bytes 388
  76.2 6.0 %copy-start.9 = (s32[4]{0:T(128)S(1)}, s32[4]{0:T(128)}, u32[]{:S(2)}) copy-start(s32[4]{0:T(128)} %param.31) | copy-start | bytes 52
  82.4 0.7 collective-permute-start.7
  83.1 0.7 collective-permute-start.8
  84.0 0.7 collective-permute-start.9
  84.7 0.7 collective-permute-start.10
  85.4 0.7 collective-permute-start.11
  86.1 0.7 collective-permute-start.12
  86.8 132.5 %collective-permute-start.13 = (bf16[256,384]{1,0:T(8,128)(2,1)S(1)}, bf16[256,384]{1,0:T(8,128)(2,1)S(1)}, u32[]{:S(2)}, u32[]{:S(2)}) collective-permute-start(bf16[256,384]{1,0:T(8,128)(2,1)S(1)} %get-tuple-element.338), channel_id=1, source_target_pairs={{384,448},{385,449},{392,456},{393,457},{402,466},{403,467},{410,4... | collective-permute-start | bytes 589832 | tf_op jit(solution)/shard_map/ppermute | solution.py:290
  235.3 22.1 %all-to-all-start.9 = ((bf16[32,3,8,384]{3,2,1,0:T(8,128)(2,1)}), bf16[32,3,8,384]{3,2,1,0:T(8,128)(2,1)S(1)}, u32[]{:S(2)}, u32[]{:S(2)}) async-start(bf16[32,3,8,384]{3,2,1,0:T(8,128)(2,1)} %maximum_bitcast_fusion), calls=%async_computation.9 | async-start | bytes 1179648 | tf_op jit(solution)/shard_map/all_to_all | solution.py:299
  257.4 5.1 %collective-permute-start.14 = (bf16[4,3,8,384]{3,2,1,0:T(8,128)(2,1)S(1)}, bf16[4,3,8,384]{3,2,1,0:T(8,128)(2,1)S(1)}, u32[]{:S(2)}, u32[]{:S(2)}) collective-permute-start(bf16[4,3,8,384]{3,2,1,0:T(8,128)(2,1)S(1)} %broadcast_select_fusion), channel_id=1, source_target_pairs={{64,65},{65,64},{66,67},{67,66},{68,69},{69,68},{70,71},{71,70},{7... | collective-permute-start | bytes 221192 | tf_op jit(solution)/shard_map/ppermute | solution.py:309

commit v4 on v3

--- a/solution.py
+++ b/solution.py
@@ -13,7 +13,7 @@
 ROWS = 48
 TAIL = 32
 PIECE = 3 * ROWS + TAIL
-MOVES = [(2, 0), (2, 1), (1, 0), (1, 1), (3, 0), (3, 1), (0, 1)]
+MOVES = [(0, 1), (2, 0), (1, 0), (3, 0), (2, 1), (1, 1), (3, 1)]
 HBM = pl.BlockSpec(memory_space=pltpu.HBM)
 VMEM = pl.BlockSpec(memory_space=pltpu.VMEM)
 SMEM = pl.BlockSpec(memory_space=pltpu.SMEM)
@@ -75,19 +75,39 @@
     return block * lax.rsqrt(mean + 1e-06) * gain
 
 
+def pack_kernel(w_ref, stale_ref, hidden_ref, out_ref):
+    micros, width = hidden_ref.shape[0], out_ref.shape[2]
+    sides = [slice(0, width), slice(width, 2 * width)]
+    for m in range(micros):
+        states = [hidden_ref[m, :, cols].astype(F32) for cols in sides]
+        states = jnp.concatenate(states, axis=0).astype(BF)
+        for side, cols in enumerate(sides):
+            place = 2 * m + side
+            for part in range(3):
+                out_ref[place, part * ROWS : (part + 1) * ROWS, :] = w_ref[part, :, cols]
+            old = [stale_ref[part, m, :, cols].astype(F32) for part in range(2)]
+            old = jnp.concatenate(old, axis=0).astype(BF)
+            out_ref[place, 3 * ROWS : 3 * ROWS + 16, :] = old
+            out_ref[place, 3 * ROWS + 16 : PIECE, :] = states
+
+
 def prep_kernel(heads, *refs):
-    pieces, (text_ref, gain_ref, qk_ref), w_ref = refs[:9], refs[9:12], refs[12]
-    tk_ref, tv_ref, sk_ref, sv_ref, state_ref = refs[13:18]
-    tails, stale_key, stale_value, state, sems = refs[18:]
+    flag_ref, patch_ref, text_len_ref, text_ref, gain_ref, qk_ref = refs[:6]
+    pieces, (w_ref, info_ref), refs = refs[6:15], refs[15:17], refs[17:]
+    tk_ref, tv_ref, sk_ref, sv_ref, state_ref = refs[:5]
+    tails, held, stale_key, stale_value, state, sems = refs[5:]
     width = heads * 128
-    _, odd, micro, half, _ = position()
+    section, odd, micro, half, _ = position()
+    line = lax.broadcasted_iota(jnp.int32, info_ref.shape, 0)
+    limits = jnp.where(line == 1, patch_ref[micro], text_len_ref[0])
+    info_ref[...] = jnp.where(line == 0, flag_ref[micro, section], limits)
 
     def block_copies(source, block, first):
         row = pl.multiple_of(block * ROWS, 16)
         made = [
             pltpu.make_async_copy(
                 source.at[pl.ds(part * ROWS, ROWS), :],
-                w_ref.at[pl.ds(row, ROWS), pl.ds(part * width, width)],
+                held.at[pl.ds(row, ROWS), pl.ds(part * width, width)],
                 sems.at[first + part],
             )
             for part in range(3)
@@ -137,34 +157,32 @@
         for copy in odd_copies:
             copy.wait()
 
+    store = pltpu.make_async_copy(held, w_ref, sems.at[128])
+    store.start()
     for b in range(32):
         tail = tails[b].astype(F32)
         stale_key[8 * b : 8 * b + 8, :] = tail[0:8]
         stale_value[8 * b : 8 * b + 8, :] = tail[8:16]
-        state[8 * b : 8 * b + 8, :] = tail[16:24]
+        state[0, 8 * b : 8 * b + 8, :] = tail[16:24]
+        state[1, 8 * b : 8 * b + 8, :] = tail[24:32]
     sv_ref[...] = stale_value[...].astype(BF)
     state_ref[...] = state[...].astype(BF)
-    kv = jnp.dot(normed, w_ref[:, width:], preferred_element_type=F32).astype(BF)
+    kv = jnp.dot(normed, held[:, width:], preferred_element_type=F32).astype(BF)
     for h in range(heads):
         cols = slice(h * 128, (h + 1) * 128)
         sk_ref[:, cols] = head_norm(stale_key[:, cols], key_gain).astype(BF)
         tk_ref[:, cols] = head_norm(kv[:, cols].astype(F32), key_gain).astype(BF)
     tv_ref[...] = kv[:, width:]
+    store.wait()
 
 
 def layer_kernel(
-    heads, flag_ref, patch_ref, text_len_ref, x_ref, w_hbm, gain_ref, qk_ref, tk_ref, tv_ref,
-    sk_ref, sv_ref, out_ref, cache_ref, w_ref, sems,
+    heads, info_ref, x_ref, w_ref, gain_ref, qk_ref, tk_ref, tv_ref,
+    sk_ref, sv_ref, out_ref, cache_ref,
 ):
     width = heads * 128
-    copies = [
-        pltpu.make_async_copy(w_hbm.at[:, part], w_ref.at[:, part], sems.at[k])
-        for k, part in enumerate((pl.ds(0, width), pl.ds(width, 2 * width)))
-    ]
-    for copy in copies:
-        copy.start()
-    section, _, micro, half, side = position()
-    stale, limit, text_limit = flag_ref[micro, section] == 1, patch_ref[micro], text_len_ref[0]
+    _, _, _, half, side = position()
+    stale, limit, text_limit = info_ref[0:1, :] == 1, info_ref[1:2, 0:1], info_ref[2:3, 0:1]
     own_ref = x_ref.at[2 * half + side]
     parts = [x_ref[q].astype(F32) for q in range(4)]
     total = sum(jnp.sum(part * part, axis=-1, keepdims=True) for part in parts)
@@ -176,33 +194,28 @@
         ],
         axis=1,
     )
+    projected = jnp.dot(normed, w_ref[...], preferred_element_type=F32)
+    fresh = projected[:, width:].astype(BF)
+    cache_ref[0] = fresh[:, :width]
+    cache_ref[1] = fresh[:, width:]
     query_gain, key_gain = qk_ref[0:1, :], qk_ref[1:2, :]
     tokens = out_ref.shape[0]
     own_mask = lax.broadcasted_iota(jnp.int32, (tokens, tokens), 1) < limit
     text_mask = lax.broadcasted_iota(jnp.int32, (tokens, tk_ref.shape[0]), 1) < text_limit
     contract = (((1,), (1,)), ((), ()))
-    spans = [slice(h * 128, (h + 1) * 128) for h in range(heads)]
-    copies[0].wait()
-    projected = jnp.dot(normed, w_ref[:, :width], preferred_element_type=F32)
-    queries = [head_norm(projected[:, cols], query_gain).astype(BF) for cols in spans]
-    numerators, denominators = [], []
-    for h, cols in enumerate(spans):
-        text = lax.dot_general(queries[h], tk_ref[:, cols], contract, preferred_element_type=F32)
-        text = jnp.where(text_mask, jnp.exp(text * 128 ** (-0.5)), 0.0)
-        numerators.append(jnp.dot(text.astype(BF), tv_ref[:, cols], preferred_element_type=F32))
-        denominators.append(jnp.sum(text, axis=1, keepdims=True))
-    copies[1].wait()
-    fresh = jnp.dot(normed, w_ref[:, width:], preferred_element_type=F32).astype(BF)
-    cache_ref[0] = fresh[:, :width]
-    cache_ref[1] = fresh[:, width:]
-    for h, cols in enumerate(spans):
+    for h in range(heads):
+        cols = slice(h * 128, (h + 1) * 128)
+        queries = head_norm(projected[:, cols], query_gain).astype(BF)
         keys = head_norm(fresh[:, cols].astype(F32), key_gain).astype(BF)
         keys = jnp.where(stale, sk_ref[:, cols], keys)
         values = jnp.where(stale, sv_ref[:, cols], fresh[:, width + h * 128 : width + (h + 1) * 128])
-        own = lax.dot_general(queries[h], keys, contract, preferred_element_type=F32)
+        own = lax.dot_general(queries, keys, contract, preferred_element_type=F32)
         own = jnp.where(own_mask, jnp.exp(own * 128 ** (-0.5)), 0.0)
-        numerator = numerators[h] + jnp.dot(own.astype(BF), values, preferred_element_type=F32)
-        denominator = denominators[h] + jnp.sum(own, axis=1, keepdims=True)
+        text = lax.dot_general(queries, tk_ref[:, cols], contract, preferred_element_type=F32)
+        text = jnp.where(text_mask, jnp.exp(text * 128 ** (-0.5)), 0.0)
+        numerator = jnp.dot(text.astype(BF), tv_ref[:, cols], preferred_element_type=F32)
+        numerator += jnp.dot(own.astype(BF), values, preferred_element_type=F32)
+        denominator = jnp.sum(own, axis=1, keepdims=True) + jnp.sum(text, axis=1, keepdims=True)
         out_ref[:, cols] = (own_ref[:, cols].astype(F32) + numerator / denominator).astype(BF)
 
 
@@ -219,19 +232,18 @@
     heads = width // 128
     tokens, text_count, depth = 32 * tok, text_states.shape[1], text_states.shape[2]
 
-    w = jnp.moveaxis(w_qkv[0], 1, 0).reshape(3, ROWS, 2, width)
-    w = jnp.moveaxis(w, 2, 0).reshape(1, 2, 3 * ROWS, width)
-    old = jnp.moveaxis(stale_kv[0].reshape(2, micros, tok, 2, width), (1, 3), (0, 1))
-    first = jnp.moveaxis(hidden_in.reshape(micros, tok, 2, width), 2, 1)
-    packed = jnp.concatenate(
-        [
-            jnp.broadcast_to(w, (micros,) + w.shape[1:]),
-            old.reshape(micros, 2, 2 * tok, width),
-            first,
-            jnp.zeros((micros, 2, TAIL - 3 * tok, width), BF),
-        ],
-        axis=2,
-    ).reshape(2 * micros, PIECE, width)
+    sources = [
+        pltpu.with_memory_space_constraint(source, pltpu.HBM)
+        for source in (jnp.moveaxis(w_qkv[0], 1, 0), stale_kv[0], hidden_in)
+    ]
+    packed = pl.pallas_call(
+        pack_kernel,
+        out_shape=jax.ShapeDtypeStruct((2 * micros, PIECE, width), BF),
+        in_specs=[VMEM] * 3,
+        out_specs=VMEM,
+        compiler_params=pltpu.CompilerParams(vmem_limit_bytes=16 * 2**20),
+        name="pack",
+    )(*sources)
     ring = lax.all_to_all(packed, AX, 0, 0, axis_index_groups=ring_groups(sections), tiled=True)
     by_half = ring.reshape(4, 2, PIECE, width)
     low = z % 2 == 1
@@ -245,53 +257,62 @@
     qk = qk_gain[0]
     block = jax.ShapeDtypeStruct((tokens, width), BF)
     text_block = jax.ShapeDtypeStruct((text_count, width), BF)
-    weights, text_key, text_value, stale_key, stale_value, state = pl.pallas_call(
+    weights, info, text_key, text_value, stale_key, stale_value, state = pl.pallas_call(
         functools.partial(prep_kernel, heads),
-        out_shape=[jax.ShapeDtypeStruct((depth, 3 * width), BF), text_block, text_block]
-        + [block] * 3,
-        in_specs=[HBM] * 9 + [VMEM] * 3,
-        out_specs=[VMEM] * 6,
+        out_shape=[
+            jax.ShapeDtypeStruct((depth, 3 * width), BF),
+            jax.ShapeDtypeStruct((8, 128), jnp.int32),
+            text_block,
+            text_block,
+            block,
+            block,
+            jax.ShapeDtypeStruct((2, tokens, width), BF),
+        ],
+        in_specs=[SMEM] * 3 + [VMEM] * 3 + [HBM] * 9,
+        out_specs=[HBM] + [VMEM] * 6,
         scratch_shapes=[
             pltpu.VMEM((32, TAIL, width), BF),
+            pltpu.VMEM((depth, 3 * width), BF),
             pltpu.VMEM((tokens, width), F32),
             pltpu.VMEM((tokens, width), F32),
-            pltpu.VMEM((tokens, width), F32),
-            pltpu.SemaphoreType.DMA((128,)),
+            pltpu.VMEM((2, tokens, width), F32),
+            pltpu.SemaphoreType.DMA((129,)),
         ],
         compiler_params=pltpu.CompilerParams(vmem_limit_bytes=16 * 2**20),
         name="prepare",
-    )(*pieces, text_states[0], norm_gain, qk)
+    )(stale_flags, patch_len, text_len, text_states[0], norm_gain, qk, *pieces)
 
     layer = pl.pallas_call(
         functools.partial(layer_kernel, heads),
         out_shape=[block, jax.ShapeDtypeStruct((2, tokens, width), BF)],
-        in_specs=[SMEM] * 3 + [VMEM] + [HBM] + [VMEM] * 6,
+        in_specs=[VMEM] * 9,
         out_specs=[VMEM] * 2,
-        scratch_shapes=[pltpu.VMEM((depth, 3 * width), BF), pltpu.SemaphoreType.DMA((2,))],
         compiler_params=pltpu.CompilerParams(vmem_limit_bytes=16 * 2**20),
         name="layer",
     )
+
+    weights = pltpu.with_memory_space_constraint(weights, pltpu.HBM)
+    rest = (weights, norm_gain, qk, text_key, text_value, stale_key, stale_value)
 
     def advance(step, entering):
         whole = lax.all_to_all(
             jnp.broadcast_to(entering[None], (4,) + entering.shape),
-            PLANE, 0, 0,
-            axis_index_groups=block_groups(step > 0 and step % 2 == 0),
-            tiled=True,
+            PLANE, 0, 0, axis_index_groups=block_groups(step % 2 == 0), tiled=True,
         )
-        return layer(
-            stale_flags, patch_len, text_len, whole, weights, norm_gain, qk, text_key, text_value,
-            stale_key, stale_value,
-        )
-
-    weights = pltpu.with_memory_space_constraint(weights, pltpu.HBM)
-    kept = (state, jnp.zeros((2, tokens, width), BF))
-    for step in range(sections):
-        entering = lax.ppermute(kept[0], AX, hop_pairs(step - 1)) if step else state
+        return tuple(layer(info, whole, *rest))
+
+    whole = lax.all_gather(state, "head", axis=0, tiled=True)
+    kept = (jnp.zeros((tokens, width), BF), jnp.zeros((2, tokens, width), BF))
+    kept = lax.cond(
+        section == 0, lambda whole, *kept: tuple(layer(info, whole, *rest)), lambda whole, *kept: kept,
+        whole, *kept,
+    )
+    for step in range(1, sections):
+        entering = lax.ppermute(kept[0], AX, hop_pairs(step - 1))
         kept = lax.cond(
             section == step,
-            lambda entering, *kept: tuple(advance(step, entering)),
-            lambda entering, *kept: tuple(kept),
+            lambda entering, *kept: advance(step, entering),
+            lambda entering, *kept: kept,
             entering, *kept,
         )
 

time: 265 us -> 257 us (0.970)
  waiting for transfers between devices: 201 us -> 183 us
  blocking collectives: 9.8 us -> 18.9 us
  local copies, waits for them, and re-layouts: 4.53 us -> 1.7 us
    ppermute x7, waiting for transfers between devices: 131 us -> 114 us  [shards(): entering = lax.ppermute(kept[0], AX, hop_pairs(step - 1))]
    all_gather x0 -> x1, blocking collectives: none -> 9.12 us  [shards(): whole = lax.all_gather(state, 'head', axis=0, tiled=True)]
    pallas_call x1 -> x2, Pallas kernels: 4.91 us -> 6.16 us  [the longest x1 4.08 us: advance(): return tuple(layer(info, whole, *rest))]
where the time goes in v4:
time: 257 us; the launch traced here: 256 us
  waiting for transfers between devices  183 us (71%)
  starting transfers between devices  36.4 us (14%)
  blocking collectives  18.9 us (7%)
  Pallas kernels  12.8 us (5%)
    ppermute x7, waiting for transfers between devices, shards(): entering = lax.ppermute(kept[0], AX, hop_pairs(step - 1))  114 us
    ppermute x7, waiting for transfers between devices, shards(): lax.ppermute(lanes[lane], AX, move_pairs(ahead, lane, sections))  34.8 us
    all_to_all x1, waiting for transfers between devices, shards(): lax.all_to_all(packed, AX, 0, 0, axis_index_groups=ring_groups(sections),...  18.2 us
    all_to_all x1, waiting for transfers between devices, shards(): result = lax.all_to_all(jnp.moveaxis(result, 1, 0), 'blk', 0, 0, tiled=True)  14 us
    ppermute x7, starting transfers between devices, shards(): lax.ppermute(lanes[lane], AX, move_pairs(ahead, lane, sections))  12.2 us
    all_to_all x1, blocking collectives, advance(): lax.all_to_all(jnp.broadcast_to(entering[None], (4,) + entering.shape), P...  9.79 us
    all_to_all x1, starting transfers between devices, shards(): result = lax.all_to_all(jnp.moveaxis(result, 1, 0), 'blk', 0, 0, tiled=True)  9.22 us
    all_gather x1, blocking collectives, shards(): whole = lax.all_gather(state, 'head', axis=0, tiled=True)  9.12 us
  transfers between devices with their start and end apart: 17, of which 8 were waited for; matrix products, arithmetic and copies ran while one was open for 0% of the time, Pallas kernels for 0%

profile of v4, /device:TPU:7, one launch (start us, length us, event | category | flops | bytes accessed | tf_op | source)
XLA Modules:
  0.0 255.6 jit_solution(7330181157307092978)
XLA Ops:
  0.6 2.1 pack.1
  2.7 6.8 %all-to-all-start.7 = ((bf16[8,176,384]{2,1,0:T(8,128)(2,1)}), bf16[8,176,384]{2,1,0:T(8,128)(2,1)S(1)}, u32[]{:S(2)}, u32[]{:S(2)}) async-start(bf16[8,176,384]{2,1,0:T(8,128)(2,1)} %pack.1), calls=%async_computation.7 | async-start | bytes 2162688 | tf_op jit(solution)/shard_map/all_to_all | solution.py:247
  9.5 18.2 %all-to-all-done.7 = bf16[8,176,384]{2,1,0:T(8,128)(2,1)S(1)} async-done(((bf16[8,176,384]{2,1,0:T(8,128)(2,1)}), bf16[8,176,384]{2,1,0:T(8,128)(2,1)S(1)}, u32[]{:S(2)}, u32[]{:S(2)}) %all-to-all-start.7) | async-done | bytes 1081376 | tf_op jit(solution)/shard_map/all_to_all | solution.py:247
  27.9 4.4 %collective-permute-start = (bf16[4,176,384]{2,1,0:T(8,128)(2,1)S(1)}, bf16[4,176,384]{2,1,0:T(8,128)(2,1)S(1)}, u32[]{:S(2)}, u32[]{:S(2)}) collective-permute-start(bf16[4,176,384]{2,1,0:T(8,128)(2,1)S(1)} %get-tuple-element.303.refs_14_), channel_id=1, source_target_pairs={{64,72},{65,73},{82,90},{83,91},{100,108},{101,109},{118,126},{119... | collective-permute-start | bytes 1622024 | tf_op jit(solution)/shard_map/ppermute | solution.py:254
  32.3 1.3 collective-permute-start.1
  33.6 1.3 collective-permute-start.2
  34.9 1.3 collective-permute-start.3
  36.2 1.3 collective-permute-start.4
  37.5 1.6 collective-permute-done.refs_6_
  39.1 1.3 collective-permute-start.5
  40.4 6.4 %collective-permute-done.1.refs_7_ = bf16[4,176,384]{2,1,0:T(8,128)(2,1)S(1)} collective-permute-done((bf16[4,176,384]{2,1,0:T(8,128)(2,1)S(1)}, bf16[4,176,384]{2,1,0:T(8,128)(2,1)S(1)}, u32[]{:S(2)}, u32[]{:S(2)}) %collective-permute-start.1) | collective-permute-done | bytes 540704 | tf_op jit(solution)/shard_map/ppermute | solution.py:254
  46.7 1.3 collective-permute-start.6
  48.7 19.1 %collective-permute-done.2.refs_8_ = bf16[4,176,384]{2,1,0:T(8,128)(2,1)S(1)} collective-permute-done((bf16[4,176,384]{2,1,0:T(8,128)(2,1)S(1)}, bf16[4,176,384]{2,1,0:T(8,128)(2,1)S(1)}, u32[]{:S(2)}, u32[]{:S(2)}) %collective-permute-start.2) | collective-permute-done | bytes 540704 | tf_op jit(solution)/shard_map/ppermute | solution.py:254
  67.8 7.7 %collective-permute-done.6.refs_12_ = bf16[4,176,384]{2,1,0:T(8,128)(2,1)} collective-permute-done((bf16[4,176,384]{2,1,0:T(8,128)(2,1)S(1)}, bf16[4,176,384]{2,1,0:T(8,128)(2,1)}, u32[]{:S(2)}, u32[]{:S(2)}) %collective-permute-start.6) | collective-permute-done | bytes 540704 | tf_op jit(solution)/shard_map/ppermute | solution.py:254
  75.6 6.6 %prepare.1 = (bf16[1536,1152]{1,0:T(8,128)(2,1)}, s32[8,128]{1,0:T(8,128)S(1)}, bf16[256,384]{1,0:T(8,128)(2,1)S(1)}, bf16[256,384]{1,0:T(8,128)(2,1)S(1)}, bf16...) custom-call(s32[4,8]{1,0:T(4,128)S(1)} %copy-done.1, s32[4]{0:T(128)S(1)} %copy-done.2, ...), custom_call_target="tpu_custom_call" | custom-call | tf_op jit(solution)/shard_map/prepare/pallas_call | solution.py:260
  82.2 9.1 %all_gather.3 = bf16[4,256,384]{2,1,0:T(8,128)(2,1)S(1)} all-gather(bf16[2,256,384]{2,1,0:T(8,128)(2,1)S(1)} %get-tuple-element.279), channel_id=1, replica_groups=mesh['section'=8,'blk'=32,'head'=2] {'head'}, dimensions={0}, use_global_device_ids=true | all-gather | bytes 1179648 | tf_op jit(solution)/shard_map/all_gather | solution.py:304
  92.1 0.7 collective-permute-start.8
  92.8 0.7 collective-permute-start.9
  93.6 0.7 collective-permute-start.10
  94.4 0.7 collective-permute-start.11
  95.2 0.7 collective-permute-start.12
  95.9 1.3 collective-permute-start.13
  97.2 113.6 %collective-permute-done.13 = bf16[256,384]{1,0:T(8,128)(2,1)S(1)} collective-permute-done((bf16[256,384]{1,0:T(8,128)(2,1)S(1)}, bf16[256,384]{1,0:T(8,128)(2,1)S(1)}, u32[]{:S(2)}, u32[]{:S(2)}) %collective-permute-start.13) | collective-permute-done | bytes 196640 | tf_op jit(solution)/shard_map/ppermute | solution.py:311
  210.8 14.0 %conditional.15 = ((bf16[256,384]{1,0:T(8,128)(2,1)S(1)}, bf16[2,256,384]{2,1,0:T(8,128)(2,1)S(1)})) conditional(s32[]{:T(128)} %convert_element_type.24, (bf16[256,384]{1,0:T(8,128)(2,1)S(1)}, bf16[2,256,384]{2,1,0:T(8,128)(2,1)S(1)}) %get-tuple-element.352, (bf16[256,384]{1,0:T(8,128)(2,1)S(1)}, s32[8,128]{1,0:T(8,128)S(1)}, ...), branch_computations={%region_14.15_spmd, %region_15.16_spmd} | conditional | bytes 2555912 | solution.py:312
  210.8 9.8 %all_to_all.44.x_ref = bf16[4,256,384]{2,1,0:T(8,128)(2,1)S(1)} all-to-all(bf16[4,256,384]{2,1,0:T(8,128)(2,1)S(1)} %broadcast_in_dim.36), channel_id=1, replica_groups={{0,8,1,9},{2,10,3,11},{4,12,5,13},{6,14,7,15},{16,24,17,25},{18,26,19,2..., dimensions={0} | all-to-all | bytes 1572864 | tf_op jit(solution)/shard_map/cond/branch_1_fun/all_to_all | solution.py:298
  220.6 4.1 %layer.15 = (bf16[256,384]{1,0:T(8,128)(2,1)S(1)}, bf16[2,256,384]{2,1,0:T(8,128)(2,1)S(1)}) custom-call(s32[8,128]{1,0:T(8,128)S(1)} %get-tuple-element.251.info_ref, bf16[4,256,384]{2,1,0:T(8,128)(2,1)S(1)} %all_to_all.44.x_ref, bf16[1536,1152]{1,0:T(8,128)(2,1)} %get-tuple-element.253.w_ref, f32[1,1536]{1,0:T(1,128)S(1)} %get-tuple-element.254.gain_ref, ...), custom_call_target="tpu_custom_call" | custom-call | tf_op jit(solution)/shard_map/cond/branch_1_fun/layer/pallas_call | solution.py:302
  224.7 0.9 maximum_bitcast_fusion
  225.6 9.2 %all-to-all-start.8 = ((bf16[32,3,8,384]{3,2,1,0:T(8,128)(2,1)}), bf16[32,3,8,384]{3,2,1,0:T(8,128)(2,1)S(1)}, u32[]{:S(2)}, u32[]{:S(2)}) async-start(bf16[32,3,8,384]{3,2,1,0:T(8,128)(2,1)} %maximum_bitcast_fusion), calls=%async_computation.8 | async-start | bytes 1179648 | tf_op jit(solution)/shard_map/all_to_all | solution.py:320
  234.8 14.0 %all-to-all-done.8 = bf16[32,3,8,384]{3,2,1,0:T(8,128)(2,1)S(1)} async-done(((bf16[32,3,8,384]{3,2,1,0:T(8,128)(2,1)}), bf16[32,3,8,384]{3,2,1,0:T(8,128)(2,1)S(1)}, u32[]{:S(2)}, u32[]{:S(2)}) %all-to-all-start.8) | async-done | bytes 589856 | tf_op jit(solution)/shard_map/all_to_all | solution.py:320
  248.9 2.9 %collective-permute-start.14 = (bf16[4,3,8,384]{3,2,1,0:T(8,128)(2,1)S(1)}, bf16[4,3,8,384]{3,2,1,0:T(8,128)(2,1)S(1)}, u32[]{:S(2)}, u32[]{:S(2)}) collective-permute-start(bf16[4,3,8,384]{3,2,1,0:T(8,128)(2,1)S(1)} %broadcast_select_fusion), channel_id=1, source_target_pairs={{64,65},{65,64},{66,67},{67,66},{68,69},{69,68},{70,71},{71,70},{7... | collective-permute-start | bytes 221192 | tf_op jit(solution)/shard_map/ppermute | solution.py:330
  251.8 2.2 collective-permute-done.14
  254.2 0.7 broadcast_in_dim.38
  (50 shorter events, 2.2 us)
Async XLA Ops:
  2.7 25.0 %all-to-all-start.7 = ((bf16[8,176,384]{2,1,0:T(8,128)(2,1)}), bf16[8,176,384]{2,1,0:T(8,128)(2,1)S(1)}, u32[]{:S(2)}, u32[]{:S(2)}) async-start(bf16[8,176,384]{2,1,0:T(8,128)(2,1)} %pack.1), calls=%async_computation.7 | async-start | bytes 2162688 | tf_op jit(solution)/shard_map/all_to_all | solution.py:247
  27.7 47.9 %copy-start = (bf16[1,256,1536]{2,1,0:T(8,128)(2,1)S(1)}, bf16[1,256,1536]{2,1,0:T(8,128)(2,1)}, u32[]{:S(2)}) copy-start(bf16[1,256,1536]{2,1,0:T(8,128)(2,1)} %param.29) | copy-start | bytes 2359300
  27.7 47.9 %copy-start.1 = (s32[4,8]{1,0:T(4,128)S(1)}, s32[4,8]{1,0:T(4,128)}, u32[]{:S(2)}) copy-start(s32[4,8]{1,0:T(4,128)} %refs_0_.1) | copy-start | bytes 388
  27.7 47.9 %copy-start.2 = (s32[4]{0:T(128)S(1)}, s32[4]{0:T(128)}, u32[]{:S(2)}) copy-start(s32[4]{0:T(128)} %refs_1_.1) | copy-start | bytes 52
  27.7 47.9 %copy-start.8 = (f32[1,1536]{1,0:T(1,128)S(1)}, f32[1,1536]{1,0:T(1,128)}, u32[]{:S(2)}) copy-start(f32[1,1536]{1,0:T(1,128)} %refs_4_.1) | copy-start | bytes 18436
  27.7 47.9 %copy-start.9 = (f32[1,2,128]{2,1,0:T(2,128)S(1)}, f32[1,2,128]{2,1,0:T(2,128)}, u32[]{:S(2)}) copy-start(f32[1,2,128]{2,1,0:T(2,128)} %param.28) | copy-start | bytes 3076
  27.9 47.7 %copy-start.3 = (bf16[4,176,384]{2,1,0:T(8,128)(2,1)}, bf16[4,176,384]{2,1,0:T(8,128)(2,1)S(1)}, u32[]{:S(2)}) copy-start(bf16[4,176,384]{2,1,0:T(8,128)(2,1)S(1)} %get-tuple-element.302.refs_13_) | copy-start | bytes 1622020
  27.9 47.7 %copy-start.4 = (bf16[4,176,384]{2,1,0:T(8,128)(2,1)}, bf16[4,176,384]{2,1,0:T(8,128)(2,1)S(1)}, u32[]{:S(2)}) copy-start(bf16[4,176,384]{2,1,0:T(8,128)(2,1)S(1)} %get-tuple-element.303.refs_14_) | copy-start | bytes 1622020
  27.9 11.2 %collective-permute-start = (bf16[4,176,384]{2,1,0:T(8,128)(2,1)S(1)}, bf16[4,176,384]{2,1,0:T(8,128)(2,1)S(1)}, u32[]{:S(2)}, u32[]{:S(2)}) collective-permute-start(bf16[4,176,384]{2,1,0:T(8,128)(2,1)S(1)} %get-tuple-element.303.refs_14_), channel_id=1, source_target_pairs={{64,72},{65,73},{82,90},{83,91},{100,108},{101,109},{118,126},{119... | collective-permute-start | bytes 1622024 | tf_op jit(solution)/shard_map/ppermute | solution.py:254
  32.3 14.4 %collective-permute-start.1 = (bf16[4,176,384]{2,1,0:T(8,128)(2,1)S(1)}, bf16[4,176,384]{2,1,0:T(8,128)(2,1)S(1)}, u32[]{:S(2)}, u32[]{:S(2)}) collective-permute-start(bf16[4,176,384]{2,1,0:T(8,128)(2,1)S(1)} %get-tuple-element.302.refs_13_), channel_id=1, source_target_pairs={{4,0},{5,1},{12,8},{13,9},{22,18},{23,19},{30,26},{31,27},{32,36},... | collective-permute-start | bytes 1622024 | tf_op jit(solution)/shard_map/ppermute | solution.py:254
  33.6 34.2 %collective-permute-start.2 = (bf16[4,176,384]{2,1,0:T(8,128)(2,1)S(1)}, bf16[4,176,384]{2,1,0:T(8,128)(2,1)S(1)}, u32[]{:S(2)}, u32[]{:S(2)}) collective-permute-start(bf16[4,176,384]{2,1,0:T(8,128)(2,1)S(1)} %get-tuple-element.302.refs_13_), channel_id=1, source_target_pairs={{2,0},{3,1},{10,8},{11,9},{20,18},{21,19},{28,26},{29,27},{38,36},... | collective-permute-start | bytes 1622024 | tf_op jit(solution)/shard_map/ppermute | solution.py:254
  34.9 32.9 %collective-permute-start.3 = (bf16[4,176,384]{2,1,0:T(8,128)(2,1)S(1)}, bf16[4,176,384]{2,1,0:T(8,128)(2,1)}, u32[]{:S(2)}, u32[]{:S(2)}) collective-permute-start(bf16[4,176,384]{2,1,0:T(8,128)(2,1)S(1)} %get-tuple-element.302.refs_13_), channel_id=1, source_target_pairs={{6,0},{7,1},{14,8},{15,9},{16,18},{17,19},{24,26},{25,27},{34,36},... | collective-permute-start | bytes 1622024 | tf_op jit(solution)/shard_map/ppermute | solution.py:254
  36.2 31.6 %collective-permute-start.4 = (bf16[4,176,384]{2,1,0:T(8,128)(2,1)S(1)}, bf16[4,176,384]{2,1,0:T(8,128)(2,1)}, u32[]{:S(2)}, u32[]{:S(2)}) collective-permute-start(bf16[4,176,384]{2,1,0:T(8,128)(2,1)S(1)} %get-tuple-element.303.refs_14_), channel_id=1, source_target_pairs={{4,0},{5,1},{12,8},{13,9},{22,18},{23,19},{30,26},{31,27},{32,36},... | collective-permute-start | bytes 1622024 | tf_op jit(solution)/shard_map/ppermute | solution.py:254
  39.1 36.5 %copy-start.5 = (bf16[4,176,384]{2,1,0:T(8,128)(2,1)}, bf16[4,176,384]{2,1,0:T(8,128)(2,1)S(1)}, u32[]{:S(2)}) copy-start(bf16[4,176,384]{2,1,0:T(8,128)(2,1)S(1)} %collective-permute-done.refs_6_) | copy-start | bytes 1622020
  39.1 28.8 %collective-permute-start.5 = (bf16[4,176,384]{2,1,0:T(8,128)(2,1)S(1)}, bf16[4,176,384]{2,1,0:T(8,128)(2,1)}, u32[]{:S(2)}, u32[]{:S(2)}) collective-permute-start(bf16[4,176,384]{2,1,0:T(8,128)(2,1)S(1)} %get-tuple-element.303.refs_14_), channel_id=1, source_target_pairs={{2,0},{3,1},{10,8},{11,9},{20,18},{21,19},{28,26},{29,27},{38,36},... | collective-permute-start | bytes 1622024 | tf_op jit(solution)/shard_map/ppermute | solution.py:254
  46.7 28.8 %copy-start.6 = (bf16[4,176,384]{2,1,0:T(8,128)(2,1)}, bf16[4,176,384]{2,1,0:T(8,128)(2,1)S(1)}, u32[]{:S(2)}) copy-start(bf16[4,176,384]{2,1,0:T(8,128)(2,1)S(1)} %collective-permute-done.1.refs_7_) | copy-start | bytes 1622020
  46.7 28.8 %collective-permute-start.6 = (bf16[4,176,384]{2,1,0:T(8,128)(2,1)S(1)}, bf16[4,176,384]{2,1,0:T(8,128)(2,1)}, u32[]{:S(2)}, u32[]{:S(2)}) collective-permute-start(bf16[4,176,384]{2,1,0:T(8,128)(2,1)S(1)} %get-tuple-element.303.refs_14_), channel_id=1, source_target_pairs={{6,0},{7,1},{14,8},{15,9},{16,18},{17,19},{24,26},{25,27},{34,36},... | collective-permute-start | bytes 1622024 | tf_op jit(solution)/shard_map/ppermute | solution.py:254
  67.8 7.7 %copy-start.7 = (bf16[4,176,384]{2,1,0:T(8,128)(2,1)}, bf16[4,176,384]{2,1,0:T(8,128)(2,1)S(1)}, u32[]{:S(2)}) copy-start(bf16[4,176,384]{2,1,0:T(8,128)(2,1)S(1)} %collective-permute-done.2.refs_8_) | copy-start | bytes 1622020
  91.4 0.7 collective-permute-start.7
  92.1 0.7 collective-permute-start.8
  92.8 0.7 collective-permute-start.9
  93.6 0.7 collective-permute-start.10
  94.4 0.7 collective-permute-start.11
  95.2 0.7 collective-permute-start.12
  95.9 114.9 %collective-permute-start.13 = (bf16[256,384]{1,0:T(8,128)(2,1)S(1)}, bf16[256,384]{1,0:T(8,128)(2,1)S(1)}, u32[]{:S(2)}, u32[]{:S(2)}) collective-permute-start(bf16[256,384]{1,0:T(8,128)(2,1)S(1)} %get-tuple-element.291), channel_id=1, source_target_pairs={{384,448},{385,449},{392,456},{393,457},{402,466},{403,467},{410,4... | collective-permute-start | bytes 589832 | tf_op jit(solution)/shard_map/ppermute | solution.py:311
  225.6 23.2 %all-to-all-start.8 = ((bf16[32,3,8,384]{3,2,1,0:T(8,128)(2,1)}), bf16[32,3,8,384]{3,2,1,0:T(8,128)(2,1)S(1)}, u32[]{:S(2)}, u32[]{:S(2)}) async-start(bf16[32,3,8,384]{3,2,1,0:T(8,128)(2,1)} %maximum_bitcast_fusion), calls=%async_computation.8 | async-start | bytes 1179648 | tf_op jit(solution)/shard_map/all_to_all | solution.py:320
  248.9 5.1 %collective-permute-start.14 = (bf16[4,3,8,384]{3,2,1,0:T(8,128)(2,1)S(1)}, bf16[4,3,8,384]{3,2,1,0:T(8,128)(2,1)S(1)}, u32[]{:S(2)}, u32[]{:S(2)}) collective-permute-start(bf16[4,3,8,384]{3,2,1,0:T(8,128)(2,1)S(1)} %broadcast_select_fusion), channel_id=1, source_target_pairs={{64,65},{65,64},{66,67},{67,66},{68,69},{69,68},{70,71},{71,70},{7... | collective-permute-start | bytes 221192 | tf_op jit(solution)/shard_map/ppermute | solution.py:330

commit v5 on v4

--- a/solution.py
+++ b/solution.py
@@ -27,7 +27,7 @@
     groups = []
     for s in range(sections):
         for i in range(8):
-            groups.append([at(s, j, i) if s % 2 == 0 else at(s, i, j) for j in range(8)])
+            groups.append([at(s, j, i) if s % 2 == 0 else at(s, i, j) for j in range(7, -1, -1)])
     return groups
 
 
@@ -50,6 +50,15 @@
 def block_groups(odd):
     order = [(h, q) if odd else (q, h) for h in range(2) for q in range(2)]
     return [[at(0, 2 * i + z, 2 * j + y) for z, y in order] for i in range(4) for j in range(4)]
+
+
+def pair_pairs():
+    return [
+        (at(0, 2 * m + i, 2 * m + j), at(0, 2 * m + i, 2 * m + 1 - j))
+        for m in range(4)
+        for i in range(2)
+        for j in range(2)
+    ]
 
 
 def hop_pairs(step):
@@ -82,7 +91,7 @@
         states = [hidden_ref[m, :, cols].astype(F32) for cols in sides]
         states = jnp.concatenate(states, axis=0).astype(BF)
         for side, cols in enumerate(sides):
-            place = 2 * m + side
+            place = 2 * micros - 1 - (2 * m + side)
             for part in range(3):
                 out_ref[place, part * ROWS : (part + 1) * ROWS, :] = w_ref[part, :, cols]
             old = [stale_ref[part, m, :, cols].astype(F32) for part in range(2)]
@@ -91,35 +100,9 @@
             out_ref[place, 3 * ROWS + 16 : PIECE, :] = states
 
 
-def prep_kernel(heads, *refs):
-    flag_ref, patch_ref, text_len_ref, text_ref, gain_ref, qk_ref = refs[:6]
-    pieces, (w_ref, info_ref), refs = refs[6:15], refs[15:17], refs[17:]
-    tk_ref, tv_ref, sk_ref, sv_ref, state_ref = refs[:5]
-    tails, held, stale_key, stale_value, state, sems = refs[5:]
-    width = heads * 128
-    section, odd, micro, half, _ = position()
-    line = lax.broadcasted_iota(jnp.int32, info_ref.shape, 0)
-    limits = jnp.where(line == 1, patch_ref[micro], text_len_ref[0])
-    info_ref[...] = jnp.where(line == 0, flag_ref[micro, section], limits)
-
-    def block_copies(source, block, first):
-        row = pl.multiple_of(block * ROWS, 16)
-        made = [
-            pltpu.make_async_copy(
-                source.at[pl.ds(part * ROWS, ROWS), :],
-                held.at[pl.ds(row, ROWS), pl.ds(part * width, width)],
-                sems.at[first + part],
-            )
-            for part in range(3)
-        ]
-        made.append(
-            pltpu.make_async_copy(
-                source.at[pl.ds(3 * ROWS, TAIL), :], tails.at[block], sems.at[first + 3]
-            )
-        )
-        return made
-
-    even_copies, odd_copies = [], []
+def with_blocks(pieces, act):
+    _, odd, micro, half, _ = position()
+    evens, odds = [], []
     for ahead in range(4):
         far = lax.rem(micro + ahead, 4)
         for lane in range(2):
@@ -128,37 +111,32 @@
             odd_piece = pieces[MOVES.index((ahead, lane)) if ahead or lane else local]
             z = 2 * far + (half if lane == 0 else 1 - half)
             for j in range(4):
-                first = len(even_copies)
-                even_copies += block_copies(even_piece.at[j], (4 * lane + j) * 4 + far, first)
-                odd_copies += block_copies(odd_piece.at[j], z * 4 + j, first)
-
-    @pl.when(odd == 0)
-    def _():
-        for copy in even_copies:
-            copy.start()
-
-    @pl.when(odd == 1)
-    def _():
-        for copy in odd_copies:
-            copy.start()
-
-    text = text_ref[...].astype(F32)
-    mean = jnp.mean(text * text, axis=-1, keepdims=True)
-    normed = (text * lax.rsqrt(mean + 1e-06) * gain_ref[...]).astype(BF)
-    key_gain = qk_ref[1:2, :]
-
-    @pl.when(odd == 0)
-    def _():
-        for copy in even_copies:
-            copy.wait()
-
-    @pl.when(odd == 1)
-    def _():
-        for copy in odd_copies:
-            copy.wait()
-
-    store = pltpu.make_async_copy(held, w_ref, sems.at[128])
-    store.start()
+                evens.append((even_piece.at[j], (7 - 4 * lane - j) * 4 + far))
+                odds.append((odd_piece.at[j], z * 4 + 3 - j))
+    for parity, blocks in enumerate((evens, odds)):
+
+        @pl.when(odd == parity)
+        def _(blocks=blocks):
+            for i, (source, block) in enumerate(blocks):
+                act(i, source, block)
+
+
+def tail_kernel(heads, *refs):
+    flag_ref, patch_ref, text_len_ref, qk_ref = refs[:4]
+    pieces, (info_ref, sk_ref, sv_ref, state_ref) = refs[4:13], refs[13:17]
+    tails, stale_key, stale_value, state, sems = refs[17:]
+    section, _, micro, _, _ = position()
+
+    def tail_copy(i, source, block):
+        return pltpu.make_async_copy(
+            source.at[pl.ds(3 * ROWS, TAIL), :], tails.at[block], sems.at[i]
+        )
+
+    with_blocks(pieces, lambda *block: tail_copy(*block).start())
+    line = lax.broadcasted_iota(jnp.int32, info_ref.shape, 0)
+    limits = jnp.where(line == 1, patch_ref[micro], text_len_ref[0])
+    info_ref[...] = jnp.where(line == 0, flag_ref[micro, section], limits)
+    with_blocks(pieces, lambda *block: tail_copy(*block).wait())
     for b in range(32):
         tail = tails[b].astype(F32)
         stale_key[8 * b : 8 * b + 8, :] = tail[0:8]
@@ -167,11 +145,38 @@
         state[1, 8 * b : 8 * b + 8, :] = tail[24:32]
     sv_ref[...] = stale_value[...].astype(BF)
     state_ref[...] = state[...].astype(BF)
+    for h in range(heads):
+        cols = slice(h * 128, (h + 1) * 128)
+        sk_ref[:, cols] = head_norm(stale_key[:, cols], qk_ref[1:2, :]).astype(BF)
+
+
+def prep_kernel(heads, *refs):
+    text_ref, gain_ref, qk_ref = refs[:3]
+    pieces, (w_ref, tk_ref, tv_ref), (held, sems) = refs[3:12], refs[12:15], refs[15:]
+    width = heads * 128
+
+    def weight_copies(i, source, block):
+        row = pl.multiple_of(block * ROWS, 16)
+        return [
+            pltpu.make_async_copy(
+                source.at[pl.ds(part * ROWS, ROWS), :],
+                held.at[pl.ds(row, ROWS), pl.ds(part * width, width)],
+                sems.at[3 * i + part],
+            )
+            for part in range(3)
+        ]
+
+    with_blocks(pieces, lambda *block: [copy.start() for copy in weight_copies(*block)])
+    text = text_ref[...].astype(F32)
+    mean = jnp.mean(text * text, axis=-1, keepdims=True)
+    normed = (text * lax.rsqrt(mean + 1e-06) * gain_ref[...]).astype(BF)
+    with_blocks(pieces, lambda *block: [copy.wait() for copy in weight_copies(*block)])
+    store = pltpu.make_async_copy(held, w_ref, sems.at[96])
+    store.start()
     kv = jnp.dot(normed, held[:, width:], preferred_element_type=F32).astype(BF)
     for h in range(heads):
         cols = slice(h * 128, (h + 1) * 128)
-        sk_ref[:, cols] = head_norm(stale_key[:, cols], key_gain).astype(BF)
-        tk_ref[:, cols] = head_norm(kv[:, cols].astype(F32), key_gain).astype(BF)
+        tk_ref[:, cols] = head_norm(kv[:, cols].astype(F32), qk_ref[1:2, :]).astype(BF)
     tv_ref[...] = kv[:, width:]
     store.wait()
 
@@ -248,8 +253,8 @@
     by_half = ring.reshape(4, 2, PIECE, width)
     low = z % 2 == 1
     lanes = (
-        jnp.where(odd, jnp.where(low, by_half[:, 1], by_half[:, 0]), ring[:4]),
-        jnp.where(odd, jnp.where(low, by_half[:, 0], by_half[:, 1]), ring[4:]),
+        jnp.where(odd, jnp.where(low, by_half[:, 0], by_half[:, 1]), ring[:4]),
+        jnp.where(odd, jnp.where(low, by_half[:, 1], by_half[:, 0]), ring[4:]),
     )
     pieces = [lax.ppermute(lanes[lane], AX, move_pairs(ahead, lane, sections)) for ahead, lane in MOVES]
     pieces = [pltpu.with_memory_space_constraint(piece, pltpu.HBM) for piece in (*pieces, *lanes)]
@@ -257,30 +262,44 @@
     qk = qk_gain[0]
     block = jax.ShapeDtypeStruct((tokens, width), BF)
     text_block = jax.ShapeDtypeStruct((text_count, width), BF)
-    weights, info, text_key, text_value, stale_key, stale_value, state = pl.pallas_call(
-        functools.partial(prep_kernel, heads),
+    info, stale_key, stale_value, state = pl.pallas_call(
+        functools.partial(tail_kernel, heads),
         out_shape=[
-            jax.ShapeDtypeStruct((depth, 3 * width), BF),
             jax.ShapeDtypeStruct((8, 128), jnp.int32),
-            text_block,
-            text_block,
             block,
             block,
             jax.ShapeDtypeStruct((2, tokens, width), BF),
         ],
-        in_specs=[SMEM] * 3 + [VMEM] * 3 + [HBM] * 9,
-        out_specs=[HBM] + [VMEM] * 6,
+        in_specs=[SMEM] * 3 + [VMEM] + [HBM] * 9,
+        out_specs=[VMEM] * 4,
         scratch_shapes=[
             pltpu.VMEM((32, TAIL, width), BF),
-            pltpu.VMEM((depth, 3 * width), BF),
             pltpu.VMEM((tokens, width), F32),
             pltpu.VMEM((tokens, width), F32),
             pltpu.VMEM((2, tokens, width), F32),
-            pltpu.SemaphoreType.DMA((129,)),
+            pltpu.SemaphoreType.DMA((32,)),
         ],
         compiler_params=pltpu.CompilerParams(vmem_limit_bytes=16 * 2**20),
+        name="tails",
+    )(stale_flags, patch_len, text_len, qk, *pieces)
+    other = lax.ppermute(state, AX, pair_pairs())
+    weights, text_key, text_value = pl.pallas_call(
+        functools.partial(prep_kernel, heads),
+        out_shape=[jax.ShapeDtypeStruct((depth, 3 * width), BF), text_block, text_block],
+        in_specs=[VMEM] * 3 + [HBM] * 9,
+        out_specs=[HBM] + [VMEM] * 2,
+        scratch_shapes=[pltpu.VMEM((depth, 3 * width), BF), pltpu.SemaphoreType.DMA((97,))],
+        compiler_params=pltpu.CompilerParams(vmem_limit_bytes=16 * 2**20),
+        cost_estimate=pl.CostEstimate(
+            flops=4 * text_count * depth * width,
+            bytes_accessed=12 * depth * width,
+            transcendentals=0,
+        ),
         name="prepare",
-    )(stale_flags, patch_len, text_len, text_states[0], norm_gain, qk, *pieces)
+    )(text_states[0], norm_gain, qk, *pieces)
+    whole = jnp.where(
+        head == 0, jnp.concatenate([state, other]), jnp.concatenate([other, state])
+    )
 
     layer = pl.pallas_call(
         functools.partial(layer_kernel, heads),
@@ -301,7 +320,6 @@
         )
         return tuple(layer(info, whole, *rest))
 
-    whole = lax.all_gather(state, "head", axis=0, tiled=True)
     kept = (jnp.zeros((tokens, width), BF), jnp.zeros((2, tokens, width), BF))
     kept = lax.cond(
         section == 0, lambda whole, *kept: tuple(layer(info, whole, *rest)), lambda whole, *kept: kept,

time: 257 us -> 251 us (0.977)
  blocking collectives: 18.9 us -> 32.8 us
  waiting for transfers between devices: 183 us -> 170 us
  starting transfers between devices: 36.4 us -> 27.8 us
    all_to_all x0 -> x1, blocking collectives: none -> 23 us  [shards(): result = lax.all_to_all(jnp.moveaxis(result, 1, 0), 'blk', 0, 0, tiled=True)]
    all_to_all x1 -> x0, waiting for transfers between devices: 14 us -> none  [shards(): result = lax.all_to_all(jnp.moveaxis(result, 1, 0), 'blk', 0, 0, tiled=True)]
    all_to_all x1 -> x0, starting transfers between devices: 9.22 us -> none  [shards(): result = lax.all_to_all(jnp.moveaxis(result, 1, 0), 'blk', 0, 0, tiled=True)]
    all_gather x1 -> x0, blocking collectives: 9.12 us -> none  [shards(): whole = lax.all_gather(state, 'head', axis=0, tiled=True)]
    ppermute x7, waiting for transfers between devices: 114 us -> 122 us  [shards(): entering = lax.ppermute(kept[0], AX, hop_pairs(step - 1))]
    all_to_all x1, waiting for transfers between devices: 18.2 us -> 12 us  [shards(): lax.all_to_all(packed, AX, 0, 0, axis_index_groups=ring_groups(sections),...]
  transfers between devices with their start and end apart: 17 -> 17, of which waited for: 8 -> 7; matrix products, arithmetic and copies ran while one was open for 0% -> 0% of each run, Pallas kernels for 0% -> 2%
where the time goes in v5:
time: 251 us; the launch traced here: 250 us
  waiting for transfers between devices  170 us (68%)
  blocking collectives  32.8 us (13%)
  starting transfers between devices  27.8 us (11%)
  Pallas kernels  13.8 us (5%)
    ppermute x7, waiting for transfers between devices, shards(): entering = lax.ppermute(kept[0], AX, hop_pairs(step - 1))  122 us
    ppermute x7, waiting for transfers between devices, shards(): lax.ppermute(lanes[lane], AX, move_pairs(ahead, lane, sections))  34.6 us
    all_to_all x1, blocking collectives, shards(): result = lax.all_to_all(jnp.moveaxis(result, 1, 0), 'blk', 0, 0, tiled=True)  23 us
    all_to_all x1, waiting for transfers between devices, shards(): lax.all_to_all(packed, AX, 0, 0, axis_index_groups=ring_groups(sections),...  12 us
    ppermute x7, starting transfers between devices, shards(): lax.ppermute(lanes[lane], AX, move_pairs(ahead, lane, sections))  11.7 us
    all_to_all x1, blocking collectives, advance(): lax.all_to_all(jnp.broadcast_to(entering[None], (4,) + entering.shape), P...  9.79 us
    all_to_all x1, starting transfers between devices, shards(): lax.all_to_all(packed, AX, 0, 0, axis_index_groups=ring_groups(sections),...  7.1 us
    pallas_call x1, Pallas kernels, shards(): pl.pallas_call(functools.partial(prep_kernel, heads), out_shape=[jax.Shap...  5.41 us
  transfers between devices with their start and end apart: 17, of which 7 were waited for; matrix products, arithmetic and copies ran while one was open for 0% of the time, Pallas kernels for 2%

profile of v5, /device:TPU:7, one launch (start us, length us, event | category | flops | bytes accessed | tf_op | source)
XLA Modules:
  0.0 249.7 jit_solution(6520016094584838287)
XLA Ops:
  0.6 2.1 pack.1
  2.7 7.1 %all-to-all-start.7 = ((bf16[8,176,384]{2,1,0:T(8,128)(2,1)}), bf16[8,176,384]{2,1,0:T(8,128)(2,1)S(1)}, u32[]{:S(2)}, u32[]{:S(2)}) async-start(bf16[8,176,384]{2,1,0:T(8,128)(2,1)} %pack.1), calls=%async_computation.7 | async-start | bytes 2162688 | tf_op jit(solution)/shard_map/all_to_all | solution.py:252
  9.8 12.0 %all-to-all-done.7 = bf16[8,176,384]{2,1,0:T(8,128)(2,1)S(1)} async-done(((bf16[8,176,384]{2,1,0:T(8,128)(2,1)}), bf16[8,176,384]{2,1,0:T(8,128)(2,1)S(1)}, u32[]{:S(2)}, u32[]{:S(2)}) %all-to-all-start.7) | async-done | bytes 1081376 | tf_op jit(solution)/shard_map/all_to_all | solution.py:252
  22.0 4.0 %collective-permute-start = (bf16[4,176,384]{2,1,0:T(8,128)(2,1)S(1)}, bf16[4,176,384]{2,1,0:T(8,128)(2,1)S(1)}, u32[]{:S(2)}, u32[]{:S(2)}) collective-permute-start(bf16[4,176,384]{2,1,0:T(8,128)(2,1)S(1)} %get-tuple-element.303.refs_12_.refs_11_), channel_id=1, source_target_pairs={{64,72},{65,73},{82,90},{83,91},{100,108},{101,109},{118,126},{119... | collective-permute-start | bytes 1622024 | tf_op jit(solution)/shard_map/ppermute | solution.py:259
  26.0 1.3 collective-permute-start.1
  27.3 1.3 collective-permute-start.2
  28.6 1.3 collective-permute-start.3
  29.9 1.3 collective-permute-start.4
  31.2 4.8 %collective-permute-done.refs_4_.refs_3_ = bf16[4,176,384]{2,1,0:T(8,128)(2,1)S(1)} collective-permute-done((bf16[4,176,384]{2,1,0:T(8,128)(2,1)S(1)}, bf16[4,176,384]{2,1,0:T(8,128)(2,1)S(1)}, u32[]{:S(2)}, u32[]{:S(2)}) %collective-permute-start) | collective-permute-done | bytes 540704 | tf_op jit(solution)/shard_map/ppermute | solution.py:259
  36.0 1.3 collective-permute-start.5
  37.3 3.1 %collective-permute-done.1.refs_5_.refs_4_ = bf16[4,176,384]{2,1,0:T(8,128)(2,1)S(1)} collective-permute-done((bf16[4,176,384]{2,1,0:T(8,128)(2,1)S(1)}, bf16[4,176,384]{2,1,0:T(8,128)(2,1)S(1)}, u32[]{:S(2)}, u32[]{:S(2)}) %collective-permute-start.1) | collective-permute-done | bytes 540704 | tf_op jit(solution)/shard_map/ppermute | solution.py:259
  40.5 1.3 collective-permute-start.6
  42.4 19.1 %collective-permute-done.2.refs_6_.refs_5_ = bf16[4,176,384]{2,1,0:T(8,128)(2,1)S(1)} collective-permute-done((bf16[4,176,384]{2,1,0:T(8,128)(2,1)S(1)}, bf16[4,176,384]{2,1,0:T(8,128)(2,1)S(1)}, u32[]{:S(2)}, u32[]{:S(2)}) %collective-permute-start.2) | collective-permute-done | bytes 540704 | tf_op jit(solution)/shard_map/ppermute | solution.py:259
  61.6 7.6 %collective-permute-done.6.refs_10_.refs_9_ = bf16[4,176,384]{2,1,0:T(8,128)(2,1)S(1)} collective-permute-done((bf16[4,176,384]{2,1,0:T(8,128)(2,1)S(1)}, bf16[4,176,384]{2,1,0:T(8,128)(2,1)S(1)}, u32[]{:S(2)}, u32[]{:S(2)}) %collective-permute-start.6) | collective-permute-done | bytes 540704 | tf_op jit(solution)/shard_map/ppermute | solution.py:259
  69.2 0.8 copy-done.11
  70.0 2.2 tails.1
  72.2 0.7 collective-permute-start.7
  72.9 5.4 %prepare.1 = (bf16[1536,1152]{1,0:T(8,128)(2,1)}, bf16[256,384]{1,0:T(8,128)(2,1)S(1)}, bf16[256,384]{1,0:T(8,128)(2,1)S(1)}) custom-call(bf16[256,1536]{1,0:T(8,128)(2,1)S(1)} %bitcast.38, f32[1,1536]{1,0:T(1,128)S(1)} %copy-done.12, f32[2,128]{1,0:T(2,128)S(1)} %bitcast.43, bf16[4,176,384]{2,1,0:T(8,128)(2,1)} %copy-done.5, ...), custom_call_target="tpu_custom_call" | custom-call | flops 603979776 | bytes 7077888 | tf_op jit(solution)/shard_map/prepare/pallas_call | solution.py:286
  78.6 0.7 collective-permute-start.8
  79.3 0.7 collective-permute-start.9
  80.0 0.7 collective-permute-start.10
  80.9 0.7 collective-permute-start.11
  81.6 0.7 collective-permute-start.12
  83.1 1.3 collective-permute-start.14
  84.4 121.7 %collective-permute-done.14 = bf16[256,384]{1,0:T(8,128)(2,1)S(1)} collective-permute-done((bf16[256,384]{1,0:T(8,128)(2,1)S(1)}, bf16[256,384]{1,0:T(8,128)(2,1)S(1)}, u32[]{:S(2)}, u32[]{:S(2)}) %collective-permute-start.14) | collective-permute-done | bytes 196640 | tf_op jit(solution)/shard_map/ppermute | solution.py:329
  206.0 13.9 %conditional.15 = ((bf16[256,384]{1,0:T(8,128)(2,1)S(1)}, bf16[2,256,384]{2,1,0:T(8,128)(2,1)S(1)})) conditional(s32[]{:T(128)} %convert_element_type.24, (bf16[256,384]{1,0:T(8,128)(2,1)S(1)}, bf16[2,256,384]{2,1,0:T(8,128)(2,1)S(1)}) %get-tuple-element.352, (bf16[256,384]{1,0:T(8,128)(2,1)S(1)}, s32[8,128]{1,0:T(8,128)S(1)}, ...), branch_computations={%region_14.15_spmd, %region_15.16_spmd} | conditional | bytes 2555912 | solution.py:330
  206.1 9.8 %all_to_all.44.x_ref = bf16[4,256,384]{2,1,0:T(8,128)(2,1)S(1)} all-to-all(bf16[4,256,384]{2,1,0:T(8,128)(2,1)S(1)} %broadcast_in_dim.36), channel_id=1, replica_groups={{0,8,1,9},{2,10,3,11},{4,12,5,13},{6,14,7,15},{16,24,17,25},{18,26,19,2..., dimensions={0} | all-to-all | bytes 1572864 | tf_op jit(solution)/shard_map/cond/branch_1_fun/all_to_all | solution.py:317
  215.9 4.0 %layer.15 = (bf16[256,384]{1,0:T(8,128)(2,1)S(1)}, bf16[2,256,384]{2,1,0:T(8,128)(2,1)S(1)}) custom-call(s32[8,128]{1,0:T(8,128)S(1)} %get-tuple-element.251.info_ref, bf16[4,256,384]{2,1,0:T(8,128)(2,1)S(1)} %all_to_all.44.x_ref, bf16[1536,1152]{1,0:T(8,128)(2,1)} %get-tuple-element.253.w_ref, f32[1,1536]{1,0:T(1,128)S(1)} %get-tuple-element.254.gain_ref, ...), custom_call_target="tpu_custom_call" | custom-call | tf_op jit(solution)/shard_map/cond/branch_1_fun/layer/pallas_call | solution.py:321
  220.0 23.0 %all_to_all.45 = bf16[32,3,8,384]{3,2,1,0:T(8,128)(2,1)S(1)} all-to-all(bf16[32,3,8,384]{3,2,1,0:T(8,128)(2,1)S(1)} %maximum_bitcast_fusion), channel_id=1, replica_groups=mesh['section'=8,'blk'=32,'head'=2] {'blk'}, dimensions={0} | all-to-all | bytes 1179648 | tf_op jit(solution)/shard_map/all_to_all | solution.py:338
  243.0 2.9 %collective-permute-start.15 = (bf16[4,3,8,384]{3,2,1,0:T(8,128)(2,1)S(1)}, bf16[4,3,8,384]{3,2,1,0:T(8,128)(2,1)S(1)}, u32[]{:S(2)}, u32[]{:S(2)}) collective-permute-start(bf16[4,3,8,384]{3,2,1,0:T(8,128)(2,1)S(1)} %broadcast_select_fusion), channel_id=1, source_target_pairs={{64,65},{65,64},{66,67},{67,66},{68,69},{69,68},{70,71},{71,70},{7... | collective-permute-start | bytes 221192 | tf_op jit(solution)/shard_map/ppermute | solution.py:348
  246.0 2.1 collective-permute-done.15
  248.3 0.7 broadcast_in_dim.38
  (60 shorter events, 2.4 us)
Async XLA Ops:
  2.7 19.1 %all-to-all-start.7 = ((bf16[8,176,384]{2,1,0:T(8,128)(2,1)}), bf16[8,176,384]{2,1,0:T(8,128)(2,1)S(1)}, u32[]{:S(2)}, u32[]{:S(2)}) async-start(bf16[8,176,384]{2,1,0:T(8,128)(2,1)} %pack.1), calls=%async_computation.7 | async-start | bytes 2162688 | tf_op jit(solution)/shard_map/all_to_all | solution.py:252
  21.9 48.1 %copy-start.1 = (s32[4,8]{1,0:T(4,128)S(1)}, s32[4,8]{1,0:T(4,128)}, u32[]{:S(2)}) copy-start(s32[4,8]{1,0:T(4,128)} %refs_0_.1) | copy-start | bytes 388
  21.9 48.1 %copy-start.2 = (s32[4]{0:T(128)S(1)}, s32[4]{0:T(128)}, u32[]{:S(2)}) copy-start(s32[4]{0:T(128)} %refs_1_.2) | copy-start | bytes 52
  21.9 48.1 %copy-start.13 = (f32[1,2,128]{2,1,0:T(2,128)S(1)}, f32[1,2,128]{2,1,0:T(2,128)}, u32[]{:S(2)}) copy-start(f32[1,2,128]{2,1,0:T(2,128)} %param.28) | copy-start | bytes 3076
  22.0 47.1 %copy-start.3 = (bf16[4,176,384]{2,1,0:T(8,128)(2,1)}, bf16[4,176,384]{2,1,0:T(8,128)(2,1)S(1)}, u32[]{:S(2)}) copy-start(bf16[4,176,384]{2,1,0:T(8,128)(2,1)S(1)} %get-tuple-element.302.refs_11_.refs_10_) | copy-start | bytes 1622020
  22.0 47.1 %copy-start.4 = (bf16[4,176,384]{2,1,0:T(8,128)(2,1)}, bf16[4,176,384]{2,1,0:T(8,128)(2,1)S(1)}, u32[]{:S(2)}) copy-start(bf16[4,176,384]{2,1,0:T(8,128)(2,1)S(1)} %get-tuple-element.303.refs_12_.refs_11_) | copy-start | bytes 1622020
  22.0 14.0 %collective-permute-start = (bf16[4,176,384]{2,1,0:T(8,128)(2,1)S(1)}, bf16[4,176,384]{2,1,0:T(8,128)(2,1)S(1)}, u32[]{:S(2)}, u32[]{:S(2)}) collective-permute-start(bf16[4,176,384]{2,1,0:T(8,128)(2,1)S(1)} %get-tuple-element.303.refs_12_.refs_11_), channel_id=1, source_target_pairs={{64,72},{65,73},{82,90},{83,91},{100,108},{101,109},{118,126},{119... | collective-permute-start | bytes 1622024 | tf_op jit(solution)/shard_map/ppermute | solution.py:259
  26.0 14.4 %collective-permute-start.1 = (bf16[4,176,384]{2,1,0:T(8,128)(2,1)S(1)}, bf16[4,176,384]{2,1,0:T(8,128)(2,1)S(1)}, u32[]{:S(2)}, u32[]{:S(2)}) collective-permute-start(bf16[4,176,384]{2,1,0:T(8,128)(2,1)S(1)} %get-tuple-element.302.refs_11_.refs_10_), channel_id=1, source_target_pairs={{4,0},{5,1},{12,8},{13,9},{22,18},{23,19},{30,26},{31,27},{32,36},... | collective-permute-start | bytes 1622024 | tf_op jit(solution)/shard_map/ppermute | solution.py:259
  27.3 34.2 %collective-permute-start.2 = (bf16[4,176,384]{2,1,0:T(8,128)(2,1)S(1)}, bf16[4,176,384]{2,1,0:T(8,128)(2,1)S(1)}, u32[]{:S(2)}, u32[]{:S(2)}) collective-permute-start(bf16[4,176,384]{2,1,0:T(8,128)(2,1)S(1)} %get-tuple-element.302.refs_11_.refs_10_), channel_id=1, source_target_pairs={{2,0},{3,1},{10,8},{11,9},{20,18},{21,19},{28,26},{29,27},{38,36},... | collective-permute-start | bytes 1622024 | tf_op jit(solution)/shard_map/ppermute | solution.py:259
  28.6 32.9 %collective-permute-start.3 = (bf16[4,176,384]{2,1,0:T(8,128)(2,1)S(1)}, bf16[4,176,384]{2,1,0:T(8,128)(2,1)S(1)}, u32[]{:S(2)}, u32[]{:S(2)}) collective-permute-start(bf16[4,176,384]{2,1,0:T(8,128)(2,1)S(1)} %get-tuple-element.302.refs_11_.refs_10_), channel_id=1, source_target_pairs={{6,0},{7,1},{14,8},{15,9},{16,18},{17,19},{24,26},{25,27},{34,36},... | collective-permute-start | bytes 1622024 | tf_op jit(solution)/shard_map/ppermute | solution.py:259
  29.9 31.6 %collective-permute-start.4 = (bf16[4,176,384]{2,1,0:T(8,128)(2,1)S(1)}, bf16[4,176,384]{2,1,0:T(8,128)(2,1)S(1)}, u32[]{:S(2)}, u32[]{:S(2)}) collective-permute-start(bf16[4,176,384]{2,1,0:T(8,128)(2,1)S(1)} %get-tuple-element.303.refs_12_.refs_11_), channel_id=1, source_target_pairs={{4,0},{5,1},{12,8},{13,9},{22,18},{23,19},{30,26},{31,27},{32,36},... | collective-permute-start | bytes 1622024 | tf_op jit(solution)/shard_map/ppermute | solution.py:259
  36.0 33.1 %copy-start.5 = (bf16[4,176,384]{2,1,0:T(8,128)(2,1)}, bf16[4,176,384]{2,1,0:T(8,128)(2,1)S(1)}, u32[]{:S(2)}) copy-start(bf16[4,176,384]{2,1,0:T(8,128)(2,1)S(1)} %collective-permute-done.refs_4_.refs_3_) | copy-start | bytes 1622020
  36.0 25.5 %collective-permute-start.5 = (bf16[4,176,384]{2,1,0:T(8,128)(2,1)S(1)}, bf16[4,176,384]{2,1,0:T(8,128)(2,1)S(1)}, u32[]{:S(2)}, u32[]{:S(2)}) collective-permute-start(bf16[4,176,384]{2,1,0:T(8,128)(2,1)S(1)} %get-tuple-element.303.refs_12_.refs_11_), channel_id=1, source_target_pairs={{2,0},{3,1},{10,8},{11,9},{20,18},{21,19},{28,26},{29,27},{38,36},... | collective-permute-start | bytes 1622024 | tf_op jit(solution)/shard_map/ppermute | solution.py:259
  40.5 28.7 %copy-start.6 = (bf16[4,176,384]{2,1,0:T(8,128)(2,1)}, bf16[4,176,384]{2,1,0:T(8,128)(2,1)S(1)}, u32[]{:S(2)}) copy-start(bf16[4,176,384]{2,1,0:T(8,128)(2,1)S(1)} %collective-permute-done.1.refs_5_.refs_4_) | copy-start | bytes 1622020
  40.5 28.7 %collective-permute-start.6 = (bf16[4,176,384]{2,1,0:T(8,128)(2,1)S(1)}, bf16[4,176,384]{2,1,0:T(8,128)(2,1)S(1)}, u32[]{:S(2)}, u32[]{:S(2)}) collective-permute-start(bf16[4,176,384]{2,1,0:T(8,128)(2,1)S(1)} %get-tuple-element.303.refs_12_.refs_11_), channel_id=1, source_target_pairs={{6,0},{7,1},{14,8},{15,9},{16,18},{17,19},{24,26},{25,27},{34,36},... | collective-permute-start | bytes 1622024 | tf_op jit(solution)/shard_map/ppermute | solution.py:259
  61.5 7.6 %copy-start.7 = (bf16[4,176,384]{2,1,0:T(8,128)(2,1)}, bf16[4,176,384]{2,1,0:T(8,128)(2,1)S(1)}, u32[]{:S(2)}) copy-start(bf16[4,176,384]{2,1,0:T(8,128)(2,1)S(1)} %collective-permute-done.2.refs_6_.refs_5_) | copy-start | bytes 1622020
  61.5 7.6 %copy-start.8 = (bf16[4,176,384]{2,1,0:T(8,128)(2,1)}, bf16[4,176,384]{2,1,0:T(8,128)(2,1)S(1)}, u32[]{:S(2)}) copy-start(bf16[4,176,384]{2,1,0:T(8,128)(2,1)S(1)} %collective-permute-done.3.refs_7_.refs_6_) | copy-start | bytes 1622020
  61.5 7.6 %copy-start.9 = (bf16[4,176,384]{2,1,0:T(8,128)(2,1)}, bf16[4,176,384]{2,1,0:T(8,128)(2,1)S(1)}, u32[]{:S(2)}) copy-start(bf16[4,176,384]{2,1,0:T(8,128)(2,1)S(1)} %collective-permute-done.4.refs_8_.refs_7_) | copy-start | bytes 1622020
  61.6 7.6 %copy-start.10 = (bf16[4,176,384]{2,1,0:T(8,128)(2,1)}, bf16[4,176,384]{2,1,0:T(8,128)(2,1)S(1)}, u32[]{:S(2)}) copy-start(bf16[4,176,384]{2,1,0:T(8,128)(2,1)S(1)} %collective-permute-done.5.refs_9_.refs_8_) | copy-start | bytes 1622020
  69.1 0.8 copy-start.11
  70.0 3.0 %copy-start = (bf16[1,256,1536]{2,1,0:T(8,128)(2,1)S(1)}, bf16[1,256,1536]{2,1,0:T(8,128)(2,1)}, u32[]{:S(2)}) copy-start(bf16[1,256,1536]{2,1,0:T(8,128)(2,1)} %param.29) | copy-start | bytes 2359300
  70.0 3.0 %copy-start.12 = (f32[1,1536]{1,0:T(1,128)S(1)}, f32[1,1536]{1,0:T(1,128)}, u32[]{:S(2)}) copy-start(f32[1,1536]{1,0:T(1,128)} %refs_1_.3) | copy-start | bytes 18436
  72.2 6.1 %collective-permute-start.7 = (bf16[2,256,384]{2,1,0:T(8,128)(2,1)S(1)}, bf16[2,256,384]{2,1,0:T(8,128)(2,1)S(1)}, u32[]{:S(2)}, u32[]{:S(2)}) collective-permute-start(bf16[2,256,384]{2,1,0:T(8,128)(2,1)S(1)} %get-tuple-element.279), channel_id=1, source_target_pairs={{0,1},{1,0},{8,9},{9,8},{18,19},{19,18},{26,27},{27,26},{36,37},{3... | collective-permute-start | bytes 1179656 | tf_op jit(solution)/shard_map/ppermute | solution.py:285
  78.6 0.7 collective-permute-start.8
  79.3 0.7 collective-permute-start.9
  80.0 0.7 collective-permute-start.10
  80.9 0.7 collective-permute-start.11
  81.6 0.7 collective-permute-start.12
  82.3 0.7 collective-permute-start.13
  83.1 123.0 %collective-permute-start.14 = (bf16[256,384]{1,0:T(8,128)(2,1)S(1)}, bf16[256,384]{1,0:T(8,128)(2,1)S(1)}, u32[]{:S(2)}, u32[]{:S(2)}) collective-permute-start(bf16[256,384]{1,0:T(8,128)(2,1)S(1)} %get-tuple-element.291), channel_id=1, source_target_pairs={{384,448},{385,449},{392,456},{393,457},{402,466},{403,467},{410,4... | collective-permute-start | bytes 589832 | tf_op jit(solution)/shard_map/ppermute | solution.py:329
  243.0 5.1 %collective-permute-start.15 = (bf16[4,3,8,384]{3,2,1,0:T(8,128)(2,1)S(1)}, bf16[4,3,8,384]{3,2,1,0:T(8,128)(2,1)S(1)}, u32[]{:S(2)}, u32[]{:S(2)}) collective-permute-start(bf16[4,3,8,384]{3,2,1,0:T(8,128)(2,1)S(1)} %broadcast_select_fusion), channel_id=1, source_target_pairs={{64,65},{65,64},{66,67},{67,66},{68,69},{69,68},{70,71},{71,70},{7... | collective-permute-start | bytes 221192 | tf_op jit(solution)/shard_map/ppermute | solution.py:348

commit v6 on v5

--- a/solution.py
+++ b/solution.py
@@ -257,7 +257,11 @@
         jnp.where(odd, jnp.where(low, by_half[:, 1], by_half[:, 0]), ring[4:]),
     )
     pieces = [lax.ppermute(lanes[lane], AX, move_pairs(ahead, lane, sections)) for ahead, lane in MOVES]
-    pieces = [pltpu.with_memory_space_constraint(piece, pltpu.HBM) for piece in (*pieces, *lanes)]
+    pieces = [
+        *[pltpu.with_memory_space_constraint(piece, pltpu.HBM) for piece in pieces[:-2]],
+        *pieces[-2:],
+        *[pltpu.with_memory_space_constraint(lane, pltpu.HBM) for lane in lanes],
+    ]
 
     qk = qk_gain[0]
     block = jax.ShapeDtypeStruct((tokens, width), BF)
@@ -348,9 +352,10 @@
     other = lax.ppermute(jnp.where(head == 0, found[1], found[0]), AX, swap)
     left = jnp.where(odd & (head == 1), other, found[0])
     right = jnp.where(odd & (head == 0), other, found[1])
-    out = jnp.stack([left, right]).transpose(2, 1, 3, 0, 4)
-    out = out.reshape(3, micros, tok, half_width)
-    return (out[0][None], out[1:][None])
+    sides = jnp.stack([left, right])
+    hidden = sides[:, :, 0].transpose(1, 2, 0, 3).reshape(1, micros, tok, half_width)
+    cache = sides[:, :, 1:].transpose(2, 1, 3, 0, 4).reshape(1, 2, micros, tok, half_width)
+    return (hidden, cache)
 
 
 def solution(mesh):

time: 251 us -> 250 us (level)
  no operation moved by 1% of the time
where the time goes in v6:
time: 250 us; the launch traced here: 249 us
  waiting for transfers between devices  171 us (68%)
  blocking collectives  32.8 us (13%)
  starting transfers between devices  27.8 us (11%)
  Pallas kernels  13.5 us (5%)
    ppermute x7, waiting for transfers between devices, shards(): entering = lax.ppermute(kept[0], AX, hop_pairs(step - 1))  122 us
    ppermute x7, waiting for transfers between devices, shards(): lax.ppermute(lanes[lane], AX, move_pairs(ahead, lane, sections))  34.7 us
    all_to_all x1, blocking collectives, shards(): result = lax.all_to_all(jnp.moveaxis(result, 1, 0), 'blk', 0, 0, tiled=True)  23 us
    all_to_all x1, waiting for transfers between devices, shards(): lax.all_to_all(packed, AX, 0, 0, axis_index_groups=ring_groups(sections),...  12 us
    ppermute x7, starting transfers between devices, shards(): lax.ppermute(lanes[lane], AX, move_pairs(ahead, lane, sections))  11.7 us
    all_to_all x1, blocking collectives, advance(): lax.all_to_all(jnp.broadcast_to(entering[None], (4,) + entering.shape), P...  9.79 us
    all_to_all x1, starting transfers between devices, shards(): lax.all_to_all(packed, AX, 0, 0, axis_index_groups=ring_groups(sections),...  7.1 us
    ppermute x7, starting transfers between devices, shards(): entering = lax.ppermute(kept[0], AX, hop_pairs(step - 1))  5.33 us
  transfers between devices with their start and end apart: 17, of which 7 were waited for; matrix products, arithmetic and copies ran while one was open for 0% of the time, Pallas kernels for 2%

profile of v6, /device:TPU:7, one launch (start us, length us, event | category | flops | bytes accessed | tf_op | source)
XLA Modules:
  0.0 249.0 jit_solution(10858017622353184471)
XLA Ops:
  0.6 2.1 pack.1
  2.7 7.1 %all-to-all-start.7 = ((bf16[8,176,384]{2,1,0:T(8,128)(2,1)}), bf16[8,176,384]{2,1,0:T(8,128)(2,1)S(1)}, u32[]{:S(2)}, u32[]{:S(2)}) async-start(bf16[8,176,384]{2,1,0:T(8,128)(2,1)} %pack.1), calls=%async_computation.7 | async-start | bytes 2162688 | tf_op jit(solution)/shard_map/all_to_all | solution.py:252
  9.8 12.0 %all-to-all-done.7 = bf16[8,176,384]{2,1,0:T(8,128)(2,1)S(1)} async-done(((bf16[8,176,384]{2,1,0:T(8,128)(2,1)}), bf16[8,176,384]{2,1,0:T(8,128)(2,1)S(1)}, u32[]{:S(2)}, u32[]{:S(2)}) %all-to-all-start.7) | async-done | bytes 1081376 | tf_op jit(solution)/shard_map/all_to_all | solution.py:252
  22.0 4.0 %collective-permute-start = (bf16[4,176,384]{2,1,0:T(8,128)(2,1)S(1)}, bf16[4,176,384]{2,1,0:T(8,128)(2,1)S(1)}, u32[]{:S(2)}, u32[]{:S(2)}) collective-permute-start(bf16[4,176,384]{2,1,0:T(8,128)(2,1)S(1)} %get-tuple-element.303.refs_12_.refs_11_), channel_id=1, source_target_pairs={{64,72},{65,73},{82,90},{83,91},{100,108},{101,109},{118,126},{119... | collective-permute-start | bytes 1622024 | tf_op jit(solution)/shard_map/ppermute | solution.py:259
  26.0 1.3 collective-permute-start.1
  27.3 1.3 collective-permute-start.2
  28.6 1.3 collective-permute-start.3
  29.9 1.3 collective-permute-start.4
  31.2 4.8 %collective-permute-done.refs_4_.refs_3_ = bf16[4,176,384]{2,1,0:T(8,128)(2,1)S(1)} collective-permute-done((bf16[4,176,384]{2,1,0:T(8,128)(2,1)S(1)}, bf16[4,176,384]{2,1,0:T(8,128)(2,1)S(1)}, u32[]{:S(2)}, u32[]{:S(2)}) %collective-permute-start) | collective-permute-done | bytes 540704 | tf_op jit(solution)/shard_map/ppermute | solution.py:259
  36.0 1.3 collective-permute-start.5
  37.3 3.1 %collective-permute-done.1.refs_5_.refs_4_ = bf16[4,176,384]{2,1,0:T(8,128)(2,1)S(1)} collective-permute-done((bf16[4,176,384]{2,1,0:T(8,128)(2,1)S(1)}, bf16[4,176,384]{2,1,0:T(8,128)(2,1)S(1)}, u32[]{:S(2)}, u32[]{:S(2)}) %collective-permute-start.1) | collective-permute-done | bytes 540704 | tf_op jit(solution)/shard_map/ppermute | solution.py:259
  40.5 1.3 collective-permute-start.6
  42.4 19.1 %collective-permute-done.2.refs_6_.refs_5_ = bf16[4,176,384]{2,1,0:T(8,128)(2,1)S(1)} collective-permute-done((bf16[4,176,384]{2,1,0:T(8,128)(2,1)S(1)}, bf16[4,176,384]{2,1,0:T(8,128)(2,1)S(1)}, u32[]{:S(2)}, u32[]{:S(2)}) %collective-permute-start.2) | collective-permute-done | bytes 540704 | tf_op jit(solution)/shard_map/ppermute | solution.py:259
  61.5 7.6 %collective-permute-done.6.refs_10_.refs_9_ = bf16[4,176,384]{2,1,0:T(8,128)(2,1)S(1)} collective-permute-done((bf16[4,176,384]{2,1,0:T(8,128)(2,1)S(1)}, bf16[4,176,384]{2,1,0:T(8,128)(2,1)S(1)}, u32[]{:S(2)}, u32[]{:S(2)}) %collective-permute-start.6) | collective-permute-done | bytes 540704 | tf_op jit(solution)/shard_map/ppermute | solution.py:259
  69.2 2.2 tails.1
  71.5 0.7 collective-permute-start.7
  72.2 5.2 %prepare.1 = (bf16[1536,1152]{1,0:T(8,128)(2,1)}, bf16[256,384]{1,0:T(8,128)(2,1)S(1)}, bf16[256,384]{1,0:T(8,128)(2,1)S(1)}) custom-call(bf16[256,1536]{1,0:T(8,128)(2,1)S(1)} %bitcast.42, f32[1,1536]{1,0:T(1,128)S(1)} %copy-done.10, f32[2,128]{1,0:T(2,128)S(1)} %bitcast.47, bf16[4,176,384]{2,1,0:T(8,128)(2,1)} %copy-done.5, ...), custom_call_target="tpu_custom_call" | custom-call | flops 603979776 | bytes 7077888 | tf_op jit(solution)/shard_map/prepare/pallas_call | solution.py:290
  77.7 0.7 collective-permute-start.8
  78.4 0.7 collective-permute-start.9
  79.1 0.7 collective-permute-start.10
  80.0 0.7 collective-permute-start.11
  80.7 0.7 collective-permute-start.12
  81.4 0.7 collective-permute-start.13
  82.1 1.3 collective-permute-start.14
  83.4 121.9 %collective-permute-done.14 = bf16[256,384]{1,0:T(8,128)(2,1)S(1)} collective-permute-done((bf16[256,384]{1,0:T(8,128)(2,1)S(1)}, bf16[256,384]{1,0:T(8,128)(2,1)S(1)}, u32[]{:S(2)}, u32[]{:S(2)}) %collective-permute-start.14) | collective-permute-done | bytes 196640 | tf_op jit(solution)/shard_map/ppermute | solution.py:333
  205.3 13.9 %conditional.15 = ((bf16[256,384]{1,0:T(8,128)(2,1)S(1)}, bf16[2,256,384]{2,1,0:T(8,128)(2,1)S(1)})) conditional(s32[]{:T(128)} %convert_element_type.24, (bf16[256,384]{1,0:T(8,128)(2,1)S(1)}, bf16[2,256,384]{2,1,0:T(8,128)(2,1)S(1)}) %get-tuple-element.352, (bf16[256,384]{1,0:T(8,128)(2,1)S(1)}, s32[8,128]{1,0:T(8,128)S(1)}, ...), branch_computations={%region_14.15_spmd, %region_15.16_spmd} | conditional | bytes 2555912 | solution.py:334
  205.4 9.8 %all_to_all.44.x_ref = bf16[4,256,384]{2,1,0:T(8,128)(2,1)S(1)} all-to-all(bf16[4,256,384]{2,1,0:T(8,128)(2,1)S(1)} %broadcast_in_dim.31), channel_id=1, replica_groups={{0,8,1,9},{2,10,3,11},{4,12,5,13},{6,14,7,15},{16,24,17,25},{18,26,19,2..., dimensions={0} | all-to-all | bytes 1572864 | tf_op jit(solution)/shard_map/cond/branch_1_fun/all_to_all | solution.py:321
  215.2 4.0 %layer.15 = (bf16[256,384]{1,0:T(8,128)(2,1)S(1)}, bf16[2,256,384]{2,1,0:T(8,128)(2,1)S(1)}) custom-call(s32[8,128]{1,0:T(8,128)S(1)} %get-tuple-element.251.info_ref, bf16[4,256,384]{2,1,0:T(8,128)(2,1)S(1)} %all_to_all.44.x_ref, bf16[1536,1152]{1,0:T(8,128)(2,1)} %get-tuple-element.253.w_ref, f32[1,1536]{1,0:T(1,128)S(1)} %get-tuple-element.254.gain_ref, ...), custom_call_target="tpu_custom_call" | custom-call | tf_op jit(solution)/shard_map/cond/branch_1_fun/layer/pallas_call | solution.py:325
  219.3 23.0 %all_to_all.45 = bf16[32,3,8,384]{3,2,1,0:T(8,128)(2,1)S(1)} all-to-all(bf16[32,3,8,384]{3,2,1,0:T(8,128)(2,1)S(1)} %maximum_bitcast_fusion), channel_id=1, replica_groups=mesh['section'=8,'blk'=32,'head'=2] {'blk'}, dimensions={0} | all-to-all | bytes 1179648 | tf_op jit(solution)/shard_map/all_to_all | solution.py:342
  242.3 2.9 %collective-permute-start.15 = (bf16[4,3,8,384]{3,2,1,0:T(8,128)(2,1)S(1)}, bf16[4,3,8,384]{3,2,1,0:T(8,128)(2,1)S(1)}, u32[]{:S(2)}, u32[]{:S(2)}) collective-permute-start(bf16[4,3,8,384]{3,2,1,0:T(8,128)(2,1)S(1)} %broadcast_select_fusion), channel_id=1, source_target_pairs={{64,65},{65,64},{66,67},{67,66},{68,69},{69,68},{70,71},{71,70},{7... | collective-permute-start | bytes 221192 | tf_op jit(solution)/shard_map/ppermute | solution.py:352
  245.3 2.1 collective-permute-done.15
  247.6 0.7 reshape.42
  (55 shorter events, 1.8 us)
Async XLA Ops:
  2.7 19.1 %all-to-all-start.7 = ((bf16[8,176,384]{2,1,0:T(8,128)(2,1)}), bf16[8,176,384]{2,1,0:T(8,128)(2,1)S(1)}, u32[]{:S(2)}, u32[]{:S(2)}) async-start(bf16[8,176,384]{2,1,0:T(8,128)(2,1)} %pack.1), calls=%async_computation.7 | async-start | bytes 2162688 | tf_op jit(solution)/shard_map/all_to_all | solution.py:252
  21.8 47.3 %copy-start.1 = (s32[4,8]{1,0:T(4,128)S(1)}, s32[4,8]{1,0:T(4,128)}, u32[]{:S(2)}) copy-start(s32[4,8]{1,0:T(4,128)} %refs_0_.1) | copy-start | bytes 388
  21.8 47.4 %copy-start.2 = (s32[4]{0:T(128)S(1)}, s32[4]{0:T(128)}, u32[]{:S(2)}) copy-start(s32[4]{0:T(128)} %refs_1_.2) | copy-start | bytes 52
  21.8 47.4 %copy-start.11 = (f32[1,2,128]{2,1,0:T(2,128)S(1)}, f32[1,2,128]{2,1,0:T(2,128)}, u32[]{:S(2)}) copy-start(f32[1,2,128]{2,1,0:T(2,128)} %param.28) | copy-start | bytes 3076
  22.0 47.1 %copy-start.3 = (bf16[4,176,384]{2,1,0:T(8,128)(2,1)}, bf16[4,176,384]{2,1,0:T(8,128)(2,1)S(1)}, u32[]{:S(2)}) copy-start(bf16[4,176,384]{2,1,0:T(8,128)(2,1)S(1)} %get-tuple-element.302.refs_11_.refs_10_) | copy-start | bytes 1622020
  22.0 47.1 %copy-start.4 = (bf16[4,176,384]{2,1,0:T(8,128)(2,1)}, bf16[4,176,384]{2,1,0:T(8,128)(2,1)S(1)}, u32[]{:S(2)}) copy-start(bf16[4,176,384]{2,1,0:T(8,128)(2,1)S(1)} %get-tuple-element.303.refs_12_.refs_11_) | copy-start | bytes 1622020
  22.0 14.0 %collective-permute-start = (bf16[4,176,384]{2,1,0:T(8,128)(2,1)S(1)}, bf16[4,176,384]{2,1,0:T(8,128)(2,1)S(1)}, u32[]{:S(2)}, u32[]{:S(2)}) collective-permute-start(bf16[4,176,384]{2,1,0:T(8,128)(2,1)S(1)} %get-tuple-element.303.refs_12_.refs_11_), channel_id=1, source_target_pairs={{64,72},{65,73},{82,90},{83,91},{100,108},{101,109},{118,126},{119... | collective-permute-start | bytes 1622024 | tf_op jit(solution)/shard_map/ppermute | solution.py:259
  26.0 14.4 %collective-permute-start.1 = (bf16[4,176,384]{2,1,0:T(8,128)(2,1)S(1)}, bf16[4,176,384]{2,1,0:T(8,128)(2,1)S(1)}, u32[]{:S(2)}, u32[]{:S(2)}) collective-permute-start(bf16[4,176,384]{2,1,0:T(8,128)(2,1)S(1)} %get-tuple-element.302.refs_11_.refs_10_), channel_id=1, source_target_pairs={{4,0},{5,1},{12,8},{13,9},{22,18},{23,19},{30,26},{31,27},{32,36},... | collective-permute-start | bytes 1622024 | tf_op jit(solution)/shard_map/ppermute | solution.py:259
  27.3 34.2 %collective-permute-start.2 = (bf16[4,176,384]{2,1,0:T(8,128)(2,1)S(1)}, bf16[4,176,384]{2,1,0:T(8,128)(2,1)S(1)}, u32[]{:S(2)}, u32[]{:S(2)}) collective-permute-start(bf16[4,176,384]{2,1,0:T(8,128)(2,1)S(1)} %get-tuple-element.302.refs_11_.refs_10_), channel_id=1, source_target_pairs={{2,0},{3,1},{10,8},{11,9},{20,18},{21,19},{28,26},{29,27},{38,36},... | collective-permute-start | bytes 1622024 | tf_op jit(solution)/shard_map/ppermute | solution.py:259
  28.6 32.9 %collective-permute-start.3 = (bf16[4,176,384]{2,1,0:T(8,128)(2,1)S(1)}, bf16[4,176,384]{2,1,0:T(8,128)(2,1)S(1)}, u32[]{:S(2)}, u32[]{:S(2)}) collective-permute-start(bf16[4,176,384]{2,1,0:T(8,128)(2,1)S(1)} %get-tuple-element.302.refs_11_.refs_10_), channel_id=1, source_target_pairs={{6,0},{7,1},{14,8},{15,9},{16,18},{17,19},{24,26},{25,27},{34,36},... | collective-permute-start | bytes 1622024 | tf_op jit(solution)/shard_map/ppermute | solution.py:259
  29.9 31.6 %collective-permute-start.4 = (bf16[4,176,384]{2,1,0:T(8,128)(2,1)S(1)}, bf16[4,176,384]{2,1,0:T(8,128)(2,1)S(1)}, u32[]{:S(2)}, u32[]{:S(2)}) collective-permute-start(bf16[4,176,384]{2,1,0:T(8,128)(2,1)S(1)} %get-tuple-element.303.refs_12_.refs_11_), channel_id=1, source_target_pairs={{4,0},{5,1},{12,8},{13,9},{22,18},{23,19},{30,26},{31,27},{32,36},... | collective-permute-start | bytes 1622024 | tf_op jit(solution)/shard_map/ppermute | solution.py:259
  36.0 33.1 %copy-start.5 = (bf16[4,176,384]{2,1,0:T(8,128)(2,1)}, bf16[4,176,384]{2,1,0:T(8,128)(2,1)S(1)}, u32[]{:S(2)}) copy-start(bf16[4,176,384]{2,1,0:T(8,128)(2,1)S(1)} %collective-permute-done.refs_4_.refs_3_) | copy-start | bytes 1622020
  36.0 25.5 %collective-permute-start.5 = (bf16[4,176,384]{2,1,0:T(8,128)(2,1)S(1)}, bf16[4,176,384]{2,1,0:T(8,128)(2,1)S(1)}, u32[]{:S(2)}, u32[]{:S(2)}) collective-permute-start(bf16[4,176,384]{2,1,0:T(8,128)(2,1)S(1)} %get-tuple-element.303.refs_12_.refs_11_), channel_id=1, source_target_pairs={{2,0},{3,1},{10,8},{11,9},{20,18},{21,19},{28,26},{29,27},{38,36},... | collective-permute-start | bytes 1622024 | tf_op jit(solution)/shard_map/ppermute | solution.py:259
  40.5 28.7 %copy-start.6 = (bf16[4,176,384]{2,1,0:T(8,128)(2,1)}, bf16[4,176,384]{2,1,0:T(8,128)(2,1)S(1)}, u32[]{:S(2)}) copy-start(bf16[4,176,384]{2,1,0:T(8,128)(2,1)S(1)} %collective-permute-done.1.refs_5_.refs_4_) | copy-start | bytes 1622020
  40.5 28.7 %collective-permute-start.6 = (bf16[4,176,384]{2,1,0:T(8,128)(2,1)S(1)}, bf16[4,176,384]{2,1,0:T(8,128)(2,1)S(1)}, u32[]{:S(2)}, u32[]{:S(2)}) collective-permute-start(bf16[4,176,384]{2,1,0:T(8,128)(2,1)S(1)} %get-tuple-element.303.refs_12_.refs_11_), channel_id=1, source_target_pairs={{6,0},{7,1},{14,8},{15,9},{16,18},{17,19},{24,26},{25,27},{34,36},... | collective-permute-start | bytes 1622024 | tf_op jit(solution)/shard_map/ppermute | solution.py:259
  61.5 7.6 %copy-start.7 = (bf16[4,176,384]{2,1,0:T(8,128)(2,1)}, bf16[4,176,384]{2,1,0:T(8,128)(2,1)S(1)}, u32[]{:S(2)}) copy-start(bf16[4,176,384]{2,1,0:T(8,128)(2,1)S(1)} %collective-permute-done.2.refs_6_.refs_5_) | copy-start | bytes 1622020
  61.5 7.6 %copy-start.8 = (bf16[4,176,384]{2,1,0:T(8,128)(2,1)}, bf16[4,176,384]{2,1,0:T(8,128)(2,1)S(1)}, u32[]{:S(2)}) copy-start(bf16[4,176,384]{2,1,0:T(8,128)(2,1)S(1)} %collective-permute-done.3.refs_7_.refs_6_) | copy-start | bytes 1622020
  61.5 7.6 %copy-start.9 = (bf16[4,176,384]{2,1,0:T(8,128)(2,1)}, bf16[4,176,384]{2,1,0:T(8,128)(2,1)S(1)}, u32[]{:S(2)}) copy-start(bf16[4,176,384]{2,1,0:T(8,128)(2,1)S(1)} %collective-permute-done.4.refs_8_.refs_7_) | copy-start | bytes 1622020
  69.2 3.0 %copy-start = (bf16[1,256,1536]{2,1,0:T(8,128)(2,1)S(1)}, bf16[1,256,1536]{2,1,0:T(8,128)(2,1)}, u32[]{:S(2)}) copy-start(bf16[1,256,1536]{2,1,0:T(8,128)(2,1)} %param.29) | copy-start | bytes 2359300
  69.2 3.0 %copy-start.10 = (f32[1,1536]{1,0:T(1,128)S(1)}, f32[1,1536]{1,0:T(1,128)}, u32[]{:S(2)}) copy-start(f32[1,1536]{1,0:T(1,128)} %refs_1_.3) | copy-start | bytes 18436
  71.5 5.9 %collective-permute-start.7 = (bf16[2,256,384]{2,1,0:T(8,128)(2,1)S(1)}, bf16[2,256,384]{2,1,0:T(8,128)(2,1)S(1)}, u32[]{:S(2)}, u32[]{:S(2)}) collective-permute-start(bf16[2,256,384]{2,1,0:T(8,128)(2,1)S(1)} %get-tuple-element.279), channel_id=1, source_target_pairs={{0,1},{1,0},{8,9},{9,8},{18,19},{19,18},{26,27},{27,26},{36,37},{3... | collective-permute-start | bytes 1179656 | tf_op jit(solution)/shard_map/ppermute | solution.py:289
  77.7 0.7 collective-permute-start.8
  78.4 0.7 collective-permute-start.9
  79.1 0.7 collective-permute-start.10
  80.0 0.7 collective-permute-start.11
  80.7 0.7 collective-permute-start.12
  81.4 0.7 collective-permute-start.13
  82.1 123.2 %collective-permute-start.14 = (bf16[256,384]{1,0:T(8,128)(2,1)S(1)}, bf16[256,384]{1,0:T(8,128)(2,1)S(1)}, u32[]{:S(2)}, u32[]{:S(2)}) collective-permute-start(bf16[256,384]{1,0:T(8,128)(2,1)S(1)} %get-tuple-element.291), channel_id=1, source_target_pairs={{384,448},{385,449},{392,456},{393,457},{402,466},{403,467},{410,4... | collective-permute-start | bytes 589832 | tf_op jit(solution)/shard_map/ppermute | solution.py:333
  242.3 5.1 %collective-permute-start.15 = (bf16[4,3,8,384]{3,2,1,0:T(8,128)(2,1)S(1)}, bf16[4,3,8,384]{3,2,1,0:T(8,128)(2,1)S(1)}, u32[]{:S(2)}, u32[]{:S(2)}) collective-permute-start(bf16[4,3,8,384]{3,2,1,0:T(8,128)(2,1)S(1)} %broadcast_select_fusion), channel_id=1, source_target_pairs={{64,65},{65,64},{66,67},{67,66},{68,69},{69,68},{70,71},{71,70},{7... | collective-permute-start | bytes 221192 | tf_op jit(solution)/shard_map/ppermute | solution.py:352

commit v7 on v6

--- a/solution.py
+++ b/solution.py
@@ -13,7 +13,7 @@
 ROWS = 48
 TAIL = 32
 PIECE = 3 * ROWS + TAIL
-MOVES = [(0, 1), (2, 0), (1, 0), (3, 0), (2, 1), (1, 1), (3, 1)]
+MOVES = [(2, 0), (2, 1), (0, 1), (1, 0), (1, 1), (3, 0), (3, 1)]
 HBM = pl.BlockSpec(memory_space=pltpu.HBM)
 VMEM = pl.BlockSpec(memory_space=pltpu.VMEM)
 SMEM = pl.BlockSpec(memory_space=pltpu.SMEM)

time: 250 us -> 250 us (level)
  no operation moved by 1% of the time
where the time goes in v7:
time: 250 us; the launch traced here: 249 us
  waiting for transfers between devices  172 us (69%)
  blocking collectives  32.2 us (13%)
  starting transfers between devices  27.8 us (11%)
  Pallas kernels  13.5 us (5%)
    ppermute x7, waiting for transfers between devices, shards(): entering = lax.ppermute(kept[0], AX, hop_pairs(step - 1))  123 us
    ppermute x7, waiting for transfers between devices, shards(): lax.ppermute(lanes[lane], AX, move_pairs(ahead, lane, sections))  34.5 us
    all_to_all x1, blocking collectives, shards(): result = lax.all_to_all(jnp.moveaxis(result, 1, 0), 'blk', 0, 0, tiled=True)  22.4 us
    all_to_all x1, waiting for transfers between devices, shards(): lax.all_to_all(packed, AX, 0, 0, axis_index_groups=ring_groups(sections),...  12 us
    ppermute x7, starting transfers between devices, shards(): lax.ppermute(lanes[lane], AX, move_pairs(ahead, lane, sections))  11.7 us
    all_to_all x1, blocking collectives, advance(): lax.all_to_all(jnp.broadcast_to(entering[None], (4,) + entering.shape), P...  9.79 us
    all_to_all x1, starting transfers between devices, shards(): lax.all_to_all(packed, AX, 0, 0, axis_index_groups=ring_groups(sections),...  7.1 us
    ppermute x7, starting transfers between devices, shards(): entering = lax.ppermute(kept[0], AX, hop_pairs(step - 1))  5.33 us
  transfers between devices with their start and end apart: 17, of which 7 were waited for; matrix products, arithmetic and copies ran while one was open for 0% of the time, Pallas kernels for 2%

profile of v7, /device:TPU:7, one launch (start us, length us, event | category | flops | bytes accessed | tf_op | source)
XLA Modules:
  0.0 249.4 jit_solution(9985764753125346607)
XLA Ops:
  0.6 2.1 pack.1
  2.7 7.1 %all-to-all-start.7 = ((bf16[8,176,384]{2,1,0:T(8,128)(2,1)}), bf16[8,176,384]{2,1,0:T(8,128)(2,1)S(1)}, u32[]{:S(2)}, u32[]{:S(2)}) async-start(bf16[8,176,384]{2,1,0:T(8,128)(2,1)} %pack.1), calls=%async_computation.7 | async-start | bytes 2162688 | tf_op jit(solution)/shard_map/all_to_all | solution.py:252
  9.8 12.0 %all-to-all-done.7 = bf16[8,176,384]{2,1,0:T(8,128)(2,1)S(1)} async-done(((bf16[8,176,384]{2,1,0:T(8,128)(2,1)}), bf16[8,176,384]{2,1,0:T(8,128)(2,1)S(1)}, u32[]{:S(2)}, u32[]{:S(2)}) %all-to-all-start.7) | async-done | bytes 1081376 | tf_op jit(solution)/shard_map/all_to_all | solution.py:252
  22.0 1.3 collective-permute-start
  23.3 1.3 collective-permute-start.1
  24.6 4.0 %collective-permute-start.2 = (bf16[4,176,384]{2,1,0:T(8,128)(2,1)S(1)}, bf16[4,176,384]{2,1,0:T(8,128)(2,1)S(1)}, u32[]{:S(2)}, u32[]{:S(2)}) collective-permute-start(bf16[4,176,384]{2,1,0:T(8,128)(2,1)S(1)} %get-tuple-element.302.refs_12_.refs_11_), channel_id=1, source_target_pairs={{64,72},{65,73},{82,90},{83,91},{100,108},{101,109},{118,126},{119... | collective-permute-start | bytes 1622024 | tf_op jit(solution)/shard_map/ppermute | solution.py:259
  28.6 1.3 collective-permute-start.3
  29.9 1.3 collective-permute-start.4
  31.2 8.9 %collective-permute-done.refs_4_.refs_3_ = bf16[4,176,384]{2,1,0:T(8,128)(2,1)S(1)} collective-permute-done((bf16[4,176,384]{2,1,0:T(8,128)(2,1)S(1)}, bf16[4,176,384]{2,1,0:T(8,128)(2,1)S(1)}, u32[]{:S(2)}, u32[]{:S(2)}) %collective-permute-start) | collective-permute-done | bytes 540704 | tf_op jit(solution)/shard_map/ppermute | solution.py:259
  40.1 1.3 collective-permute-start.5
  41.4 4.5 %collective-permute-done.1.refs_5_.refs_4_ = bf16[4,176,384]{2,1,0:T(8,128)(2,1)S(1)} collective-permute-done((bf16[4,176,384]{2,1,0:T(8,128)(2,1)S(1)}, bf16[4,176,384]{2,1,0:T(8,128)(2,1)S(1)}, u32[]{:S(2)}, u32[]{:S(2)}) %collective-permute-start.1) | collective-permute-done | bytes 540704 | tf_op jit(solution)/shard_map/ppermute | solution.py:259
  45.9 1.3 collective-permute-start.6
  47.8 15.0 %collective-permute-done.3.refs_7_.refs_6_ = bf16[4,176,384]{2,1,0:T(8,128)(2,1)S(1)} collective-permute-done((bf16[4,176,384]{2,1,0:T(8,128)(2,1)S(1)}, bf16[4,176,384]{2,1,0:T(8,128)(2,1)S(1)}, u32[]{:S(2)}, u32[]{:S(2)}) %collective-permute-start.3) | collective-permute-done | bytes 540704 | tf_op jit(solution)/shard_map/ppermute | solution.py:259
  62.8 6.1 %collective-permute-done.6.refs_10_.refs_9_ = bf16[4,176,384]{2,1,0:T(8,128)(2,1)S(1)} collective-permute-done((bf16[4,176,384]{2,1,0:T(8,128)(2,1)S(1)}, bf16[4,176,384]{2,1,0:T(8,128)(2,1)S(1)}, u32[]{:S(2)}, u32[]{:S(2)}) %collective-permute-start.6) | collective-permute-done | bytes 540704 | tf_op jit(solution)/shard_map/ppermute | solution.py:259
  69.1 2.2 tails.1
  71.3 0.7 collective-permute-start.7
  72.0 5.2 %prepare.1 = (bf16[1536,1152]{1,0:T(8,128)(2,1)}, bf16[256,384]{1,0:T(8,128)(2,1)S(1)}, bf16[256,384]{1,0:T(8,128)(2,1)S(1)}) custom-call(bf16[256,1536]{1,0:T(8,128)(2,1)S(1)} %bitcast.42, f32[1,1536]{1,0:T(1,128)S(1)} %copy-done.10, f32[2,128]{1,0:T(2,128)S(1)} %bitcast.47, bf16[4,176,384]{2,1,0:T(8,128)(2,1)} %copy-done.5, ...), custom_call_target="tpu_custom_call" | custom-call | flops 603979776 | bytes 7077888 | tf_op jit(solution)/shard_map/prepare/pallas_call | solution.py:290
  77.4 0.7 collective-permute-start.8
  78.1 0.7 collective-permute-start.9
  78.8 0.7 collective-permute-start.10
  79.7 0.7 collective-permute-start.11
  80.4 0.7 collective-permute-start.12
  81.2 0.7 collective-permute-start.13
  81.9 1.3 collective-permute-start.14
  83.2 123.1 %collective-permute-done.14 = bf16[256,384]{1,0:T(8,128)(2,1)S(1)} collective-permute-done((bf16[256,384]{1,0:T(8,128)(2,1)S(1)}, bf16[256,384]{1,0:T(8,128)(2,1)S(1)}, u32[]{:S(2)}, u32[]{:S(2)}) %collective-permute-start.14) | collective-permute-done | bytes 196640 | tf_op jit(solution)/shard_map/ppermute | solution.py:333
  206.3 13.9 %conditional.15 = ((bf16[256,384]{1,0:T(8,128)(2,1)S(1)}, bf16[2,256,384]{2,1,0:T(8,128)(2,1)S(1)})) conditional(s32[]{:T(128)} %convert_element_type.24, (bf16[256,384]{1,0:T(8,128)(2,1)S(1)}, bf16[2,256,384]{2,1,0:T(8,128)(2,1)S(1)}) %get-tuple-element.352, (bf16[256,384]{1,0:T(8,128)(2,1)S(1)}, s32[8,128]{1,0:T(8,128)S(1)}, ...), branch_computations={%region_14.15_spmd, %region_15.16_spmd} | conditional | bytes 2555912 | solution.py:334
  206.4 9.8 %all_to_all.44.x_ref = bf16[4,256,384]{2,1,0:T(8,128)(2,1)S(1)} all-to-all(bf16[4,256,384]{2,1,0:T(8,128)(2,1)S(1)} %broadcast_in_dim.31), channel_id=1, replica_groups={{0,8,1,9},{2,10,3,11},{4,12,5,13},{6,14,7,15},{16,24,17,25},{18,26,19,2..., dimensions={0} | all-to-all | bytes 1572864 | tf_op jit(solution)/shard_map/cond/branch_1_fun/all_to_all | solution.py:321
  216.2 4.0 %layer.15 = (bf16[256,384]{1,0:T(8,128)(2,1)S(1)}, bf16[2,256,384]{2,1,0:T(8,128)(2,1)S(1)}) custom-call(s32[8,128]{1,0:T(8,128)S(1)} %get-tuple-element.251.info_ref, bf16[4,256,384]{2,1,0:T(8,128)(2,1)S(1)} %all_to_all.44.x_ref, bf16[1536,1152]{1,0:T(8,128)(2,1)} %get-tuple-element.253.w_ref, f32[1,1536]{1,0:T(1,128)S(1)} %get-tuple-element.254.gain_ref, ...), custom_call_target="tpu_custom_call" | custom-call | tf_op jit(solution)/shard_map/cond/branch_1_fun/layer/pallas_call | solution.py:325
  220.3 22.4 %all_to_all.45 = bf16[32,3,8,384]{3,2,1,0:T(8,128)(2,1)S(1)} all-to-all(bf16[32,3,8,384]{3,2,1,0:T(8,128)(2,1)S(1)} %maximum_bitcast_fusion), channel_id=1, replica_groups=mesh['section'=8,'blk'=32,'head'=2] {'blk'}, dimensions={0} | all-to-all | bytes 1179648 | tf_op jit(solution)/shard_map/all_to_all | solution.py:342
  242.7 2.9 %collective-permute-start.15 = (bf16[4,3,8,384]{3,2,1,0:T(8,128)(2,1)S(1)}, bf16[4,3,8,384]{3,2,1,0:T(8,128)(2,1)S(1)}, u32[]{:S(2)}, u32[]{:S(2)}) collective-permute-start(bf16[4,3,8,384]{3,2,1,0:T(8,128)(2,1)S(1)} %broadcast_select_fusion), channel_id=1, source_target_pairs={{64,65},{65,64},{66,67},{67,66},{68,69},{69,68},{70,71},{71,70},{7... | collective-permute-start | bytes 221192 | tf_op jit(solution)/shard_map/ppermute | solution.py:352
  245.7 2.1 collective-permute-done.15
  248.0 0.7 reshape.42
  (55 shorter events, 1.8 us)
Async XLA Ops:
  2.7 19.1 %all-to-all-start.7 = ((bf16[8,176,384]{2,1,0:T(8,128)(2,1)}), bf16[8,176,384]{2,1,0:T(8,128)(2,1)S(1)}, u32[]{:S(2)}, u32[]{:S(2)}) async-start(bf16[8,176,384]{2,1,0:T(8,128)(2,1)} %pack.1), calls=%async_computation.7 | async-start | bytes 2162688 | tf_op jit(solution)/shard_map/all_to_all | solution.py:252
  21.8 47.2 %copy-start.1 = (s32[4,8]{1,0:T(4,128)S(1)}, s32[4,8]{1,0:T(4,128)}, u32[]{:S(2)}) copy-start(s32[4,8]{1,0:T(4,128)} %refs_0_.1) | copy-start | bytes 388
  21.8 47.2 %copy-start.2 = (s32[4]{0:T(128)S(1)}, s32[4]{0:T(128)}, u32[]{:S(2)}) copy-start(s32[4]{0:T(128)} %refs_1_.2) | copy-start | bytes 52
  21.8 47.2 %copy-start.11 = (f32[1,2,128]{2,1,0:T(2,128)S(1)}, f32[1,2,128]{2,1,0:T(2,128)}, u32[]{:S(2)}) copy-start(f32[1,2,128]{2,1,0:T(2,128)} %param.28) | copy-start | bytes 3076
  22.0 47.0 %copy-start.3 = (bf16[4,176,384]{2,1,0:T(8,128)(2,1)}, bf16[4,176,384]{2,1,0:T(8,128)(2,1)S(1)}, u32[]{:S(2)}) copy-start(bf16[4,176,384]{2,1,0:T(8,128)(2,1)S(1)} %get-tuple-element.302.refs_12_.refs_11_) | copy-start | bytes 1622020
  22.0 47.0 %copy-start.4 = (bf16[4,176,384]{2,1,0:T(8,128)(2,1)}, bf16[4,176,384]{2,1,0:T(8,128)(2,1)S(1)}, u32[]{:S(2)}) copy-start(bf16[4,176,384]{2,1,0:T(8,128)(2,1)S(1)} %get-tuple-element.303.refs_11_.refs_10_) | copy-start | bytes 1622020
  22.0 18.1 %collective-permute-start = (bf16[4,176,384]{2,1,0:T(8,128)(2,1)S(1)}, bf16[4,176,384]{2,1,0:T(8,128)(2,1)S(1)}, u32[]{:S(2)}, u32[]{:S(2)}) collective-permute-start(bf16[4,176,384]{2,1,0:T(8,128)(2,1)S(1)} %get-tuple-element.303.refs_11_.refs_10_), channel_id=1, source_target_pairs={{4,0},{5,1},{12,8},{13,9},{22,18},{23,19},{30,26},{31,27},{32,36},... | collective-permute-start | bytes 1622024 | tf_op jit(solution)/shard_map/ppermute | solution.py:259
  23.3 22.5 %collective-permute-start.1 = (bf16[4,176,384]{2,1,0:T(8,128)(2,1)S(1)}, bf16[4,176,384]{2,1,0:T(8,128)(2,1)S(1)}, u32[]{:S(2)}, u32[]{:S(2)}) collective-permute-start(bf16[4,176,384]{2,1,0:T(8,128)(2,1)S(1)} %get-tuple-element.302.refs_12_.refs_11_), channel_id=1, source_target_pairs={{4,0},{5,1},{12,8},{13,9},{22,18},{23,19},{30,26},{31,27},{32,36},... | collective-permute-start | bytes 1622024 | tf_op jit(solution)/shard_map/ppermute | solution.py:259
  24.6 23.2 %collective-permute-start.2 = (bf16[4,176,384]{2,1,0:T(8,128)(2,1)S(1)}, bf16[4,176,384]{2,1,0:T(8,128)(2,1)S(1)}, u32[]{:S(2)}, u32[]{:S(2)}) collective-permute-start(bf16[4,176,384]{2,1,0:T(8,128)(2,1)S(1)} %get-tuple-element.302.refs_12_.refs_11_), channel_id=1, source_target_pairs={{64,72},{65,73},{82,90},{83,91},{100,108},{101,109},{118,126},{119... | collective-permute-start | bytes 1622024 | tf_op jit(solution)/shard_map/ppermute | solution.py:259
  28.6 34.2 %collective-permute-start.3 = (bf16[4,176,384]{2,1,0:T(8,128)(2,1)S(1)}, bf16[4,176,384]{2,1,0:T(8,128)(2,1)S(1)}, u32[]{:S(2)}, u32[]{:S(2)}) collective-permute-start(bf16[4,176,384]{2,1,0:T(8,128)(2,1)S(1)} %get-tuple-element.303.refs_11_.refs_10_), channel_id=1, source_target_pairs={{2,0},{3,1},{10,8},{11,9},{20,18},{21,19},{28,26},{29,27},{38,36},... | collective-permute-start | bytes 1622024 | tf_op jit(solution)/shard_map/ppermute | solution.py:259
  29.9 32.9 %collective-permute-start.4 = (bf16[4,176,384]{2,1,0:T(8,128)(2,1)S(1)}, bf16[4,176,384]{2,1,0:T(8,128)(2,1)S(1)}, u32[]{:S(2)}, u32[]{:S(2)}) collective-permute-start(bf16[4,176,384]{2,1,0:T(8,128)(2,1)S(1)} %get-tuple-element.302.refs_12_.refs_11_), channel_id=1, source_target_pairs={{2,0},{3,1},{10,8},{11,9},{20,18},{21,19},{28,26},{29,27},{38,36},... | collective-permute-start | bytes 1622024 | tf_op jit(solution)/shard_map/ppermute | solution.py:259
  40.1 28.9 %copy-start.5 = (bf16[4,176,384]{2,1,0:T(8,128)(2,1)}, bf16[4,176,384]{2,1,0:T(8,128)(2,1)S(1)}, u32[]{:S(2)}) copy-start(bf16[4,176,384]{2,1,0:T(8,128)(2,1)S(1)} %collective-permute-done.refs_4_.refs_3_) | copy-start | bytes 1622020
  40.1 22.7 %collective-permute-start.5 = (bf16[4,176,384]{2,1,0:T(8,128)(2,1)S(1)}, bf16[4,176,384]{2,1,0:T(8,128)(2,1)S(1)}, u32[]{:S(2)}, u32[]{:S(2)}) collective-permute-start(bf16[4,176,384]{2,1,0:T(8,128)(2,1)S(1)} %get-tuple-element.303.refs_11_.refs_10_), channel_id=1, source_target_pairs={{6,0},{7,1},{14,8},{15,9},{16,18},{17,19},{24,26},{25,27},{34,36},... | collective-permute-start | bytes 1622024 | tf_op jit(solution)/shard_map/ppermute | solution.py:259
  45.9 23.1 %copy-start.6 = (bf16[4,176,384]{2,1,0:T(8,128)(2,1)}, bf16[4,176,384]{2,1,0:T(8,128)(2,1)S(1)}, u32[]{:S(2)}) copy-start(bf16[4,176,384]{2,1,0:T(8,128)(2,1)S(1)} %collective-permute-done.1.refs_5_.refs_4_) | copy-start | bytes 1622020
  45.9 23.1 %collective-permute-start.6 = (bf16[4,176,384]{2,1,0:T(8,128)(2,1)S(1)}, bf16[4,176,384]{2,1,0:T(8,128)(2,1)S(1)}, u32[]{:S(2)}, u32[]{:S(2)}) collective-permute-start(bf16[4,176,384]{2,1,0:T(8,128)(2,1)S(1)} %get-tuple-element.302.refs_12_.refs_11_), channel_id=1, source_target_pairs={{6,0},{7,1},{14,8},{15,9},{16,18},{17,19},{24,26},{25,27},{34,36},... | collective-permute-start | bytes 1622024 | tf_op jit(solution)/shard_map/ppermute | solution.py:259
  47.8 21.2 %copy-start.7 = (bf16[4,176,384]{2,1,0:T(8,128)(2,1)}, bf16[4,176,384]{2,1,0:T(8,128)(2,1)S(1)}, u32[]{:S(2)}) copy-start(bf16[4,176,384]{2,1,0:T(8,128)(2,1)S(1)} %collective-permute-done.2.refs_6_.refs_5_) | copy-start | bytes 1622020
  62.8 6.2 %copy-start.8 = (bf16[4,176,384]{2,1,0:T(8,128)(2,1)}, bf16[4,176,384]{2,1,0:T(8,128)(2,1)S(1)}, u32[]{:S(2)}) copy-start(bf16[4,176,384]{2,1,0:T(8,128)(2,1)S(1)} %collective-permute-done.3.refs_7_.refs_6_) | copy-start | bytes 1622020
  62.8 6.2 %copy-start.9 = (bf16[4,176,384]{2,1,0:T(8,128)(2,1)}, bf16[4,176,384]{2,1,0:T(8,128)(2,1)S(1)}, u32[]{:S(2)}) copy-start(bf16[4,176,384]{2,1,0:T(8,128)(2,1)S(1)} %collective-permute-done.4.refs_8_.refs_7_) | copy-start | bytes 1622020
  69.0 2.9 %copy-start = (bf16[1,256,1536]{2,1,0:T(8,128)(2,1)S(1)}, bf16[1,256,1536]{2,1,0:T(8,128)(2,1)}, u32[]{:S(2)}) copy-start(bf16[1,256,1536]{2,1,0:T(8,128)(2,1)} %param.29) | copy-start | bytes 2359300
  69.1 2.9 %copy-start.10 = (f32[1,1536]{1,0:T(1,128)S(1)}, f32[1,1536]{1,0:T(1,128)}, u32[]{:S(2)}) copy-start(f32[1,1536]{1,0:T(1,128)} %refs_1_.3) | copy-start | bytes 18436
  71.3 5.9 %collective-permute-start.7 = (bf16[2,256,384]{2,1,0:T(8,128)(2,1)S(1)}, bf16[2,256,384]{2,1,0:T(8,128)(2,1)S(1)}, u32[]{:S(2)}, u32[]{:S(2)}) collective-permute-start(bf16[2,256,384]{2,1,0:T(8,128)(2,1)S(1)} %get-tuple-element.279), channel_id=1, source_target_pairs={{0,1},{1,0},{8,9},{9,8},{18,19},{19,18},{26,27},{27,26},{36,37},{3... | collective-permute-start | bytes 1179656 | tf_op jit(solution)/shard_map/ppermute | solution.py:289
  77.4 0.7 collective-permute-start.8
  78.1 0.7 collective-permute-start.9
  78.8 0.7 collective-permute-start.10
  79.7 0.7 collective-permute-start.11
  80.4 0.7 collective-permute-start.12
  81.2 0.7 collective-permute-start.13
  81.9 124.4 %collective-permute-start.14 = (bf16[256,384]{1,0:T(8,128)(2,1)S(1)}, bf16[256,384]{1,0:T(8,128)(2,1)S(1)}, u32[]{:S(2)}, u32[]{:S(2)}) collective-permute-start(bf16[256,384]{1,0:T(8,128)(2,1)S(1)} %get-tuple-element.291), channel_id=1, source_target_pairs={{384,448},{385,449},{392,456},{393,457},{402,466},{403,467},{410,4... | collective-permute-start | bytes 589832 | tf_op jit(solution)/shard_map/ppermute | solution.py:333
  242.7 5.1 %collective-permute-start.15 = (bf16[4,3,8,384]{3,2,1,0:T(8,128)(2,1)S(1)}, bf16[4,3,8,384]{3,2,1,0:T(8,128)(2,1)S(1)}, u32[]{:S(2)}, u32[]{:S(2)}) collective-permute-start(bf16[4,3,8,384]{3,2,1,0:T(8,128)(2,1)S(1)} %broadcast_select_fusion), channel_id=1, source_target_pairs={{64,65},{65,64},{66,67},{67,66},{68,69},{69,68},{70,71},{71,70},{7... | collective-permute-start | bytes 221192 | tf_op jit(solution)/shard_map/ppermute | solution.py:352
